TPU v7x, 32 devices: a whole 2x2x4 slice. The times are simulated.
32 devices in a mesh: ctx: 8 (over y, x, core), fsdp: 4 (over z).
Axes of the slice: x: 2, y: 2, z: 4, core: 2. Of those that a mesh axis runs over, the one named last changes fastest.
Arguments:
- queries: bfloat16 [2048, 512], P('ctx', 'fsdp'), may hold values from -6 to 6
- keys: bfloat16 [2048, 128], P('ctx'), may hold values from -6 to 6
- values: bfloat16 [2048, 128], P('ctx'), may hold values from -6 to 6
- out_grad: bfloat16 [2048, 512], P('ctx', 'fsdp'), may hold values from -6 to 6
- block_ids: int32 [16], replicated, may hold values from 0 to 15, as said below
- block_mask: int32 [16, 16], replicated, may hold values from 0 to 1, as said below
Outputs:
- query_grad: float32 [2048, 512], P('ctx', 'fsdp')
- key_grad: float32 [2048, 128], P('ctx', 'fsdp')
- value_grad: float32 [2048, 128], P('ctx', 'fsdp')
Inputs may be any that keep to these rules, and one draw needn't show every extreme that they name: `block_ids`: A permutation of the 16 sequence blocks; the two entries 2c and 2c + 1, the blocks of the rows of ctx device c, sum to 15. block_mask[i, j] is 1 for j = i and 0 for j > i; below the diagonal it is 0 or 1.
All inputs are finite; a program needn't handle non-finite values.
Results may differ from a plain program's by a relative error of at most 0.025.
Values may be sent and summed in bfloat16 or wider, within the bound.
No kernel may reach another device: no remote copies, remote signals or barrier semaphores. Data moves between devices by JAX's collectives and lax.ppermute only.
A program may use at most 64 MiB of HBM per device.

v0:
```python
import math

import jax
import jax.numpy as jnp
from jax import lax
from jax.sharding import PartitionSpec as P

GROUP = 4


def from_behind(x, axis, by):
    size = lax.axis_size(axis)
    pairs = [(i, i + by) for i in range(size) if 0 <= i + by < size]
    return lax.ppermute(x, axis, pairs)


def contract_last(left, right):
    return lax.dot_general(
        left, right, (((1,), (1,)), ((), ())), preferred_element_type=jnp.float32
    )


def contract_first(left, right):
    return lax.dot_general(
        left, right, (((0,), (0,)), ((), ())), preferred_element_type=jnp.float32
    )


def exact_weighted(weights, values_here):
    high_part = weights.astype(jnp.bfloat16)
    rest = weights - high_part.astype(jnp.float32)
    middle_part = rest.astype(jnp.bfloat16)
    low_part = (rest - middle_part.astype(jnp.float32)).astype(jnp.bfloat16)
    total = jnp.dot(high_part, values_here, preferred_element_type=jnp.float32)
    total = total + jnp.dot(middle_part, values_here, preferred_element_type=jnp.float32)
    return total + jnp.dot(low_part, values_here, preferred_element_type=jnp.float32)


def row_meta(block_ids, start_row, row_count, half_rows):
    row_ids = start_row + jnp.arange(row_count, dtype=jnp.int32)
    seq_block = jnp.take(block_ids, row_ids // half_rows)
    return (seq_block, seq_block * half_rows + row_ids % half_rows)


def allowed_pairs(block_ids, block_mask, query_start, query_count, key_start, key_count, half_rows):
    query_block, query_pos = row_meta(block_ids, query_start, query_count, half_rows)
    key_block, key_pos = row_meta(block_ids, key_start, key_count, half_rows)
    query_table = jnp.take(block_mask, query_block, axis=0)
    block_range = jnp.arange(block_mask.shape[0], dtype=jnp.int32)
    key_onehot = (key_block[:, None] == block_range[None, :]).astype(jnp.int32)
    linked = lax.dot_general(query_table, key_onehot, (((1,), (1,)), ((), ())))
    return (linked > 0) & (query_pos[:, None] >= key_pos[None, :])


def pair_grads(
    q_rows,
    g_rows,
    log_total,
    row_delta,
    k_rows,
    v_rows,
    query_start,
    key_start,
    block_ids,
    block_mask,
    half_rows,
    score_scale,
):
    scores = contract_last(q_rows, k_rows) * score_scale
    allowed = allowed_pairs(
        block_ids, block_mask, query_start, q_rows.shape[0], key_start, k_rows.shape[0], half_rows
    )
    soft_weights = jnp.where(allowed, jnp.exp(scores - log_total[:, None]), 0.0)
    grad_weights = contract_last(g_rows, v_rows)
    grad_scores = (soft_weights * (grad_weights - row_delta[:, None])).astype(jnp.bfloat16)
    query_term = jnp.dot(grad_scores, k_rows, preferred_element_type=jnp.float32) * score_scale
    key_term = contract_first(grad_scores, q_rows) * score_scale
    value_term = contract_first(soft_weights.astype(jnp.bfloat16), g_rows)
    return (query_term, key_term, value_term)


def body(queries, keys, values, out_grad, block_ids, block_mask):
    tok_rows, head_width = queries.shape
    half_rows = tok_rows // 2
    score_scale = head_width ** (-0.5)
    ctx_index = lax.axis_index("ctx")
    lane_index = lax.axis_index("fsdp")
    group_head = lane_index // GROUP
    own_start = ctx_index * tok_rows
    own_keys = lax.dynamic_slice_in_dim(keys, group_head * head_width, head_width, 1)
    own_values = lax.dynamic_slice_in_dim(values, group_head * head_width, head_width, 1)
    all_keys, all_values = (
        lax.all_gather(own_keys, "ctx", axis=0, tiled=True),
        lax.all_gather(own_values, "ctx", axis=0, tiled=True),
    )
    seq_rows = all_keys.shape[0]
    key_span = math.gcd(seq_rows, 4 * tok_rows)
    span_count = seq_rows // key_span

    def one_span(loop_index, loop_state):
        row_top, row_total, weighted = loop_state
        first_row = loop_index * key_span
        keys_here = lax.dynamic_slice_in_dim(all_keys, first_row, key_span, 0)
        values_here = lax.dynamic_slice_in_dim(all_values, first_row, key_span, 0)
        scores = contract_last(queries, keys_here) * score_scale
        allowed = allowed_pairs(
            block_ids, block_mask, own_start, tok_rows, first_row, key_span, half_rows
        )
        span_top = jnp.max(jnp.where(allowed, scores, -1e30), axis=1)
        new_top = jnp.maximum(row_top, span_top)
        weights = jnp.where(allowed, jnp.exp(scores - new_top[:, None]), 0.0)
        factor = jnp.exp(row_top - new_top)
        row_total = row_total * factor + jnp.sum(weights, axis=1)
        weighted = weighted * factor[:, None] + exact_weighted(weights, values_here)
        return (new_top, row_total, weighted)

    start_state = (
        jnp.full((tok_rows,), -1e30, jnp.float32),
        jnp.zeros((tok_rows,), jnp.float32),
        jnp.zeros((tok_rows, head_width), jnp.float32),
    )
    row_top, row_total, weighted = lax.fori_loop(0, span_count, one_span, start_state)
    log_total = row_top + jnp.log(row_total)
    row_delta = jnp.sum(out_grad.astype(jnp.float32) * (weighted / row_total[:, None]), axis=1)

    def grad_span(loop_index, loop_state):
        full_grads, query_acc = loop_state
        first_row = loop_index * key_span
        keys_here = lax.dynamic_slice_in_dim(all_keys, first_row, key_span, 0)
        values_here = lax.dynamic_slice_in_dim(all_values, first_row, key_span, 0)
        query_term, key_term, value_term = pair_grads(
            queries,
            out_grad,
            log_total,
            row_delta,
            keys_here,
            values_here,
            own_start,
            first_row,
            block_ids,
            block_mask,
            half_rows,
            score_scale,
        )
        full_grads = lax.dynamic_update_slice(
            full_grads, jnp.stack([key_term, value_term]), (0, first_row, 0)
        )
        return (full_grads, query_acc + query_term)

    grad_start = (
        jnp.zeros((2, seq_rows, head_width), jnp.float32),
        jnp.zeros((tok_rows, head_width), jnp.float32),
    )
    full_grads, query_grads = lax.fori_loop(0, span_count, grad_span, grad_start)
    key_grads = lax.psum_scatter(
        full_grads.astype(jnp.bfloat16), "ctx", scatter_dimension=1, tiled=True
    ).astype(jnp.float32)
    sub_width = head_width // GROUP
    own_part = lane_index % GROUP
    shared = lax.dynamic_slice_in_dim(key_grads, own_part * sub_width, sub_width, 2)
    for offset in list(range(1, GROUP)) + [-step for step in range(1, GROUP)]:
        target_part = jnp.mod(lane_index + offset, GROUP)
        outgoing = lax.dynamic_slice_in_dim(key_grads, target_part * sub_width, sub_width, 2)
        incoming = from_behind(outgoing.astype(jnp.bfloat16), "fsdp", offset).astype(outgoing.dtype)
        sender = lane_index - offset
        same_group = jnp.floor_divide(sender, GROUP) == group_head
        shared = shared + jnp.where(same_group, incoming, 0.0)
    return (query_grads, shared[0], shared[1])


def solution(mesh):
    in_specs = (P("ctx", "fsdp"), P("ctx", None), P("ctx", None), P("ctx", "fsdp"), P(), P())
    out_specs = (P("ctx", "fsdp"), P("ctx", "fsdp"), P("ctx", "fsdp"))
    return jax.shard_map(body, mesh=mesh, in_specs=in_specs, out_specs=out_specs, check_vma=False)
```

profile of v0, /device:TPU:0, one launch (start us, length us, event | category | flops | bytes accessed | tf_op | source)
XLA Modules:
  0.0 193.8 jit_solution(4966255445082638618)
XLA Ops:
  7.3 11.7 %all_gather.6 = bf16[2048,128]{1,0:T(8,128)(2,1)S(1)} all-gather(bf16[256,128]{1,0:T(8,128)(2,1)} %param.17), channel_id=1, replica_groups=mesh['ctx'=8,'fsdp'=4] {'ctx'}, dimensions={0}, use_global_device_ids=true | all-gather | bytes 589824 | tf_op jit(solution)/shard_map/all_gather | solution.py:93
  19.0 9.7 %all_gather.7 = bf16[2048,128]{1,0:T(8,128)(2,1)S(1)} all-gather(bf16[256,128]{1,0:T(8,128)(2,1)S(1)} %copy-done.6), channel_id=1, replica_groups=mesh['ctx'=8,'fsdp'=4] {'ctx'}, dimensions={0}, use_global_device_ids=true | all-gather | bytes 589824 | tf_op jit(solution)/shard_map/all_gather | solution.py:94
  28.7 0.6 copy-done.2
  29.4 50.3 %while.40 = (s32[]{:T(128)}, f32[256]{0:T(256)S(1)}, f32[256]{0:T(256)S(1)}, f32[256,128]{1,0:T(8,128)S(1)}, s32[]{:T(128)}, /*index=5*/s32[16]{0:T(128)S(1)}, s...) while((s32[]{:T(128)}, f32[256]{0:T(256)S(1)}, ...), condition=%wide.region_3.7_spmd.clone, body=%wide.region_0.6_spmd.clone.sunk | while | flops 284168448 | bytes 9598947 | solution.py:122
  29.4 0.7 fusion.111
  30.1 10.2 %compare_and_fusion.4 = (pred[256]{0:T(512)(128)(4,1)S(1)}, s32[256]{0:T(256)S(1)}) fusion(s32[]{:T(128)} %bitcast.137, s32[]{:T(128)} %bitcast.138, s32[]{:T(128)} %bitcast.139, s32[]{:T(128)} %bitcast.140, s32[]{:T(128)} %bitcast.141, s32[]{:T(128)} %bitcast.142, s32[]{:T(128)} %bitcast.143, s32[]{:T(128)} %bitcast.144, s32[]{:T(128)} %bitcast.145, ...), kind=kLoop, calls=%fused_computation.44.clone.1 | loop fusion | flops 15104 | bytes 1348 | tf_op jit(solution)/shard_map/while/body/eval_jaxpr/jit(_take)/and | solution.py:48
  40.3 10.2 %fusion.112 = (s32[1024]{0:T(1024)S(1)}, s32[1024]{0:T(1024)S(1)}) fusion(s32[]{:T(128)S(6)} %mul.267, s32[]{:T(128)} %bitcast.137, s32[]{:T(128)} %bitcast.138, s32[]{:T(128)} %bitcast.139, s32[]{:T(128)} %bitcast.140, s32[]{:T(128)} %bitcast.141, s32[]{:T(128)} %bitcast.142, s32[]{:T(128)} %bitcast.143, s32[]{:T(128)} %bitcast.144, s32[]{:T(128)} %bitcast.145, ...), kind=kLoop, calls=%fused_computation.32.clone.1 | loop fusion | flops 60416 | bytes 8260 | tf_op jit(solution)/shard_map/while/body/eval_jaxpr/add | solution.py:42
  50.5 0.7 gather_fusion
  51.6 1.1 select_reduce_fusion.2
  52.7 0.4 fusion.114
  53.1 0.4 fusion.116
  53.5 0.5 convolution_add_fusion.3
  54.0 0.5 fusion.117
  54.5 0.7 fusion.111
  55.2 10.2 %compare_and_fusion.4 = (pred[256]{0:T(512)(128)(4,1)S(1)}, s32[256]{0:T(256)S(1)}) fusion(s32[]{:T(128)} %bitcast.137, s32[]{:T(128)} %bitcast.138, s32[]{:T(128)} %bitcast.139, s32[]{:T(128)} %bitcast.140, s32[]{:T(128)} %bitcast.141, s32[]{:T(128)} %bitcast.142, s32[]{:T(128)} %bitcast.143, s32[]{:T(128)} %bitcast.144, s32[]{:T(128)} %bitcast.145, ...), kind=kLoop, calls=%fused_computation.44.clone.1 | loop fusion | flops 15104 | bytes 1348 | tf_op jit(solution)/shard_map/while/body/eval_jaxpr/jit(_take)/and | solution.py:48
  65.4 10.2 %fusion.112 = (s32[1024]{0:T(1024)S(1)}, s32[1024]{0:T(1024)S(1)}) fusion(s32[]{:T(128)S(6)} %mul.267, s32[]{:T(128)} %bitcast.137, s32[]{:T(128)} %bitcast.138, s32[]{:T(128)} %bitcast.139, s32[]{:T(128)} %bitcast.140, s32[]{:T(128)} %bitcast.141, s32[]{:T(128)} %bitcast.142, s32[]{:T(128)} %bitcast.143, s32[]{:T(128)} %bitcast.144, s32[]{:T(128)} %bitcast.145, ...), kind=kLoop, calls=%fused_computation.32.clone.1 | loop fusion | flops 60416 | bytes 8260 | tf_op jit(solution)/shard_map/while/body/eval_jaxpr/add | solution.py:42
  75.7 0.7 gather_fusion
  76.7 1.1 select_reduce_fusion.2
  77.8 0.4 fusion.114
  78.2 0.4 fusion.116
  78.7 0.5 convolution_add_fusion.3
  79.1 0.5 fusion.117
  80.0 50.1 %while.41 = (s32[]{:T(128)}, bf16[2,2048,128]{1,2,0:T(8,128)(2,1)S(1)}, f32[256,128]{1,0:T(8,128)S(1)}, s32[]{:T(128)}, s32[16]{0:T(128)S(1)}, /*index=5*/s32[16...) while((s32[]{:T(128)}, ...), condition=%wide.region_6.10_spmd.clone, body=%wide.region_5.9_spmd.clone.sunk | while | flops 347278336 | bytes 10303473 | solution.py:154
  80.0 0.7 fusion.129
  80.7 10.2 %compare_and_fusion.5 = (pred[256]{0:T(512)(128)(4,1)S(1)}, s32[256]{0:T(256)S(1)}) fusion(s32[]{:T(128)} %bitcast.163, s32[]{:T(128)} %bitcast.164, s32[]{:T(128)} %bitcast.165, s32[]{:T(128)} %bitcast.166, s32[]{:T(128)} %bitcast.167, s32[]{:T(128)} %bitcast.168, s32[]{:T(128)} %bitcast.169, s32[]{:T(128)} %bitcast.170, s32[]{:T(128)} %bitcast.171, ...), kind=kLoop, calls=%fused_computation.125.clone.1 | loop fusion | flops 15104 | bytes 1348 | tf_op jit(solution)/shard_map/while/body/eval_jaxpr/jit(_take)/and | solution.py:48
  90.9 10.2 %fusion.130 = (s32[1024]{0:T(1024)S(1)}, s32[1024]{0:T(1024)S(1)}) fusion(s32[]{:T(128)S(6)} %mul.273, s32[]{:T(128)} %bitcast.163, s32[]{:T(128)} %bitcast.164, s32[]{:T(128)} %bitcast.165, s32[]{:T(128)} %bitcast.166, s32[]{:T(128)} %bitcast.167, s32[]{:T(128)} %bitcast.168, s32[]{:T(128)} %bitcast.169, s32[]{:T(128)} %bitcast.170, s32[]{:T(128)} %bitcast.171, ...), kind=kLoop, calls=%fused_computation.113.clone.1 | loop fusion | flops 60416 | bytes 8260 | tf_op jit(solution)/shard_map/while/body/eval_jaxpr/add | solution.py:42
  101.2 0.7 gather_fusion.1
  101.9 1.0 fusion.131
  102.9 0.4 fusion.132
  104.3 0.4 fusion.134
  105.1 0.7 fusion.129
  105.8 10.2 %compare_and_fusion.5 = (pred[256]{0:T(512)(128)(4,1)S(1)}, s32[256]{0:T(256)S(1)}) fusion(s32[]{:T(128)} %bitcast.163, s32[]{:T(128)} %bitcast.164, s32[]{:T(128)} %bitcast.165, s32[]{:T(128)} %bitcast.166, s32[]{:T(128)} %bitcast.167, s32[]{:T(128)} %bitcast.168, s32[]{:T(128)} %bitcast.169, s32[]{:T(128)} %bitcast.170, s32[]{:T(128)} %bitcast.171, ...), kind=kLoop, calls=%fused_computation.125.clone.1 | loop fusion | flops 15104 | bytes 1348 | tf_op jit(solution)/shard_map/while/body/eval_jaxpr/jit(_take)/and | solution.py:48
  116.0 10.2 %fusion.130 = (s32[1024]{0:T(1024)S(1)}, s32[1024]{0:T(1024)S(1)}) fusion(s32[]{:T(128)S(6)} %mul.273, s32[]{:T(128)} %bitcast.163, s32[]{:T(128)} %bitcast.164, s32[]{:T(128)} %bitcast.165, s32[]{:T(128)} %bitcast.166, s32[]{:T(128)} %bitcast.167, s32[]{:T(128)} %bitcast.168, s32[]{:T(128)} %bitcast.169, s32[]{:T(128)} %bitcast.170, s32[]{:T(128)} %bitcast.171, ...), kind=kLoop, calls=%fused_computation.113.clone.1 | loop fusion | flops 60416 | bytes 8260 | tf_op jit(solution)/shard_map/while/body/eval_jaxpr/add | solution.py:42
  126.3 0.7 gather_fusion.1
  127.0 1.0 fusion.131
  128.0 0.4 fusion.132
  129.4 0.4 fusion.134
  130.1 1.0 copy-done.4
  131.3 36.4 %reduce-scatter.2.cloned.1.call-done = bf16[2,256,128]{1,2,0:T(8,128)(2,1)} async-done(((bf16[2,2048,128]{1,2,0:T(8,128)(2,1)}), bf16[2,256,128]{1,2,0:T(8,128)(2,1)}) %reduce-scatter.2.cloned.1.call-update) | async-done | bytes 131088 | tf_op jit(solution)/shard_map/reduce_scatter | solution.py:155
  167.6 0.9 convert_element_type.130
  168.6 3.4 %collective-permute-start = (bf16[2,256,32]{1,2,0:T(8,128)(2,1)S(1)}, bf16[2,256,32]{1,2,0:T(8,128)(2,1)S(1)}, u32[]{:S(2)}, u32[]{:S(2)}) collective-permute-start(bf16[2,256,32]{1,2,0:T(8,128)(2,1)S(1)} %get-tuple-element.780), channel_id=1, source_target_pairs={{0,1},{1,2},{2,3},{4,5},{5,6},{6,7},{8,9},{9,10},{10,11},{12,13},{... | collective-permute-start | bytes 98312 | tf_op jit(solution)/shard_map/ppermute | solution.py:14
  172.0 1.3 collective-permute-start.5
  173.3 1.3 collective-permute-start.4
  174.6 1.3 collective-permute-start.3
  175.9 7.5 %collective-permute-start.2 = (bf16[2,256,32]{1,2,0:T(8,128)(2,1)S(1)}, bf16[2,256,32]{1,2,0:T(8,128)(2,1)S(1)}, u32[]{:S(2)}, u32[]{:S(2)}) collective-permute-start(bf16[2,256,32]{1,2,0:T(8,128)(2,1)S(1)} %get-tuple-element.784), channel_id=1, source_target_pairs={{0,3},{4,7},{8,11},{12,15},{16,19},{20,23},{24,27},{28,31}} | collective-permute-start | bytes 98312 | tf_op jit(solution)/shard_map/ppermute | solution.py:14
  183.4 1.3 collective-permute-start.1
  185.0 1.3 collective-permute-done.1
  186.3 0.6 slice_bitcast_fusion
  (56 shorter events, 4.0 us)
Async XLA Ops:
  7.2 160.5 %reduce-scatter.2.cloned.1.call-start = ((), (), s32[]{:S(2)}) async-start(), calls=%async_computation.1 | async-start | bytes 1179648 | tf_op jit(solution)/shard_map/reduce_scatter | solution.py:155
  7.3 11.8 %copy-start.6 = (bf16[256,128]{1,0:T(8,128)(2,1)S(1)}, bf16[256,128]{1,0:T(8,128)(2,1)}, u32[]{:S(2)}) copy-start(bf16[256,128]{1,0:T(8,128)(2,1)} %param.18) | copy-start | bytes 196612
  19.0 9.7 %copy-start = (s32[16,16]{1,0:T(8,128)S(1)}, s32[16,16]{1,0:T(8,128)}, u32[]{:S(2)}) copy-start(s32[16,16]{1,0:T(8,128)} %param.21) | copy-start | bytes 3076
  19.0 9.7 %copy-start.1 = (bf16[256,128]{1,0:T(8,128)(2,1)S(1)}, bf16[256,128]{1,0:T(8,128)(2,1)}, u32[]{:S(2)}) copy-start(bf16[256,128]{1,0:T(8,128)(2,1)} %param.16) | copy-start | bytes 196612
  28.7 0.7 copy-start.2
  29.4 50.3 %copy-start.3 = (bf16[256,128]{1,0:T(8,128)(2,1)S(1)}, bf16[256,128]{1,0:T(8,128)(2,1)}, u32[]{:S(2)}) copy-start(bf16[256,128]{1,0:T(8,128)(2,1)} %param.19) | copy-start | bytes 196612
  130.1 1.0 copy-start.4
  130.1 1.0 copy-start.5
  168.6 14.8 %collective-permute-start = (bf16[2,256,32]{1,2,0:T(8,128)(2,1)S(1)}, bf16[2,256,32]{1,2,0:T(8,128)(2,1)S(1)}, u32[]{:S(2)}, u32[]{:S(2)}) collective-permute-start(bf16[2,256,32]{1,2,0:T(8,128)(2,1)S(1)} %get-tuple-element.780), channel_id=1, source_target_pairs={{0,1},{1,2},{2,3},{4,5},{5,6},{6,7},{8,9},{9,10},{10,11},{12,13},{... | collective-permute-start | bytes 98312 | tf_op jit(solution)/shard_map/ppermute | solution.py:14
  172.0 12.8 %collective-permute-start.5 = (bf16[2,256,32]{1,2,0:T(8,128)(2,1)S(1)}, bf16[2,256,32]{1,2,0:T(8,128)(2,1)S(1)}, u32[]{:S(2)}, u32[]{:S(2)}) collective-permute-start(bf16[2,256,32]{1,2,0:T(8,128)(2,1)S(1)} %get-tuple-element.781), channel_id=1, source_target_pairs={{3,0},{7,4},{11,8},{15,12},{19,16},{23,20},{27,24},{31,28}} | collective-permute-start | bytes 98312 | tf_op jit(solution)/shard_map/ppermute | solution.py:14
  173.3 11.6 %collective-permute-start.4 = (bf16[2,256,32]{1,2,0:T(8,128)(2,1)S(1)}, bf16[2,256,32]{1,2,0:T(8,128)(2,1)S(1)}, u32[]{:S(2)}, u32[]{:S(2)}) collective-permute-start(bf16[2,256,32]{1,2,0:T(8,128)(2,1)S(1)} %get-tuple-element.782), channel_id=1, source_target_pairs={{2,0},{3,1},{6,4},{7,5},{10,8},{11,9},{14,12},{15,13},{18,16},{19,... | collective-permute-start | bytes 98312 | tf_op jit(solution)/shard_map/ppermute | solution.py:14
  174.6 10.3 %collective-permute-start.3 = (bf16[2,256,32]{1,2,0:T(8,128)(2,1)S(1)}, bf16[2,256,32]{1,2,0:T(8,128)(2,1)S(1)}, u32[]{:S(2)}, u32[]{:S(2)}) collective-permute-start(bf16[2,256,32]{1,2,0:T(8,128)(2,1)S(1)} %get-tuple-element.783), channel_id=1, source_target_pairs={{1,0},{2,1},{3,2},{5,4},{6,5},{7,6},{9,8},{10,9},{11,10},{13,12},{... | collective-permute-start | bytes 98312 | tf_op jit(solution)/shard_map/ppermute | solution.py:14
  175.9 9.1 %collective-permute-start.2 = (bf16[2,256,32]{1,2,0:T(8,128)(2,1)S(1)}, bf16[2,256,32]{1,2,0:T(8,128)(2,1)S(1)}, u32[]{:S(2)}, u32[]{:S(2)}) collective-permute-start(bf16[2,256,32]{1,2,0:T(8,128)(2,1)S(1)} %get-tuple-element.784), channel_id=1, source_target_pairs={{0,3},{4,7},{8,11},{12,15},{16,19},{20,23},{24,27},{28,31}} | collective-permute-start | bytes 98312 | tf_op jit(solution)/shard_map/ppermute | solution.py:14
  183.4 2.9 %collective-permute-start.1 = (bf16[2,256,32]{1,2,0:T(8,128)(2,1)S(1)}, bf16[2,256,32]{1,2,0:T(8,128)(2,1)S(1)}, u32[]{:S(2)}, u32[]{:S(2)}) collective-permute-start(bf16[2,256,32]{1,2,0:T(8,128)(2,1)S(1)} %get-tuple-element.785), channel_id=1, source_target_pairs={{0,2},{1,3},{4,6},{5,7},{8,10},{9,11},{12,14},{13,15},{16,18},{17,... | collective-permute-start | bytes 98312 | tf_op jit(solution)/shard_map/ppermute | solution.py:14
Sparse Core Ops, SparseCore 0:
  131.2 36.3 reduce-scatter.1
where the time goes:
time: 195 us; the launch traced here: 194 us
  other arithmetic  83.8 us (43%)
  waiting for transfers between devices  37.8 us (19%)
  blocking collectives  21.4 us (11%)
  starting transfers between devices  16.1 us (8%)
  between operations  14.5 us (7%)
  matrix products  11 us (6%)
  local copies, waits for them, and re-layouts  8.79 us (5%)
    and x4, other arithmetic, allowed_pairs(): query_table = jnp.take(block_mask, query_block, axis=0)  40.8 us
    add x4, other arithmetic, row_meta(): return (seq_block, seq_block * half_rows + row_ids % half_rows)  40.8 us
    reduce_scatter x1, waiting for transfers between devices, body(): lax.psum_scatter(full_grads.astype(jnp.bfloat16), 'ctx', scatter_dimensio...  36.4 us
    ppermute x6, starting transfers between devices, from_behind(): return lax.ppermute(x, axis, pairs)  16.1 us
    all_gather x1, blocking collectives, body(): lax.all_gather(own_keys, 'ctx', axis=0, tiled=True)  11.7 us
    all_gather x1, blocking collectives, body(): lax.all_gather(own_values, 'ctx', axis=0, tiled=True)  9.69 us
    dot_general x4, matrix products, allowed_pairs(): linked = lax.dot_general(query_table, key_onehot, (((1,), (1,)), ((), ())))  4.19 us
  transfers between devices with their start and end apart: 7, of which 3 were waited for; matrix products, arithmetic and copies ran while one was open for 0% of the time, Pallas kernels for 0%

commit v1 on v0

v1 whole, which is shorter than its diff:
```python
import functools
import math

import jax
import jax.numpy as jnp
from jax import lax
from jax.experimental import pallas as pl
from jax.experimental.pallas import tpu as pltpu
from jax.sharding import PartitionSpec as P

GROUP = 4
SHARE = 4
MASKED = -1e30
FLOOR = -1e20
VMEM_LIMIT = 48 * 1024 * 1024

F32 = jnp.float32
BF16 = jnp.bfloat16


def dot(left, right, left_dim, right_dim):
    return lax.dot_general(
        left, right, (((left_dim,), (right_dim,)), ((), ())), preferred_element_type=F32
    )


def vmem():
    return pl.BlockSpec(memory_space=pltpu.VMEM)


def smem():
    return pl.BlockSpec(memory_space=pltpu.SMEM)


def call(kernel, out_shape, ins, flops=0, scratch=()):
    size = sum(math.prod(x.shape) * x.dtype.itemsize for x in list(ins) + list(out_shape))
    specs = [smem() if x.dtype == jnp.int32 else vmem() for x in ins]
    return pl.pallas_call(
        kernel,
        out_shape=out_shape,
        in_specs=specs,
        out_specs=[vmem() for _ in out_shape],
        scratch_shapes=list(scratch),
        compiler_params=pltpu.CompilerParams(vmem_limit_bytes=VMEM_LIMIT),
        cost_estimate=pl.CostEstimate(flops=flops, bytes_accessed=size, transcendentals=0),
    )(*ins)


def pack_kernel(q_ref, g_ref, k_ref, v_ref, qg_ref, kv_ref):
    qg_ref[0] = q_ref[...]
    qg_ref[1] = g_ref[...]
    kv_ref[0] = k_ref[...]
    kv_ref[1] = v_ref[...]


def masked_scores(place_ref, ids_ref, mask_ref, q_rows, keys_here, key_group, factor):
    unit = keys_here.shape[0]
    half = unit // 2
    queries = q_rows.shape[0]
    first_query = place_ref[0] * SHARE * 2
    key_unit = key_group * SHARE + place_ref[1]
    scores = dot(keys_here, q_rows, 1, 1) * factor
    lane = lax.broadcasted_iota(jnp.int32, (1, half), 1)
    row = lax.broadcasted_iota(jnp.int32, (half, 1), 0)
    halves = []
    for part in range(2):
        key_block = ids_ref[key_unit * 2 + part]
        limits = []
        for block in range(queries // half):
            query_block = ids_ref[first_query + block]
            linked = mask_ref[query_block, key_block] > 0
            start = jnp.where(linked, (query_block - key_block) * half, -2 * half)
            limits.append(lane + start)
        limit = jnp.concatenate(limits, axis=1)
        halves.append(jnp.where(limit >= row, scores[part * half : (part + 1) * half], MASKED))
    return jnp.concatenate(halves, axis=0)


def stats_kernel(units, factor, place_ref, ids_ref, mask_ref, qg_ref, *refs):
    kv_refs, out_ref = refs[:units], refs[units]
    width = qg_ref.shape[-1]
    q_rows = qg_ref[:, 0].reshape(-1, width)
    g_rows = qg_ref[:, 1].reshape(-1, width)
    scores = [
        masked_scores(place_ref, ids_ref, mask_ref, q_rows, kv_refs[u][0], place_ref[2 + u], factor)
        for u in range(units)
    ]
    top = functools.reduce(jnp.maximum, [jnp.max(s, axis=0, keepdims=True) for s in scores])
    top = jnp.maximum(top, FLOOR)
    total = jnp.zeros_like(top)
    weighted = jnp.zeros_like(top)
    for u in range(units):
        weights = jnp.exp2(scores[u] - top)
        total += jnp.sum(weights, axis=0, keepdims=True)
        grads = dot(kv_refs[u][1], g_rows, 1, 1)
        weighted += jnp.sum(weights * grads, axis=0, keepdims=True)
    out_ref[0:1, :] = top
    out_ref[1:2, :] = total
    out_ref[2:3, :] = weighted


def grads_kernel(units, factor, scale, place_ref, ids_ref, mask_ref, qg_ref, stats_ref, *refs):
    kv_refs = refs[:units]
    kv_out_ref, own_ref = refs[units], refs[units + 1]
    far_refs = refs[units + 2 : units + 1 + SHARE]
    dq_ref = refs[-1]
    width = qg_ref.shape[-1]
    sub = width // GROUP
    unit = qg_ref.shape[2]
    q_rows = qg_ref[:, 0].reshape(-1, width)
    g_rows = qg_ref[:, 1].reshape(-1, width)
    tops = [stats_ref[s, 0:1, :] for s in range(SHARE)]
    top = functools.reduce(jnp.maximum, tops)
    scaled = [jnp.exp2(t - top) for t in tops]
    total = sum(stats_ref[s, 1:2, :] * scaled[s] for s in range(SHARE))
    weighted = sum(stats_ref[s, 2:3, :] * scaled[s] for s in range(SHARE))
    log_total = top + jnp.log2(total)
    delta = weighted / total
    dq = None
    for u in range(units):
        keys_here, values_here = kv_refs[u][0], kv_refs[u][1]
        key_group = place_ref[2 + u]
        scores = masked_scores(place_ref, ids_ref, mask_ref, q_rows, keys_here, key_group, factor)
        probs = jnp.exp2(scores - log_total)
        dprobs = dot(values_here, g_rows, 1, 1)
        dscores = (probs * (dprobs - delta)).astype(BF16)
        dv = dot(probs.astype(BF16), g_rows, 1, 0)
        dk = dot(dscores, q_rows, 1, 0) * scale
        dk = dk.T.astype(BF16)
        dv = dv.T.astype(BF16)
        for part in range(GROUP):
            kv_out_ref[key_group, part, 0] = dk[part * sub : (part + 1) * sub]
            kv_out_ref[key_group, part, 1] = dv[part * sub : (part + 1) * sub]
        term = dot(keys_here, dscores, 0, 0)
        dq = term if dq is None else dq + term
    dq = dq * scale
    for s in range(SHARE):
        dq_ref[s] = dq[:, s * unit : (s + 1) * unit]
    me = place_ref[1]
    own_ref[...] = dq_ref[me]
    for step in range(1, SHARE):
        far_refs[step - 1][...] = dq_ref[me ^ step].astype(BF16)


def final_kernel(own_ref, *refs):
    far_refs = refs[: SHARE - 1]
    kv_ref, dq_ref, dk_ref, dv_ref = refs[SHARE - 1 :]
    dq = own_ref[...]
    for ref in far_refs:
        dq += ref[...].astype(F32)
    dq_ref[...] = dq.T
    for which, out_ref in ((0, dk_ref), (1, dv_ref)):
        total = kv_ref[0, which].astype(F32)
        for source in range(1, kv_ref.shape[0]):
            total += kv_ref[source, which].astype(F32)
        out_ref[...] = total.T


def body(queries, keys, values, out_grad, block_ids, block_mask):
    unit, width = queries.shape
    ctx_size, lanes = lax.axis_size("ctx"), lax.axis_size("fsdp")
    units = ctx_size // SHARE
    scale = width ** (-0.5)
    factor = scale * math.log2(math.e)
    ctx_index = lax.axis_index("ctx")
    key_group = lax.axis_index("fsdp") // GROUP
    sub = width // GROUP
    if keys.shape[1] != width:
        keys = lax.dynamic_slice_in_dim(keys, key_group * width, width, 1)
        values = lax.dynamic_slice_in_dim(values, key_group * width, width, 1)

    pair = jax.ShapeDtypeStruct((2, unit, width), BF16)
    qg, kv = call(pack_kernel, [pair, pair], [queries, out_grad, keys, values])

    def swap(x, step):
        return lax.ppermute(x, "ctx", [(i, i ^ step) for i in range(ctx_size)])

    own_group, own_place = ctx_index // SHARE, ctx_index % SHARE
    key_groups = [own_group ^ u for u in range(units)]
    place = jnp.stack([own_group, own_place] + key_groups).astype(jnp.int32)
    groups = [list(range(g * SHARE, (g + 1) * SHARE)) for g in range(units)]
    kvs = [kv] + [swap(kv, u * SHARE) for u in range(1, units)]
    qgs = lax.all_gather(qg, "ctx", axis_index_groups=groups)

    rows = SHARE * unit
    product = 2 * rows * units * unit * width
    (stats,) = call(
        functools.partial(stats_kernel, units, factor),
        [jax.ShapeDtypeStruct((3, rows), F32)],
        [place, block_ids, block_mask, qgs] + kvs,
        flops=2 * product,
    )
    all_stats = lax.all_gather(stats, "ctx", axis_index_groups=groups)
    tall = (width, unit)
    outs = call(
        functools.partial(grads_kernel, units, factor, scale),
        [
            jax.ShapeDtypeStruct((units, GROUP, 2, sub, unit), BF16),
            jax.ShapeDtypeStruct(tall, F32),
        ]
        + [jax.ShapeDtypeStruct(tall, BF16)] * (SHARE - 1),
        [place, block_ids, block_mask, qgs, all_stats] + kvs,
        flops=5 * product,
        scratch=[pltpu.VMEM((SHARE,) + tall, F32)],
    )
    kv_parts, own, far = outs[0], outs[1], outs[2:]
    far = [swap(x, step + 1) for step, x in enumerate(far)]
    places = [
        [(g * SHARE + s) * lanes + head * GROUP + h for g in range(units) for h in range(GROUP)]
        for s in range(SHARE)
        for head in range(lanes // GROUP)
    ]
    kv_parts = kv_parts.reshape(units * GROUP, 2, sub, unit)
    kv_parts = lax.all_to_all(
        kv_parts, ("ctx", "fsdp"), 0, 0, axis_index_groups=places, tiled=True
    )
    return tuple(
        call(
            final_kernel,
            [
                jax.ShapeDtypeStruct((unit, width), F32),
                jax.ShapeDtypeStruct((unit, sub), F32),
                jax.ShapeDtypeStruct((unit, sub), F32),
            ],
            [own] + far + [kv_parts],
        )
    )


def solution(mesh):
    in_specs = (P("ctx", "fsdp"), P("ctx", None), P("ctx", None), P("ctx", "fsdp"), P(), P())
    out_specs = (P("ctx", "fsdp"), P("ctx", "fsdp"), P("ctx", "fsdp"))
    return jax.shard_map(body, mesh=mesh, in_specs=in_specs, out_specs=out_specs, check_vma=False)
```

time: 195 us -> 42.5 us (0.22)
  other arithmetic: 83.8 us -> 0.08 us
  waiting for transfers between devices: 37.8 us -> 8.41 us
  between operations: 14.5 us -> 0.66 us
  matrix products: 11 us -> 0 us
  blocking collectives: 21.4 us -> 12.4 us
  starting transfers between devices: 16.1 us -> 9.77 us
  Pallas kernels: 0 us -> 5.33 us
  local copies, waits for them, and re-layouts: 8.79 us -> 5.38 us
    add x8 -> x0, other arithmetic: 40.9 us -> none  [the longest x4 40.8 us: row_meta(): return (seq_block, seq_block * half_rows + row_ids % half_rows)]
    and x4 -> x0, other arithmetic: 40.8 us -> none  [allowed_pairs(): query_table = jnp.take(block_mask, query_block, axis=0)]
    reduce_scatter x1 -> x0, waiting for transfers between devices: 36.4 us -> none  [body(): lax.psum_scatter(full_grads.astype(jnp.bfloat16), 'ctx', scatter_dimensio...]
    ppermute x6 -> x4, starting transfers between devices: 16.1 us -> 4.89 us  [swap(): return lax.ppermute(x, 'ctx', [(i, i ^ step) for i in range(ctx_size)])]
    dot_general x22 -> x0, matrix products: 11 us -> none  [the longest x4 4.19 us: allowed_pairs(): linked = lax.dot_general(query_table, key_onehot, (((1,), (1,)), ((), ())))]
    all_gather x2, blocking collectives: 21.4 us -> 12.4 us  [the longest x1 7.16 us: body(): qgs = lax.all_gather(qg, 'ctx', axis_index_groups=groups)]
    gather x8 -> x0, local copies, waits for them, and re-layouts: 5.81 us -> none  [the longest x4 2.92 us: allowed_pairs(): query_table = jnp.take(block_mask, query_block, axis=0)]
    pallas_call x0 -> x4, Pallas kernels: none -> 5.33 us  [call(): pl.pallas_call(kernel, out_shape=out_shape, in_specs=specs, out_specs=[vm...]
  transfers between devices with their start and end apart: 7 -> 5, of which waited for: 3 -> 3; matrix products, arithmetic and copies ran while one was open for 0% -> 0% of each run, Pallas kernels for 0% -> 0%
where the time goes in v1:
time: 42.5 us; the launch traced here: 42 us
  blocking collectives  12.4 us (29%)
  starting transfers between devices  9.77 us (23%)
  waiting for transfers between devices  8.41 us (20%)
  local copies, waits for them, and re-layouts  5.38 us (13%)
  Pallas kernels  5.33 us (13%)
  between operations  0.66 us (2%)
    all_gather x1, blocking collectives, body(): qgs = lax.all_gather(qg, 'ctx', axis_index_groups=groups)  7.16 us
    pallas_call x4, Pallas kernels, call(): pl.pallas_call(kernel, out_shape=out_shape, in_specs=specs, out_specs=[vm...  5.33 us
    all_gather x1, blocking collectives, body(): all_stats = lax.all_gather(stats, 'ctx', axis_index_groups=groups)  5.25 us
    ppermute x4, starting transfers between devices, swap(): return lax.ppermute(x, 'ctx', [(i, i ^ step) for i in range(ctx_size)])  4.89 us
    all_to_all x1, starting transfers between devices, body(): lax.all_to_all(kv_parts, ('ctx', 'fsdp'), 0, 0, axis_index_groups=places,...  4.88 us
    all_to_all x1, waiting for transfers between devices, body(): lax.all_to_all(kv_parts, ('ctx', 'fsdp'), 0, 0, axis_index_groups=places,...  4.83 us
    unnamed x12, local copies, waits for them, and re-layouts  4 us
    ppermute x4, waiting for transfers between devices, swap(): return lax.ppermute(x, 'ctx', [(i, i ^ step) for i in range(ctx_size)])  3.58 us
  transfers between devices with their start and end apart: 5, of which 3 were waited for; matrix products, arithmetic and copies ran while one was open for 0% of the time, Pallas kernels for 0%

profile of v1, /device:TPU:0, one launch (start us, length us, event | category | flops | bytes accessed | tf_op | source)
XLA Modules:
  0.0 42.0 jit_solution(4239802689142079946)
XLA Ops:
  0.6 0.0 copy-start
  0.6 0.8 %copy-done = bf16[256,128]{1,0:T(8,128)(2,1)S(1)} copy-done((bf16[256,128]{1,0:T(8,128)(2,1)S(1)}, bf16[256,128]{1,0:T(8,128)(2,1)}, u32[]{:S(2)}) %copy-start) | copy-done | bytes 65560
  1.5 0.0 copy-start.1
  1.5 0.8 %copy-done.1 = bf16[256,128]{1,0:T(8,128)(2,1)S(1)} copy-done((bf16[256,128]{1,0:T(8,128)(2,1)S(1)}, bf16[256,128]{1,0:T(8,128)(2,1)}, u32[]{:S(2)}) %copy-start.1) | copy-done | bytes 65560
  2.3 0.0 copy-start.2
  2.3 0.8 %copy-done.2 = bf16[256,128]{1,0:T(8,128)(2,1)S(1)} copy-done((bf16[256,128]{1,0:T(8,128)(2,1)S(1)}, bf16[256,128]{1,0:T(8,128)(2,1)}, u32[]{:S(2)}) %copy-start.2) | copy-done | bytes 65560
  3.2 0.0 copy-start.3
  3.2 0.8 %copy-done.3 = bf16[256,128]{1,0:T(8,128)(2,1)S(1)} copy-done((bf16[256,128]{1,0:T(8,128)(2,1)S(1)}, bf16[256,128]{1,0:T(8,128)(2,1)}, u32[]{:S(2)}) %copy-start.3) | copy-done | bytes 65560
  4.0 3.0 %collective-permute-start = (bf16[2,256,128]{2,1,0:T(8,128)(2,1)S(1)}, bf16[2,256,128]{2,1,0:T(8,128)(2,1)S(1)}, u32[]{:S(2)}, u32[]{:S(2)}) collective-permute-start(bf16[2,256,128]{2,1,0:T(8,128)(2,1)S(1)} %get-tuple-element.11.refs_0_), channel_id=1, source_target_pairs={{0,16},{4,20},{8,24},{12,28},{16,0},{20,4},{24,8},{28,12},{1,17},{... | collective-permute-start | bytes 393224 | tf_op jit(solution)/shard_map/ppermute | solution.py:176
  7.0 7.2 %all-gather = bf16[8,256,128]{2,1,0:T(8,128)(2,1)S(1)} all-gather(bf16[2,256,128]{2,1,0:T(8,128)(2,1)S(1)} %get-tuple-element.10), channel_id=2, replica_groups={{0,4,8,12},{16,20,24,28},{1,5,9,13},{17,21,25,29},{2,6,10,14},{18,22,26..., dimensions={0}, use_global_device_ids=true | all-gather | bytes 655360 | tf_op jit(solution)/shard_map/all_gather | solution.py:183
  14.2 0.0 copy-start.4
  14.2 0.1 pad_add_fusion.place_ref
  14.3 0.0 copy-start.5
  14.3 0.0 collective-permute-done.refs_1_
  14.3 0.6 %copy-done.4 = s32[16,16]{1,0:T(8,128)S(1)} copy-done((s32[16,16]{1,0:T(8,128)S(1)}, s32[16,16]{1,0:T(8,128)}, u32[]{:S(2)}) %copy-start.4) | copy-done | bytes 1048
  14.9 0.0 copy-done.5
  14.9 1.6 %shard_map.86 = f32[3,1024]{1,0:T(4,128)S(1)} custom-call(s32[4]{0:T(128)S(1)} %pad_add_fusion.place_ref, s32[16]{0:T(128)S(1)} %copy-done.5, s32[16,16]{1,0:T(8,128)S(1)} %copy-done.4, bf16[4,2,256,128]{3,2,1,0:T(8,128)(2,1)S(1)} %bitcast.6, bf16[2,256,128]{2,1,0:T(8,128)(2,1)S(1)} %get-tuple-element.11.refs_0_, ...), custom_call_target="tpu_custom_call" | custom-call | flops 268435456 | bytes 799824 | tf_op jit(solution)/shard_map/pallas_call | solution.py:38
  16.6 5.2 %all-gather.2.stats_ref = f32[4,3,1024]{2,1,0:T(4,128)S(1)} all-gather(f32[1,3,1024]{2,1,0:T(4,128)S(1)} %bitcast.8), channel_id=3, replica_groups={{0,4,8,12},{16,20,24,28},{1,5,9,13},{17,21,25,29},{2,6,10,14},{18,22,26..., dimensions={0}, use_global_device_ids=true | all-gather | bytes 61440 | tf_op jit(solution)/shard_map/all_gather | solution.py:193
  21.8 2.9 %shard_map.87 = (bf16[2,4,2,32,256]{4,3,2,1,0:T(8,128)(2,1)}, f32[128,256]{1,0:T(8,128)S(1)}, bf16[128,256]{1,0:T(8,128)(2,1)S(1)}, bf16[128,256]{1,0:T(8,128)(2,1)S(1)}, bf16[128,256]{1,0:T(8,128)(2,1)S(1)}) custom-call(s32[4]{0:T(128)S(1)} %pad_add_fusion.place_ref, s32[16]{0:T(128)S(1)} %copy-done.5, s32[16,16]{1,0:T(8,128)S(1)} %copy-done.4, ...), custom_call_target="tpu_custom_call" | custom-call | flops 671088640 | bytes 1426512 | tf_op jit(solution)/shard_map/pallas_call | solution.py:38
  24.7 4.9 %all-to-all-start = ((bf16[8,2,32,256]{3,2,1,0:T(8,128)(2,1)}), bf16[8,2,32,256]{3,2,1,0:T(8,128)(2,1)S(1)}, u32[]{:S(2)}, u32[]{:S(2)}) async-start(bf16[8,2,32,256]{3,2,1,0:T(8,128)(2,1)} %bitcast.5), calls=%async_computation | async-start | bytes 524288 | tf_op jit(solution)/shard_map/all_to_all | solution.py:214
  29.6 0.1 collective-permute-start.1
  29.7 0.8 %collective-permute-start.2 = (bf16[128,256]{1,0:T(8,128)(2,1)S(1)}, bf16[128,256]{1,0:T(8,128)(2,1)S(1)}, u32[]{:S(2)}, u32[]{:S(2)}) collective-permute-start(bf16[128,256]{1,0:T(8,128)(2,1)S(1)} %get-tuple-element.14), channel_id=1, source_target_pairs={{0,8},{4,12},{8,0},{12,4},{16,24},{20,28},{24,16},{28,20},{1,9},{5... | collective-permute-start | bytes 196616 | tf_op jit(solution)/shard_map/ppermute | solution.py:176
  30.5 1.0 %collective-permute-start.3 = (bf16[128,256]{1,0:T(8,128)(2,1)S(1)}, bf16[128,256]{1,0:T(8,128)(2,1)S(1)}, u32[]{:S(2)}, u32[]{:S(2)}) collective-permute-start(bf16[128,256]{1,0:T(8,128)(2,1)S(1)} %get-tuple-element.15), channel_id=1, source_target_pairs={{0,12},{4,8},{8,4},{12,0},{16,28},{20,24},{24,20},{28,16},{1,13},{... | collective-permute-start | bytes 196616 | tf_op jit(solution)/shard_map/ppermute | solution.py:176
  31.5 0.0 collective-permute-done.1.refs_0_
  31.5 3.1 %collective-permute-done.2.refs_1_ = bf16[128,256]{1,0:T(8,128)(2,1)S(1)} collective-permute-done((bf16[128,256]{1,0:T(8,128)(2,1)S(1)}, bf16[128,256]{1,0:T(8,128)(2,1)S(1)}, u32[]{:S(2)}, u32[]{:S(2)}) %collective-permute-start.2) | collective-permute-done | bytes 65568 | tf_op jit(solution)/shard_map/ppermute | solution.py:176
  34.6 0.5 %collective-permute-done.3.refs_2_ = bf16[128,256]{1,0:T(8,128)(2,1)S(1)} collective-permute-done((bf16[128,256]{1,0:T(8,128)(2,1)S(1)}, bf16[128,256]{1,0:T(8,128)(2,1)S(1)}, u32[]{:S(2)}, u32[]{:S(2)}) %collective-permute-start.3) | collective-permute-done | bytes 65568 | tf_op jit(solution)/shard_map/ppermute | solution.py:176
  35.1 4.8 %all-to-all-done.refs_3_ = bf16[8,2,32,256]{3,2,1,0:T(8,128)(2,1)S(1)} async-done(((bf16[8,2,32,256]{3,2,1,0:T(8,128)(2,1)}), bf16[8,2,32,256]{3,2,1,0:T(8,128)(2,1)S(1)}, u32[]{:S(2)}, u32[]{:S(2)}) %all-to-all-start) | async-done | bytes 262176 | tf_op jit(solution)/shard_map/all_to_all | solution.py:214
  39.9 0.8 %shard_map.88 = (f32[256,128]{1,0:T(8,128)}, f32[256,32]{1,0:T(8,128)S(1)}, f32[256,32]{1,0:T(8,128)S(1)}) custom-call(f32[128,256]{1,0:T(8,128)S(1)} %get-tuple-element.12.own_ref, bf16[128,256]{1,0:T(8,128)(2,1)S(1)} %collective-permute-done.1.refs_0_, bf16[128,256]{1,0:T(8,128)(2,1)S(1)} %collective-permute-done.2.refs_1_, ...), custom_call_target="tpu_custom_call" | custom-call | bytes 786432 | tf_op jit(solution)/shard_map/pallas_call | solution.py:38
  40.7 0.7 %copy.11 = f32[256,32]{0,1:T(8,128)} copy(f32[256,32]{1,0:T(8,128)S(1)} %get-tuple-element.21) | data formatting | bytes 65536 | tf_op jit(solution)/shard_map/pallas_call | solution.py:38
  41.4 0.7 %copy.12 = f32[256,32]{0,1:T(8,128)} copy(f32[256,32]{1,0:T(8,128)S(1)} %get-tuple-element.22) | data formatting | bytes 65536 | tf_op jit(solution)/shard_map/pallas_call | solution.py:38
  (1 shorter events, 0.0 us)
Async XLA Ops:
  0.6 0.8 %copy-start = (bf16[256,128]{1,0:T(8,128)(2,1)S(1)}, bf16[256,128]{1,0:T(8,128)(2,1)}, u32[]{:S(2)}) copy-start(bf16[256,128]{1,0:T(8,128)(2,1)} %q_ref.1) | copy-start | bytes 196612
  1.5 0.8 %copy-start.1 = (bf16[256,128]{1,0:T(8,128)(2,1)S(1)}, bf16[256,128]{1,0:T(8,128)(2,1)}, u32[]{:S(2)}) copy-start(bf16[256,128]{1,0:T(8,128)(2,1)} %g_ref.1) | copy-start | bytes 196612
  2.3 0.8 %copy-start.2 = (bf16[256,128]{1,0:T(8,128)(2,1)S(1)}, bf16[256,128]{1,0:T(8,128)(2,1)}, u32[]{:S(2)}) copy-start(bf16[256,128]{1,0:T(8,128)(2,1)} %k_ref.1) | copy-start | bytes 196612
  3.2 0.8 %copy-start.3 = (bf16[256,128]{1,0:T(8,128)(2,1)S(1)}, bf16[256,128]{1,0:T(8,128)(2,1)}, u32[]{:S(2)}) copy-start(bf16[256,128]{1,0:T(8,128)(2,1)} %v_ref.1) | copy-start | bytes 196612
  4.0 10.3 %collective-permute-start = (bf16[2,256,128]{2,1,0:T(8,128)(2,1)S(1)}, bf16[2,256,128]{2,1,0:T(8,128)(2,1)S(1)}, u32[]{:S(2)}, u32[]{:S(2)}) collective-permute-start(bf16[2,256,128]{2,1,0:T(8,128)(2,1)S(1)} %get-tuple-element.11.refs_0_), channel_id=1, source_target_pairs={{0,16},{4,20},{8,24},{12,28},{16,0},{20,4},{24,8},{28,12},{1,17},{... | collective-permute-start | bytes 393224 | tf_op jit(solution)/shard_map/ppermute | solution.py:176
  14.2 0.7 %copy-start.4 = (s32[16,16]{1,0:T(8,128)S(1)}, s32[16,16]{1,0:T(8,128)}, u32[]{:S(2)}) copy-start(s32[16,16]{1,0:T(8,128)} %mask_ref.3) | copy-start | bytes 3076
  14.3 0.7 %copy-start.5 = (s32[16]{0:T(128)S(1)}, s32[16]{0:T(128)}, u32[]{:S(2)}) copy-start(s32[16]{0:T(128)} %ids_ref.3) | copy-start | bytes 196
  24.7 15.2 %all-to-all-start = ((bf16[8,2,32,256]{3,2,1,0:T(8,128)(2,1)}), bf16[8,2,32,256]{3,2,1,0:T(8,128)(2,1)S(1)}, u32[]{:S(2)}, u32[]{:S(2)}) async-start(bf16[8,2,32,256]{3,2,1,0:T(8,128)(2,1)} %bitcast.5), calls=%async_computation | async-start | bytes 524288 | tf_op jit(solution)/shard_map/all_to_all | solution.py:214
  29.6 1.9 %collective-permute-start.1 = (bf16[128,256]{1,0:T(8,128)(2,1)S(1)}, bf16[128,256]{1,0:T(8,128)(2,1)S(1)}, u32[]{:S(2)}, u32[]{:S(2)}) collective-permute-start(bf16[128,256]{1,0:T(8,128)(2,1)S(1)} %get-tuple-element.13), channel_id=1, source_target_pairs={{0,4},{4,0},{8,12},{12,8},{16,20},{20,16},{24,28},{28,24},{1,5},{5... | collective-permute-start | bytes 196616 | tf_op jit(solution)/shard_map/ppermute | solution.py:176
  29.7 4.9 %collective-permute-start.2 = (bf16[128,256]{1,0:T(8,128)(2,1)S(1)}, bf16[128,256]{1,0:T(8,128)(2,1)S(1)}, u32[]{:S(2)}, u32[]{:S(2)}) collective-permute-start(bf16[128,256]{1,0:T(8,128)(2,1)S(1)} %get-tuple-element.14), channel_id=1, source_target_pairs={{0,8},{4,12},{8,0},{12,4},{16,24},{20,28},{24,16},{28,20},{1,9},{5... | collective-permute-start | bytes 196616 | tf_op jit(solution)/shard_map/ppermute | solution.py:176
  30.5 4.5 %collective-permute-start.3 = (bf16[128,256]{1,0:T(8,128)(2,1)S(1)}, bf16[128,256]{1,0:T(8,128)(2,1)S(1)}, u32[]{:S(2)}, u32[]{:S(2)}) collective-permute-start(bf16[128,256]{1,0:T(8,128)(2,1)S(1)} %get-tuple-element.15), channel_id=1, source_target_pairs={{0,12},{4,8},{8,4},{12,0},{16,28},{20,24},{24,20},{28,16},{1,13},{... | collective-permute-start | bytes 196616 | tf_op jit(solution)/shard_map/ppermute | solution.py:176

commit v2 on v1

v2 whole, which is shorter than its diff:
```python
import functools
import math

import jax
import jax.numpy as jnp
from jax import lax
from jax.experimental import pallas as pl
from jax.experimental.pallas import tpu as pltpu
from jax.sharding import PartitionSpec as P

GROUP = 4
SHARE = 4
MASKED = -1e30
FLOOR = -1e20
VMEM_LIMIT = 48 * 1024 * 1024
PACK_LIMIT = 65400 * 1024

F32 = jnp.float32
BF16 = jnp.bfloat16


def dot(left, right, left_dim, right_dim):
    return lax.dot_general(
        left, right, (((left_dim,), (right_dim,)), ((), ())), preferred_element_type=F32
    )


def vmem():
    return pl.BlockSpec(memory_space=pltpu.VMEM)


def call(kernel, out_shape, ins, in_specs=None, out_specs=None, flops=0, scratch=(), limit=VMEM_LIMIT):
    size = sum(math.prod(x.shape) * x.dtype.itemsize for x in list(ins) + list(out_shape))
    return pl.pallas_call(
        kernel,
        out_shape=out_shape,
        in_specs=in_specs or [vmem() for _ in ins],
        out_specs=out_specs or [vmem() for _ in out_shape],
        scratch_shapes=list(scratch),
        compiler_params=pltpu.CompilerParams(vmem_limit_bytes=limit),
        cost_estimate=pl.CostEstimate(flops=flops, bytes_accessed=size, transcendentals=0),
    )(*ins)


def pack_kernel(
    units, q_ref, g_ref, k_ref, v_ref, ids_ref, mask_ref, qg_ref, kv_ref, limit_ref, ids, mask, sems
):
    copies = [
        pltpu.make_async_copy(source, target, sems.at[i])
        for i, (source, target) in enumerate(
            [
                (ids_ref, ids),
                (mask_ref, mask),
                (k_ref, kv_ref.at[0]),
                (v_ref, kv_ref.at[1]),
                (q_ref, qg_ref.at[0]),
                (g_ref, qg_ref.at[1]),
            ]
        )
    ]
    for copy in copies:
        copy.start()
    half = k_ref.shape[0] // 2
    ctx_index = lax.axis_index("ctx")
    group, place = ctx_index // SHARE, ctx_index % SHARE
    lane = lax.broadcasted_iota(jnp.int32, (1, half), 1)
    copies[0].wait()
    copies[1].wait()
    query_blocks = [ids[group * SHARE * 2 + i] for i in range(SHARE * 2)]
    for u in range(units):
        for part in range(2):
            key_block = ids[((group ^ u) * SHARE + place) * 2 + part]
            row = u * 2 + part
            for i, query_block in enumerate(query_blocks):
                linked = mask[query_block, key_block] > 0
                start = jnp.where(linked, (query_block - key_block) * half, -2 * half)
                limit_ref[row : row + 1, i * half : (i + 1) * half] = lane + start
    for copy in copies[2:]:
        copy.wait()


def masked_scores(limit_ref, q_rows, keys_here, u, factor):
    half = keys_here.shape[0] // 2
    scores = dot(keys_here, q_rows, 1, 1) * factor
    row = lax.broadcasted_iota(jnp.int32, (half, 1), 0)
    halves = [
        jnp.where(
            limit_ref[u * 2 + part : u * 2 + part + 1, :] >= row,
            scores[part * half : (part + 1) * half],
            MASKED,
        )
        for part in range(2)
    ]
    return jnp.concatenate(halves, axis=0)


def stats_kernel(units, factor, limit_ref, qg_ref, *refs):
    kv_refs, out_ref = refs[:units], refs[units]
    width = qg_ref.shape[-1]
    q_rows = qg_ref[:, 0].reshape(-1, width)
    g_rows = qg_ref[:, 1].reshape(-1, width)
    scores = [masked_scores(limit_ref, q_rows, kv_refs[u][0], u, factor) for u in range(units)]
    top = functools.reduce(jnp.maximum, [jnp.max(s, axis=0, keepdims=True) for s in scores])
    top = jnp.maximum(top, FLOOR)
    total = jnp.zeros_like(top)
    weighted = jnp.zeros_like(top)
    for u in range(units):
        weights = jnp.exp2(scores[u] - top)
        total += jnp.sum(weights, axis=0, keepdims=True)
        grads = dot(kv_refs[u][1], g_rows, 1, 1)
        weighted += jnp.sum(weights * grads, axis=0, keepdims=True)
    out_ref[0:1, :] = top
    out_ref[1:2, :] = total
    out_ref[2:3, :] = weighted


def grads_kernel(units, factor, scale, limit_ref, qg_ref, stats_ref, *refs):
    kv_refs = refs[:units]
    kv_out_ref, ds_ref = refs[units:]
    width = qg_ref.shape[-1]
    sub = width // GROUP
    unit = qg_ref.shape[2]
    q_rows = qg_ref[:, 0].reshape(-1, width)
    g_rows = qg_ref[:, 1].reshape(-1, width)
    tops = [stats_ref[s, 0:1, :] for s in range(SHARE)]
    top = functools.reduce(jnp.maximum, tops)
    scaled = [jnp.exp2(t - top) for t in tops]
    total = sum(stats_ref[s, 1:2, :] * scaled[s] for s in range(SHARE))
    weighted = sum(stats_ref[s, 2:3, :] * scaled[s] for s in range(SHARE))
    log_total = top + jnp.log2(total)
    delta = weighted / total
    group = lax.axis_index("ctx") // SHARE
    for u in range(units):
        keys_here, values_here = kv_refs[u][0], kv_refs[u][1]
        scores = masked_scores(limit_ref, q_rows, keys_here, u, factor)
        probs = jnp.exp2(scores - log_total)
        dprobs = dot(values_here, g_rows, 1, 1)
        dscores = (probs * (dprobs - delta)).astype(BF16)
        ds_ref[u * unit : (u + 1) * unit] = dscores
        dv = dot(probs.astype(BF16), g_rows, 1, 0)
        dk = dot(dscores, q_rows, 1, 0) * scale
        dk = dk.T.astype(BF16)
        dv = dv.T.astype(BF16)
        for part in range(GROUP):
            kv_out_ref[group ^ u, part, 0] = dk[part * sub : (part + 1) * sub]
            kv_out_ref[group ^ u, part, 1] = dv[part * sub : (part + 1) * sub]


def query_kernel(units, scale, ds_ref, *refs):
    kv_refs, own_ref, far_refs = refs[:units], refs[units], refs[units + 1 : units + SHARE]
    dq_ref = refs[-1]
    unit = own_ref.shape[0]
    dq = sum(
        dot(kv_refs[u][0], ds_ref[u * unit : (u + 1) * unit], 0, 0) for u in range(units)
    )
    dq = (dq * scale).T
    for s in range(SHARE):
        dq_ref[s] = dq[s * unit : (s + 1) * unit]
    me = lax.axis_index("ctx") % SHARE
    own_ref[...] = dq_ref[me]
    for step in range(1, SHARE):
        far_refs[step - 1][...] = dq_ref[me ^ step].astype(BF16)


def final_kernel(own_ref, *refs):
    far_refs = refs[: SHARE - 1]
    kv_ref, dq_ref, dk_ref, dv_ref = refs[SHARE - 1 :]
    dq = own_ref[...]
    for ref in far_refs:
        dq += ref[...].astype(F32)
    dq_ref[...] = dq
    for which, out_ref in ((0, dk_ref), (1, dv_ref)):
        total = kv_ref[0, which].astype(F32)
        for source in range(1, kv_ref.shape[0]):
            total += kv_ref[source, which].astype(F32)
        out_ref[...] = total


def body(queries, keys, values, out_grad, block_ids, block_mask):
    unit, width = queries.shape
    ctx_size, lanes = lax.axis_size("ctx"), lax.axis_size("fsdp")
    units = ctx_size // SHARE
    rows = SHARE * unit
    sub = width // GROUP
    scale = width ** (-0.5)
    factor = scale * math.log2(math.e)
    if keys.shape[1] != width:
        key_group = lax.axis_index("fsdp") // GROUP
        keys = lax.dynamic_slice_in_dim(keys, key_group * width, width, 1)
        values = lax.dynamic_slice_in_dim(values, key_group * width, width, 1)

    def swap(x, step):
        return lax.ppermute(x, "ctx", [(i, i ^ step) for i in range(ctx_size)])

    pair = jax.ShapeDtypeStruct((2, unit, width), BF16)
    qg, kv, limits = call(
        functools.partial(pack_kernel, units),
        [pair, pair, jax.ShapeDtypeStruct((2 * units, rows), jnp.int32)],
        [queries, out_grad, keys, values, block_ids, block_mask],
        in_specs=[pl.BlockSpec(memory_space=pl.ANY)] * 6,
        limit=PACK_LIMIT,
        scratch=[
            pltpu.SMEM(block_ids.shape, jnp.int32),
            pltpu.SMEM(block_mask.shape, jnp.int32),
            pltpu.SemaphoreType.DMA((6,)),
        ],
    )
    groups = [list(range(g * SHARE, (g + 1) * SHARE)) for g in range(units)]
    kvs = [kv] + [swap(kv, u * SHARE) for u in range(1, units)]
    qgs = lax.all_gather(qg, "ctx", axis_index_groups=groups)

    product = 2 * rows * units * unit * width
    (stats,) = call(
        functools.partial(stats_kernel, units, factor),
        [jax.ShapeDtypeStruct((3, rows), F32)],
        [limits, qgs] + kvs,
        flops=2 * product,
    )
    all_stats = lax.all_gather(stats, "ctx", axis_index_groups=groups)
    kv_parts, dscores = call(
        functools.partial(grads_kernel, units, factor, scale),
        [
            jax.ShapeDtypeStruct((units, GROUP, 2, sub, unit), BF16),
            jax.ShapeDtypeStruct((units * unit, rows), BF16),
        ],
        [limits, qgs, all_stats] + kvs,
        flops=4 * product,
    )
    places = [
        [(g * SHARE + s) * lanes + head * GROUP + h for g in range(units) for h in range(GROUP)]
        for s in range(SHARE)
        for head in range(lanes // GROUP)
    ]
    kv_parts = kv_parts.reshape(units * GROUP, 2, sub, unit)
    kv_parts = lax.all_to_all(
        kv_parts, ("ctx", "fsdp"), 0, 0, axis_index_groups=places, tiled=True
    )
    own, *far = call(
        functools.partial(query_kernel, units, scale),
        [jax.ShapeDtypeStruct((unit, width), F32)]
        + [jax.ShapeDtypeStruct((unit, width), BF16)] * (SHARE - 1),
        [dscores] + kvs,
        flops=product,
        scratch=[pltpu.VMEM((SHARE, unit, width), F32)],
    )
    far = [swap(x, step + 1) for step, x in enumerate(far)]
    dq, dk, dv = call(
        final_kernel,
        [
            jax.ShapeDtypeStruct((unit, width), F32),
            jax.ShapeDtypeStruct((sub, unit), F32),
            jax.ShapeDtypeStruct((sub, unit), F32),
        ],
        [own] + far + [kv_parts],
    )
    return dq, dk.T, dv.T


def solution(mesh):
    in_specs = (P("ctx", "fsdp"), P("ctx", None), P("ctx", None), P("ctx", "fsdp"), P(), P())
    out_specs = (P("ctx", "fsdp"), P("ctx", "fsdp"), P("ctx", "fsdp"))
    return jax.shard_map(body, mesh=mesh, in_specs=in_specs, out_specs=out_specs, check_vma=False)
```

time: 42.5 us -> 37.5 us (0.88)
  local copies, waits for them, and re-layouts: 5.38 us -> 0.01 us
  Pallas kernels: 5.33 us -> 6.13 us
  waiting for transfers between devices: 8.41 us -> 7.83 us
    unnamed x12 -> x4, local copies, waits for them, and re-layouts: 4 us -> 0.01 us
    pallas_call x2 -> x0, local copies, waits for them, and re-layouts: 1.38 us -> none  [call(): pl.pallas_call(kernel, out_shape=out_shape, in_specs=specs, out_specs=[vm...]
    pallas_call x4 -> x5, Pallas kernels: 5.33 us -> 6.13 us  [call(): pl.pallas_call(kernel, out_shape=out_shape, in_specs=in_specs or [vmem()...]
    all_to_all x1, waiting for transfers between devices: 4.83 us -> 4.24 us  [body(): lax.all_to_all(kv_parts, ('ctx', 'fsdp'), 0, 0, axis_index_groups=places,...]
  transfers between devices with their start and end apart: 5 -> 5, of which waited for: 3 -> 3; matrix products, arithmetic and copies ran while one was open for 0% -> 0% of each run, Pallas kernels for 0% -> 1%
where the time goes in v2:
time: 37.5 us; the launch traced here: 37.2 us
  blocking collectives  12.7 us (34%)
  starting transfers between devices  9.86 us (26%)
  waiting for transfers between devices  7.83 us (21%)
  Pallas kernels  6.13 us (16%)
  between operations  0.67 us (2%)
    all_gather x1, blocking collectives, body(): qgs = lax.all_gather(qg, 'ctx', axis_index_groups=groups)  7.5 us
    pallas_call x5, Pallas kernels, call(): pl.pallas_call(kernel, out_shape=out_shape, in_specs=in_specs or [vmem()...  6.13 us
    all_gather x1, blocking collectives, body(): all_stats = lax.all_gather(stats, 'ctx', axis_index_groups=groups)  5.25 us
    ppermute x4, starting transfers between devices, swap(): return lax.ppermute(x, 'ctx', [(i, i ^ step) for i in range(ctx_size)])  4.97 us
    all_to_all x1, starting transfers between devices, body(): lax.all_to_all(kv_parts, ('ctx', 'fsdp'), 0, 0, axis_index_groups=places,...  4.89 us
    all_to_all x1, waiting for transfers between devices, body(): lax.all_to_all(kv_parts, ('ctx', 'fsdp'), 0, 0, axis_index_groups=places,...  4.24 us
    ppermute x4, waiting for transfers between devices, swap(): return lax.ppermute(x, 'ctx', [(i, i ^ step) for i in range(ctx_size)])  3.6 us
  transfers between devices with their start and end apart: 5, of which 3 were waited for; matrix products, arithmetic and copies ran while one was open for 0% of the time, Pallas kernels for 1%

profile of v2, /device:TPU:0, one launch (start us, length us, event | category | flops | bytes accessed | tf_op | source)
XLA Modules:
  0.0 37.2 jit_solution(91509571383301093)
XLA Ops:
  0.6 1.7 %shard_map.85 = (bf16[2,256,128]{2,1,0:T(8,128)(2,1)}, bf16[2,256,128]{2,1,0:T(8,128)(2,1)}, s32[4,1024]{1,0:T(4,128)}) custom-call(bf16[256,128]{1,0:T(8,128)(2,1)} %q_ref.1, bf16[256,128]{1,0:T(8,128)(2,1)} %g_ref.1, bf16[256,128]{1,0:T(8,128)(2,1)} %k_ref.1, bf16[256,128]{1,0:T(8,128)(2,1)} %v_ref.1, s32[16]{0:T(128)} %ids_ref.1, s32[16,16]{1,0:T(8,128)} %mask_ref.1), custom_call_target="tpu_custom_call" | custom-call | bytes 541760 | tf_op jit(solution)/shard_map/pallas_call | solution.py:34
  2.3 3.0 %collective-permute-start = (bf16[2,256,128]{2,1,0:T(8,128)(2,1)}, bf16[2,256,128]{2,1,0:T(8,128)(2,1)S(1)}, u32[]{:S(2)}, u32[]{:S(2)}) collective-permute-start(bf16[2,256,128]{2,1,0:T(8,128)(2,1)} %get-tuple-element.17.refs_0_), channel_id=1, source_target_pairs={{0,16},{4,20},{8,24},{12,28},{16,0},{20,4},{24,8},{28,12},{1,17},{... | collective-permute-start | bytes 393224 | tf_op jit(solution)/shard_map/ppermute | solution.py:193
  5.4 0.0 copy-start
  5.4 0.0 copy-start.1
  5.4 7.5 %all-gather = bf16[8,256,128]{2,1,0:T(8,128)(2,1)S(1)} all-gather(bf16[2,256,128]{2,1,0:T(8,128)(2,1)} %get-tuple-element.16), channel_id=2, replica_groups={{0,4,8,12},{16,20,24,28},{1,5,9,13},{17,21,25,29},{2,6,10,14},{18,22,26..., dimensions={0}, use_global_device_ids=true | all-gather | bytes 655360 | tf_op jit(solution)/shard_map/all_gather | solution.py:210
  12.9 0.0 collective-permute-done.refs_1_
  12.9 0.0 copy-done
  12.9 0.0 copy-done.1
  12.9 1.0 %shard_map.86 = f32[3,1024]{1,0:T(4,128)S(1)} custom-call(s32[4,1024]{1,0:T(4,128)S(1)} %copy-done.1, bf16[4,2,256,128]{3,2,1,0:T(8,128)(2,1)S(1)} %bitcast.5, bf16[2,256,128]{2,1,0:T(8,128)(2,1)S(1)} %copy-done, bf16[2,256,128]{2,1,0:T(8,128)(2,1)S(1)} %collective-permute-done.refs_1_), custom_call_target="tpu_custom_call" | custom-call | flops 268435456 | bytes 815104 | tf_op jit(solution)/shard_map/pallas_call | solution.py:34
  13.9 5.2 %all-gather.2.stats_ref = f32[4,3,1024]{2,1,0:T(4,128)S(1)} all-gather(f32[1,3,1024]{2,1,0:T(4,128)S(1)} %bitcast.7), channel_id=3, replica_groups={{0,4,8,12},{16,20,24,28},{1,5,9,13},{17,21,25,29},{2,6,10,14},{18,22,26..., dimensions={0}, use_global_device_ids=true | all-gather | bytes 61440 | tf_op jit(solution)/shard_map/all_gather | solution.py:219
  19.1 2.2 %shard_map.87 = (bf16[2,4,2,32,256]{4,3,2,1,0:T(8,128)(2,1)}, bf16[512,1024]{1,0:T(8,128)(2,1)S(1)}) custom-call(s32[4,1024]{1,0:T(4,128)S(1)} %copy-done.1, bf16[4,2,256,128]{3,2,1,0:T(8,128)(2,1)S(1)} %bitcast.6, f32[4,3,1024]{2,1,0:T(4,128)S(1)} %all-gather.2.stats_ref, bf16[2,256,128]{2,1,0:T(8,128)(2,1)S(1)} %copy-done, ...), custom_call_target="tpu_custom_call" | custom-call | flops 536870912 | bytes 2162688 | tf_op jit(solution)/shard_map/pallas_call | solution.py:34
  21.4 4.9 %all-to-all-start = ((bf16[8,2,32,256]{3,2,1,0:T(8,128)(2,1)}), bf16[8,2,32,256]{3,2,1,0:T(8,128)(2,1)S(1)}, u32[]{:S(2)}, u32[]{:S(2)}) async-start(bf16[8,2,32,256]{3,2,1,0:T(8,128)(2,1)} %bitcast.2), calls=%async_computation | async-start | bytes 524288 | tf_op jit(solution)/shard_map/all_to_all | solution.py:235
  26.3 0.5 %shard_map.88 = (f32[256,128]{1,0:T(8,128)S(1)}, bf16[256,128]{1,0:T(8,128)(2,1)S(1)}, bf16[256,128]{1,0:T(8,128)(2,1)S(1)}, bf16[256,128]{1,0:T(8,128)(2,1)S(1)}) custom-call(bf16[512,1024]{1,0:T(8,128)(2,1)S(1)} %get-tuple-element.18.ds_ref, bf16[2,256,128]{2,1,0:T(8,128)(2,1)S(1)} %copy-done, bf16[2,256,128]{2,1,0:T(8,128)(2,1)S(1)} %collective-permute-done.refs_1_), custom_call_target="tpu_custom_call" | custom-call | flops 134217728 | bytes 1638400 | tf_op jit(solution)/shard_map/pallas_call | solution.py:34
  26.8 0.1 collective-permute-start.1
  26.9 0.9 %collective-permute-start.2 = (bf16[256,128]{1,0:T(8,128)(2,1)S(1)}, bf16[256,128]{1,0:T(8,128)(2,1)S(1)}, u32[]{:S(2)}, u32[]{:S(2)}) collective-permute-start(bf16[256,128]{1,0:T(8,128)(2,1)S(1)} %get-tuple-element.21), channel_id=1, source_target_pairs={{0,8},{4,12},{8,0},{12,4},{16,24},{20,28},{24,16},{28,20},{1,9},{5... | collective-permute-start | bytes 196616 | tf_op jit(solution)/shard_map/ppermute | solution.py:193
  27.8 1.0 %collective-permute-start.3 = (bf16[256,128]{1,0:T(8,128)(2,1)S(1)}, bf16[256,128]{1,0:T(8,128)(2,1)S(1)}, u32[]{:S(2)}, u32[]{:S(2)}) collective-permute-start(bf16[256,128]{1,0:T(8,128)(2,1)S(1)} %get-tuple-element.22), channel_id=1, source_target_pairs={{0,12},{4,8},{8,4},{12,0},{16,28},{20,24},{24,20},{28,16},{1,13},{... | collective-permute-start | bytes 196616 | tf_op jit(solution)/shard_map/ppermute | solution.py:193
  28.7 0.0 collective-permute-done.1.refs_0_
  28.7 3.1 %collective-permute-done.2.refs_1_ = bf16[256,128]{1,0:T(8,128)(2,1)S(1)} collective-permute-done((bf16[256,128]{1,0:T(8,128)(2,1)S(1)}, bf16[256,128]{1,0:T(8,128)(2,1)S(1)}, u32[]{:S(2)}, u32[]{:S(2)}) %collective-permute-start.2) | collective-permute-done | bytes 65568 | tf_op jit(solution)/shard_map/ppermute | solution.py:193
  31.8 0.5 %collective-permute-done.3.refs_2_ = bf16[256,128]{1,0:T(8,128)(2,1)S(1)} collective-permute-done((bf16[256,128]{1,0:T(8,128)(2,1)S(1)}, bf16[256,128]{1,0:T(8,128)(2,1)S(1)}, u32[]{:S(2)}, u32[]{:S(2)}) %collective-permute-start.3) | collective-permute-done | bytes 65568 | tf_op jit(solution)/shard_map/ppermute | solution.py:193
  32.3 4.2 %all-to-all-done.refs_3_ = bf16[8,2,32,256]{3,2,1,0:T(8,128)(2,1)S(1)} async-done(((bf16[8,2,32,256]{3,2,1,0:T(8,128)(2,1)}), bf16[8,2,32,256]{3,2,1,0:T(8,128)(2,1)S(1)}, u32[]{:S(2)}, u32[]{:S(2)}) %all-to-all-start) | async-done | bytes 262176 | tf_op jit(solution)/shard_map/all_to_all | solution.py:235
  36.5 0.7 %shard_map.89 = (f32[256,128]{1,0:T(8,128)}, f32[32,256]{1,0:T(8,128)}, f32[32,256]{1,0:T(8,128)}) custom-call(f32[256,128]{1,0:T(8,128)S(1)} %get-tuple-element.19.own_ref, bf16[256,128]{1,0:T(8,128)(2,1)S(1)} %collective-permute-done.1.refs_0_, bf16[256,128]{1,0:T(8,128)(2,1)S(1)} %collective-permute-done.2.refs_1_, ...), custom_call_target="tpu_custom_call" | custom-call | bytes 786432 | tf_op jit(solution)/shard_map/pallas_call | solution.py:34
Async XLA Ops:
  2.3 10.5 %collective-permute-start = (bf16[2,256,128]{2,1,0:T(8,128)(2,1)}, bf16[2,256,128]{2,1,0:T(8,128)(2,1)S(1)}, u32[]{:S(2)}, u32[]{:S(2)}) collective-permute-start(bf16[2,256,128]{2,1,0:T(8,128)(2,1)} %get-tuple-element.17.refs_0_), channel_id=1, source_target_pairs={{0,16},{4,20},{8,24},{12,28},{16,0},{20,4},{24,8},{28,12},{1,17},{... | collective-permute-start | bytes 393224 | tf_op jit(solution)/shard_map/ppermute | solution.py:193
  5.4 7.5 %copy-start = (bf16[2,256,128]{2,1,0:T(8,128)(2,1)S(1)}, bf16[2,256,128]{2,1,0:T(8,128)(2,1)}, u32[]{:S(2)}) copy-start(bf16[2,256,128]{2,1,0:T(8,128)(2,1)} %get-tuple-element.17.refs_0_) | copy-start | bytes 393220
  5.4 7.5 %copy-start.1 = (s32[4,1024]{1,0:T(4,128)S(1)}, s32[4,1024]{1,0:T(4,128)}, u32[]{:S(2)}) copy-start(s32[4,1024]{1,0:T(4,128)} %get-tuple-element.15.limit_ref) | copy-start | bytes 49156
  21.4 15.2 %all-to-all-start = ((bf16[8,2,32,256]{3,2,1,0:T(8,128)(2,1)}), bf16[8,2,32,256]{3,2,1,0:T(8,128)(2,1)S(1)}, u32[]{:S(2)}, u32[]{:S(2)}) async-start(bf16[8,2,32,256]{3,2,1,0:T(8,128)(2,1)} %bitcast.2), calls=%async_computation | async-start | bytes 524288 | tf_op jit(solution)/shard_map/all_to_all | solution.py:235
  26.8 1.9 %collective-permute-start.1 = (bf16[256,128]{1,0:T(8,128)(2,1)S(1)}, bf16[256,128]{1,0:T(8,128)(2,1)S(1)}, u32[]{:S(2)}, u32[]{:S(2)}) collective-permute-start(bf16[256,128]{1,0:T(8,128)(2,1)S(1)} %get-tuple-element.20), channel_id=1, source_target_pairs={{0,4},{4,0},{8,12},{12,8},{16,20},{20,16},{24,28},{28,24},{1,5},{5... | collective-permute-start | bytes 196616 | tf_op jit(solution)/shard_map/ppermute | solution.py:193
  26.9 4.9 %collective-permute-start.2 = (bf16[256,128]{1,0:T(8,128)(2,1)S(1)}, bf16[256,128]{1,0:T(8,128)(2,1)S(1)}, u32[]{:S(2)}, u32[]{:S(2)}) collective-permute-start(bf16[256,128]{1,0:T(8,128)(2,1)S(1)} %get-tuple-element.21), channel_id=1, source_target_pairs={{0,8},{4,12},{8,0},{12,4},{16,24},{20,28},{24,16},{28,20},{1,9},{5... | collective-permute-start | bytes 196616 | tf_op jit(solution)/shard_map/ppermute | solution.py:193
  27.8 4.6 %collective-permute-start.3 = (bf16[256,128]{1,0:T(8,128)(2,1)S(1)}, bf16[256,128]{1,0:T(8,128)(2,1)S(1)}, u32[]{:S(2)}, u32[]{:S(2)}) collective-permute-start(bf16[256,128]{1,0:T(8,128)(2,1)S(1)} %get-tuple-element.22), channel_id=1, source_target_pairs={{0,12},{4,8},{8,4},{12,0},{16,28},{20,24},{24,20},{28,16},{1,13},{... | collective-permute-start | bytes 196616 | tf_op jit(solution)/shard_map/ppermute | solution.py:193

commit v3 on v2

v3 whole, which is shorter than its diff:
```python
import functools
import math

import jax
import jax.numpy as jnp
from jax import lax
from jax.experimental import pallas as pl
from jax.experimental.pallas import tpu as pltpu
from jax.sharding import PartitionSpec as P

GROUP = 4
SHARE = 4
MASKED = -1e30
FLOOR = -1e20
VMEM_LIMIT = 48 * 1024 * 1024

F32 = jnp.float32
BF16 = jnp.bfloat16


def dot(left, right, left_dim, right_dim):
    return lax.dot_general(
        left, right, (((left_dim,), (right_dim,)), ((), ())), preferred_element_type=F32
    )


def vmem():
    return pl.BlockSpec(memory_space=pltpu.VMEM)


def call(kernel, out_shape, ins, in_specs=None, flops=0, scratch=()):
    size = sum(math.prod(x.shape) * x.dtype.itemsize for x in list(ins) + list(out_shape))
    return pl.pallas_call(
        kernel,
        out_shape=out_shape,
        in_specs=in_specs or [vmem() for _ in ins],
        out_specs=[vmem() for _ in out_shape],
        scratch_shapes=list(scratch),
        compiler_params=pltpu.CompilerParams(vmem_limit_bytes=VMEM_LIMIT),
        cost_estimate=pl.CostEstimate(flops=flops, bytes_accessed=size, transcendentals=0),
    )(*ins)


def limits_kernel(units, half, ids_ref, mask_ref, limit_ref):
    ctx_index = lax.axis_index("ctx")
    lane = lax.broadcasted_iota(jnp.int32, (1, half), 1)
    query_blocks = [ids_ref[(ctx_index ^ r) * 2 + part] for r in range(SHARE) for part in range(2)]
    for u in range(units):
        for part in range(2):
            key_block = ids_ref[(ctx_index ^ (u * SHARE)) * 2 + part]
            row = u * 2 + part
            for i, query_block in enumerate(query_blocks):
                linked = mask_ref[query_block, key_block] > 0
                start = jnp.where(linked, (query_block - key_block) * half, -2 * half)
                limit_ref[row : row + 1, i * half : (i + 1) * half] = lane + start


def masked_scores(limit_ref, q_rows, keys_here, u, r, factor):
    unit = keys_here.shape[0]
    half = unit // 2
    scores = dot(keys_here, q_rows, 1, 1) * factor
    row = lax.broadcasted_iota(jnp.int32, (half, 1), 0)
    halves = [
        jnp.where(
            limit_ref[u * 2 + part : u * 2 + part + 1, r * unit : (r + 1) * unit] >= row,
            scores[part * half : (part + 1) * half],
            MASKED,
        )
        for part in range(2)
    ]
    return jnp.concatenate(halves, axis=0)


def stats_kernel(units, factor, limit_ref, *refs):
    qg_refs, kv_refs, out_ref = refs[:SHARE], refs[SHARE:-1], refs[-1]
    me = lax.axis_index("ctx") % SHARE
    for r in range(SHARE):
        q_rows, g_rows = qg_refs[r][0], qg_refs[r][1]
        scores = [masked_scores(limit_ref, q_rows, kv_refs[u][0], u, r, factor) for u in range(units)]
        top = functools.reduce(jnp.maximum, [jnp.max(s, axis=0, keepdims=True) for s in scores])
        top = jnp.maximum(top, FLOOR)
        total = jnp.zeros_like(top)
        weighted = jnp.zeros_like(top)
        for u in range(units):
            weights = jnp.exp2(scores[u] - top)
            total += jnp.sum(weights, axis=0, keepdims=True)
            dprobs = dot(kv_refs[u][1], g_rows, 1, 1)
            weighted += jnp.sum(weights * dprobs, axis=0, keepdims=True)
        out_ref[me ^ r, 0:1, :] = top
        out_ref[me ^ r, 1:2, :] = total
        out_ref[me ^ r, 2:3, :] = weighted


def grads_kernel(wanted, factor, scale, limit_ref, stats_ref, *refs):
    qg_refs, refs = refs[:SHARE], refs[SHARE:]
    kv_refs, ds_ref, out_refs = refs[: len(wanted)], refs[len(wanted)], refs[len(wanted) + 1 :]
    _, unit, width = qg_refs[0].shape
    sub = width // GROUP
    me = lax.axis_index("ctx") % SHARE
    dk, dv = [None] * len(wanted), [None] * len(wanted)
    for r in range(SHARE):
        tops = [stats_ref[s, me ^ r, 0:1, :] for s in range(SHARE)]
        top = functools.reduce(jnp.maximum, tops)
        scaled = [jnp.exp2(t - top) for t in tops]
        total = sum(stats_ref[s, me ^ r, 1:2, :] * scaled[s] for s in range(SHARE))
        weighted = sum(stats_ref[s, me ^ r, 2:3, :] * scaled[s] for s in range(SHARE))
        log_total = top + jnp.log2(total)
        delta = weighted / total
        q_rows, g_rows = qg_refs[r][0], qg_refs[r][1]
        for i, u in enumerate(wanted):
            scores = masked_scores(limit_ref, q_rows, kv_refs[i][0], u, r, factor)
            probs = jnp.exp2(scores - log_total)
            dprobs = dot(kv_refs[i][1], g_rows, 1, 1)
            dscores = (probs * (dprobs - delta)).astype(BF16)
            ds_ref[i * unit : (i + 1) * unit, r * unit : (r + 1) * unit] = dscores
            dv_term = dot(probs.astype(BF16), g_rows, 1, 0)
            dk_term = dot(dscores, q_rows, 1, 0)
            dv[i] = dv_term if r == 0 else dv[i] + dv_term
            dk[i] = dk_term if r == 0 else dk[i] + dk_term
    for i, out_ref in enumerate(out_refs):
        dk_tall = (dk[i] * scale).T.astype(out_ref.dtype)
        dv_tall = dv[i].T.astype(out_ref.dtype)
        for part in range(GROUP):
            out_ref[part, 0] = dk_tall[part * sub : (part + 1) * sub]
            out_ref[part, 1] = dv_tall[part * sub : (part + 1) * sub]


def merge_kernel(*refs):
    terms, total_ref, (own_ref, *far_refs) = refs[: -GROUP - 1], refs[-1], refs[-GROUP - 1 : -1]
    total_ref[...] = sum(ref[...].astype(F32) for ref in terms)
    lane = lax.axis_index("fsdp") % GROUP
    own_ref[...] = total_ref[lane]
    for h in range(1, GROUP):
        far_refs[h - 1][...] = total_ref[lane ^ h].astype(BF16)


def query_kernel(units, scale, near_ref, far_ref, *refs):
    kv_refs, own_ref, far_refs = refs[:units], refs[units], refs[units + 1 :]
    unit = own_ref.shape[0]
    dq = dot(kv_refs[0][0], near_ref[...], 0, 0)
    for u in range(1, units):
        dq += dot(kv_refs[u][0], far_ref[(u - 1) * unit : u * unit], 0, 0)
    dq = (dq * scale).T
    own_ref[...] = dq[:unit]
    for r in range(1, SHARE):
        far_refs[r - 1][...] = dq[r * unit : (r + 1) * unit].astype(BF16)


def final_kernel(own_ref, *refs):
    far_refs = refs[: SHARE - 1]
    kv_refs, (dq_ref, dk_ref, dv_ref) = refs[SHARE - 1 : -3], refs[-3:]
    dq = own_ref[...]
    for ref in far_refs:
        dq += ref[...].astype(F32)
    dq_ref[...] = dq
    for which, out_ref in ((0, dk_ref), (1, dv_ref)):
        out_ref[...] = sum(ref[which].astype(F32) for ref in kv_refs)


def body(queries, keys, values, out_grad, block_ids, block_mask):
    unit, width = queries.shape
    ctx_size, lanes = lax.axis_size("ctx"), lax.axis_size("fsdp")
    units = ctx_size // SHARE
    rows = SHARE * unit
    sub = width // GROUP
    scale = width ** (-0.5)
    factor = scale * math.log2(math.e)
    if keys.shape[1] != width:
        key_group = lax.axis_index("fsdp") // GROUP
        keys = lax.dynamic_slice_in_dim(keys, key_group * width, width, 1)
        values = lax.dynamic_slice_in_dim(values, key_group * width, width, 1)

    def swap(x, step):
        return lax.ppermute(x, "ctx", [(i, i ^ step) for i in range(ctx_size)])

    def others(x):
        beyond = swap(x, 2)
        return [x, swap(x, 1), beyond, swap(beyond, 1)]

    qg, kv = jnp.stack([queries, out_grad]), jnp.stack([keys, values])
    qgs = others(qg)
    kvs = [kv] + [swap(kv, u * SHARE) for u in range(1, units)]
    (limits,) = call(
        functools.partial(limits_kernel, units, unit // 2),
        [jax.ShapeDtypeStruct((2 * units, rows), jnp.int32)],
        [block_ids, block_mask],
        in_specs=[pl.BlockSpec(memory_space=pltpu.SMEM)] * 2,
    )
    groups = [list(range(g * SHARE, (g + 1) * SHARE)) for g in range(units)]
    operands = qgs + kvs
    product = 2 * rows * units * unit * width
    (stats,) = call(
        functools.partial(stats_kernel, units, factor),
        [jax.ShapeDtypeStruct((SHARE, 3, unit), F32)],
        [limits] + operands,
        flops=2 * product,
    )
    all_stats = lax.all_gather(stats, "ctx", axis_index_groups=groups)
    spread = (GROUP, 2, sub, unit)
    far_scores, *far_parts = call(
        functools.partial(grads_kernel, list(range(1, units)), factor, scale),
        [jax.ShapeDtypeStruct(((units - 1) * unit, rows), BF16)]
        + [jax.ShapeDtypeStruct(spread, BF16)] * (units - 1),
        [limits, all_stats] + qgs + kvs[1:],
        flops=4 * product,
    )
    far_parts = [swap(x, (u + 1) * SHARE) for u, x in enumerate(far_parts)]
    near_scores, near_part = call(
        functools.partial(grads_kernel, [0], factor, scale),
        [jax.ShapeDtypeStruct((unit, rows), BF16), jax.ShapeDtypeStruct(spread, F32)],
        [limits, all_stats] + qgs + kvs[:1],
        flops=4 * product,
    )
    own, *far = call(
        functools.partial(query_kernel, units, scale),
        [jax.ShapeDtypeStruct((unit, width), F32)]
        + [jax.ShapeDtypeStruct((unit, width), BF16)] * (SHARE - 1),
        [near_scores, far_scores] + kvs,
        flops=product,
    )
    far = [swap(x, step + 1) for step, x in enumerate(far)]
    def cross(x, step):
        return lax.ppermute(x, "fsdp", [(i, i ^ step) for i in range(lanes)])

    own_part, *others_part = call(
        merge_kernel,
        [jax.ShapeDtypeStruct(spread[1:], F32)]
        + [jax.ShapeDtypeStruct(spread[1:], BF16)] * (GROUP - 1),
        [near_part] + far_parts,
        scratch=[pltpu.VMEM(spread, F32)],
    )
    parts = [own_part] + [cross(others_part[h - 1], h) for h in reversed(range(1, GROUP))]
    dq, dk, dv = call(
        final_kernel,
        [
            jax.ShapeDtypeStruct((unit, width), F32),
            jax.ShapeDtypeStruct((sub, unit), F32),
            jax.ShapeDtypeStruct((sub, unit), F32),
        ],
        [own] + far + parts,
    )
    return dq, dk.T, dv.T


def solution(mesh):
    in_specs = (P("ctx", "fsdp"), P("ctx", None), P("ctx", None), P("ctx", "fsdp"), P(), P())
    out_specs = (P("ctx", "fsdp"), P("ctx", "fsdp"), P("ctx", "fsdp"))
    return jax.shard_map(body, mesh=mesh, in_specs=in_specs, out_specs=out_specs, check_vma=False)
```

time: 37.5 us -> 33.1 us (0.88)
  blocking collectives: 12.7 us -> 5.25 us
  starting transfers between devices: 9.86 us -> 12.6 us
  Pallas kernels: 6.13 us -> 5.05 us
  other arithmetic: 0 us -> 0.94 us
  waiting for transfers between devices: 7.83 us -> 8.38 us
    all_gather x1 -> x0, blocking collectives: 7.5 us -> none  [body(): qgs = lax.all_gather(qg, 'ctx', axis_index_groups=groups)]
    all_to_all x1 -> x0, starting transfers between devices: 4.89 us -> none  [body(): lax.all_to_all(kv_parts, ('ctx', 'fsdp'), 0, 0, axis_index_groups=places,...]
    ppermute x0 -> x3, starting transfers between devices: none -> 4.45 us  [cross(): return lax.ppermute(x, 'fsdp', [(i, i ^ step) for i in range(lanes)])]
    all_to_all x1 -> x0, waiting for transfers between devices: 4.24 us -> none  [body(): lax.all_to_all(kv_parts, ('ctx', 'fsdp'), 0, 0, axis_index_groups=places,...]
    ppermute x0 -> x3, waiting for transfers between devices: none -> 4.02 us  [cross(): return lax.ppermute(x, 'fsdp', [(i, i ^ step) for i in range(lanes)])]
    ppermute x4 -> x8, starting transfers between devices: 4.97 us -> 8.12 us  [swap(): return lax.ppermute(x, 'ctx', [(i, i ^ step) for i in range(ctx_size)])]
    pallas_call x5 -> x7, Pallas kernels: 6.13 us -> 5.05 us  [call(): pl.pallas_call(kernel, out_shape=out_shape, in_specs=in_specs or [vmem()...]
    another operation x0 -> x2, other arithmetic: none -> 0.94 us  [body(): qg, kv = (jnp.stack([queries, out_grad]), jnp.stack([keys, values]))]
  transfers between devices with their start and end apart: 5 -> 11, of which waited for: 3 -> 5; matrix products, arithmetic and copies ran while one was open for 0% -> 0% of each run, Pallas kernels for 1% -> 7%
where the time goes in v3:
time: 33.1 us; the launch traced here: 32.9 us
  starting transfers between devices  12.6 us (38%)
  waiting for transfers between devices  8.38 us (25%)
  blocking collectives  5.25 us (16%)
  Pallas kernels  5.05 us (15%)
  other arithmetic  0.94 us (3%)
  between operations  0.73 us (2%)
    ppermute x8, starting transfers between devices, swap(): return lax.ppermute(x, 'ctx', [(i, i ^ step) for i in range(ctx_size)])  8.12 us
    all_gather x1, blocking collectives, body(): all_stats = lax.all_gather(stats, 'ctx', axis_index_groups=groups)  5.25 us
    pallas_call x7, Pallas kernels, call(): pl.pallas_call(kernel, out_shape=out_shape, in_specs=in_specs or [vmem()...  5.05 us
    ppermute x3, starting transfers between devices, cross(): return lax.ppermute(x, 'fsdp', [(i, i ^ step) for i in range(lanes)])  4.45 us
    ppermute x8, waiting for transfers between devices, swap(): return lax.ppermute(x, 'ctx', [(i, i ^ step) for i in range(ctx_size)])  4.36 us
    ppermute x3, waiting for transfers between devices, cross(): return lax.ppermute(x, 'fsdp', [(i, i ^ step) for i in range(lanes)])  4.02 us
    another operation x2, other arithmetic, body(): qg, kv = (jnp.stack([queries, out_grad]), jnp.stack([keys, values]))  0.94 us
  transfers between devices with their start and end apart: 11, of which 5 were waited for; matrix products, arithmetic and copies ran while one was open for 0% of the time, Pallas kernels for 7%

profile of v3, /device:TPU:0, one launch (start us, length us, event | category | flops | bytes accessed | tf_op | source)
XLA Modules:
  0.0 32.9 jit_solution(15909125694399373785)
XLA Ops:
  0.6 0.0 copy-start.2
  0.6 0.0 copy-start.3
  0.7 0.9 %pad_maximum_fusion.refs_0_ = bf16[2,256,128]{2,1,0:T(8,128)(2,1)S(1)} fusion(bf16[1,256,128]{2,1,0:T(8,128)(2,1)} %bitcast.9, bf16[1,256,128]{2,1,0:T(8,128)(2,1)} %bitcast.10), kind=kLoop, calls=%fused_computation | loop fusion | flops 65536 | bytes 262144 | tf_op jit(solution)/shard_map/stack | solution.py:180
  1.6 3.0 %collective-permute-start.1 = (bf16[2,256,128]{2,1,0:T(8,128)(2,1)S(1)}, bf16[2,256,128]{2,1,0:T(8,128)(2,1)S(1)}, u32[]{:S(2)}, u32[]{:S(2)}) collective-permute-start(bf16[2,256,128]{2,1,0:T(8,128)(2,1)S(1)} %pad_maximum_fusion.refs_0_), channel_id=1, source_target_pairs={{0,8},{4,12},{8,0},{12,4},{16,24},{20,28},{24,16},{28,20},{1,9},{5... | collective-permute-start | bytes 393224 | tf_op jit(solution)/shard_map/ppermute | solution.py:174
  4.6 0.0 collective-permute-start
  4.6 0.0 copy-done.2
  4.6 0.0 copy-done.3
  4.6 0.0 copy-start
  4.6 0.0 copy-start.1
  4.6 1.6 %collective-permute-start.3 = (bf16[2,256,128]{2,1,0:T(8,128)(2,1)S(1)}, bf16[2,256,128]{2,1,0:T(8,128)(2,1)S(1)}, u32[]{:S(2)}, u32[]{:S(2)}) collective-permute-start(bf16[2,256,128]{2,1,0:T(8,128)(2,1)S(1)} %pad_maximum_fusion.1.refs_4_.refs_0_), channel_id=1, source_target_pairs={{0,16},{4,20},{8,24},{12,28},{16,0},{20,4},{24,8},{28,12},{1,17},{... | collective-permute-start | bytes 393224 | tf_op jit(solution)/shard_map/ppermute | solution.py:174
  6.2 1.9 %collective-permute-done.1.refs_2_ = bf16[2,256,128]{2,1,0:T(8,128)(2,1)S(1)} collective-permute-done((bf16[2,256,128]{2,1,0:T(8,128)(2,1)S(1)}, bf16[2,256,128]{2,1,0:T(8,128)(2,1)S(1)}, u32[]{:S(2)}, u32[]{:S(2)}) %collective-permute-start.1) | collective-permute-done | bytes 131104 | tf_op jit(solution)/shard_map/ppermute | solution.py:174
  8.1 0.0 collective-permute-start.2
  8.1 0.0 copy-done
  8.1 0.0 copy-done.1
  8.1 0.8 %shard_map.85.limit_ref = s32[4,1024]{1,0:T(4,128)S(1)} custom-call(s32[16]{0:T(128)S(1)} %copy-done.1, s32[16,16]{1,0:T(8,128)S(1)} %copy-done), custom_call_target="tpu_custom_call" | custom-call | bytes 17472 | tf_op jit(solution)/shard_map/pallas_call | solution.py:33
  8.9 1.7 %collective-permute-done.3.refs_5_.refs_4_.refs_1_ = bf16[2,256,128]{2,1,0:T(8,128)(2,1)S(1)} collective-permute-done((bf16[2,256,128]{2,1,0:T(8,128)(2,1)S(1)}, bf16[2,256,128]{2,1,0:T(8,128)(2,1)S(1)}, u32[]{:S(2)}, u32[]{:S(2)}) %collective-permute-start.3) | collective-permute-done | bytes 131104 | tf_op jit(solution)/shard_map/ppermute | solution.py:174
  10.6 0.0 collective-permute-done.refs_1_
  10.6 0.0 collective-permute-done.2.refs_3_
  10.6 1.0 %shard_map.86 = f32[4,3,256]{2,1,0:T(4,128)S(1)} custom-call(s32[4,1024]{1,0:T(4,128)S(1)} %shard_map.85.limit_ref, bf16[2,256,128]{2,1,0:T(8,128)(2,1)S(1)} %pad_maximum_fusion.refs_0_, bf16[2,256,128]{2,1,0:T(8,128)(2,1)S(1)} %collective-permute-done.refs_1_, bf16[2,256,128]{2,1,0:T(8,128)(2,1)S(1)} %collective-permute-done.1.refs_2_, ...), custom_call_target="tpu_custom_call" | custom-call | flops 268435456 | bytes 815104 | tf_op jit(solution)/shard_map/pallas_call | solution.py:33
  11.6 5.2 %all-gather = f32[16,3,256]{2,1,0:T(4,128)S(1)} all-gather(f32[4,3,256]{2,1,0:T(4,128)S(1)} %shard_map.86), channel_id=2, replica_groups={{0,4,8,12},{16,20,24,28},{1,5,9,13},{17,21,25,29},{2,6,10,14},{18,22,26..., dimensions={0}, use_global_device_ids=true | all-gather | bytes 61440 | tf_op jit(solution)/shard_map/all_gather | solution.py:198
  16.8 1.1 %shard_map.88 = (bf16[256,1024]{1,0:T(8,128)(2,1)S(1)}, bf16[4,2,32,256]{3,2,1,0:T(8,128)(2,1)S(1)}) custom-call(s32[4,1024]{1,0:T(4,128)S(1)} %shard_map.85.limit_ref, f32[4,4,3,256]{3,2,1,0:T(4,128)S(1)} %bitcast.7, bf16[2,256,128]{2,1,0:T(8,128)(2,1)S(1)} %pad_maximum_fusion.refs_0_, bf16[2,256,128]{2,1,0:T(8,128)(2,1)S(1)} %collective-permute-done.refs_1_, ...), custom_call_target="tpu_custom_call" | custom-call | flops 536870912 | bytes 1376256 | tf_op jit(solution)/shard_map/pallas_call | solution.py:33
  17.9 1.6 %collective-permute-start.7 = (bf16[4,2,32,256]{3,2,1,0:T(8,128)(2,1)S(1)}, bf16[4,2,32,256]{3,2,1,0:T(8,128)(2,1)S(1)}, u32[]{:S(2)}, u32[]{:S(2)}) collective-permute-start(bf16[4,2,32,256]{3,2,1,0:T(8,128)(2,1)S(1)} %get-tuple-element.25), channel_id=1, source_target_pairs={{0,16},{4,20},{8,24},{12,28},{16,0},{20,4},{24,8},{28,12},{1,17},{... | collective-permute-start | bytes 393224 | tf_op jit(solution)/shard_map/ppermute | solution.py:174
  19.5 1.1 %shard_map.87 = (bf16[256,1024]{1,0:T(8,128)(2,1)S(1)}, f32[4,2,32,256]{3,2,1,0:T(8,128)S(1)}) custom-call(s32[4,1024]{1,0:T(4,128)S(1)} %shard_map.85.limit_ref, f32[4,4,3,256]{3,2,1,0:T(4,128)S(1)} %bitcast.8, bf16[2,256,128]{2,1,0:T(8,128)(2,1)S(1)} %pad_maximum_fusion.refs_0_, bf16[2,256,128]{2,1,0:T(8,128)(2,1)S(1)} %collective-permute-done.refs_1_, ...), custom_call_target="tpu_custom_call" | custom-call | flops 536870912 | bytes 1507328 | tf_op jit(solution)/shard_map/pallas_call | solution.py:33
  20.6 0.4 %shard_map.89 = (f32[256,128]{1,0:T(8,128)S(1)}, bf16[256,128]{1,0:T(8,128)(2,1)S(1)}, bf16[256,128]{1,0:T(8,128)(2,1)S(1)}, bf16[256,128]{1,0:T(8,128)(2,1)S(1)}) custom-call(bf16[256,1024]{1,0:T(8,128)(2,1)S(1)} %get-tuple-element.18.near_ref, bf16[256,1024]{1,0:T(8,128)(2,1)S(1)} %get-tuple-element.19.far_ref, ...), custom_call_target="tpu_custom_call" | custom-call | flops 134217728 | bytes 1638400 | tf_op jit(solution)/shard_map/pallas_call | solution.py:33
  21.0 0.1 collective-permute-start.4
  21.1 0.6 %collective-permute-start.5 = (bf16[256,128]{1,0:T(8,128)(2,1)S(1)}, bf16[256,128]{1,0:T(8,128)(2,1)S(1)}, u32[]{:S(2)}, u32[]{:S(2)}) collective-permute-start(bf16[256,128]{1,0:T(8,128)(2,1)S(1)} %get-tuple-element.22), channel_id=1, source_target_pairs={{0,8},{4,12},{8,0},{12,4},{16,24},{20,28},{24,16},{28,20},{1,9},{5... | collective-permute-start | bytes 196616 | tf_op jit(solution)/shard_map/ppermute | solution.py:174
  21.7 1.2 %collective-permute-start.6 = (bf16[256,128]{1,0:T(8,128)(2,1)S(1)}, bf16[256,128]{1,0:T(8,128)(2,1)S(1)}, u32[]{:S(2)}, u32[]{:S(2)}) collective-permute-start(bf16[256,128]{1,0:T(8,128)(2,1)S(1)} %get-tuple-element.23), channel_id=1, source_target_pairs={{0,12},{4,8},{8,4},{12,0},{16,28},{20,24},{24,20},{28,16},{1,13},{... | collective-permute-start | bytes 196616 | tf_op jit(solution)/shard_map/ppermute | solution.py:174
  23.0 0.8 %collective-permute-done.7.refs_1_ = bf16[4,2,32,256]{3,2,1,0:T(8,128)(2,1)S(1)} collective-permute-done((bf16[4,2,32,256]{3,2,1,0:T(8,128)(2,1)S(1)}, bf16[4,2,32,256]{3,2,1,0:T(8,128)(2,1)S(1)}, u32[]{:S(2)}, u32[]{:S(2)}) %collective-permute-start.7) | collective-permute-done | bytes 131104 | tf_op jit(solution)/shard_map/ppermute | solution.py:174
  23.8 3.7 %collective-permute-start.8 = (bf16[2,32,256]{2,1,0:T(8,128)(2,1)S(1)}, bf16[2,32,256]{2,1,0:T(8,128)(2,1)S(1)}, u32[]{:S(2)}, u32[]{:S(2)}) collective-permute-start(bf16[2,32,256]{2,1,0:T(8,128)(2,1)S(1)} %get-tuple-element.27), channel_id=1, source_target_pairs={{0,3},{1,2},{2,1},{3,0},{4,7},{5,6},{6,5},{7,4},{8,11},{9,10},{10,... | collective-permute-start | bytes 98312 | tf_op jit(solution)/shard_map/ppermute | solution.py:223
  27.4 0.0 collective-permute-start.9
  27.4 0.0 collective-permute-done.4.refs_0_
  27.4 0.8 %collective-permute-start.10 = (bf16[2,32,256]{2,1,0:T(8,128)(2,1)S(1)}, bf16[2,32,256]{2,1,0:T(8,128)(2,1)S(1)}, u32[]{:S(2)}, u32[]{:S(2)}) collective-permute-start(bf16[2,32,256]{2,1,0:T(8,128)(2,1)S(1)} %get-tuple-element.29), channel_id=1, source_target_pairs={{0,1},{1,0},{2,3},{3,2},{4,5},{5,4},{6,7},{7,6},{8,9},{9,8},{10,11... | collective-permute-start | bytes 98312 | tf_op jit(solution)/shard_map/ppermute | solution.py:223
  28.2 0.0 collective-permute-done.5.refs_1_
  28.2 0.0 collective-permute-done.6.refs_2_
  28.2 1.6 %collective-permute-done.8.refs_4_ = bf16[2,32,256]{2,1,0:T(8,128)(2,1)S(1)} collective-permute-done((bf16[2,32,256]{2,1,0:T(8,128)(2,1)S(1)}, bf16[2,32,256]{2,1,0:T(8,128)(2,1)S(1)}, u32[]{:S(2)}, u32[]{:S(2)}) %collective-permute-start.8) | collective-permute-done | bytes 32800 | tf_op jit(solution)/shard_map/ppermute | solution.py:223
  29.8 2.4 %collective-permute-done.9.refs_5_ = bf16[2,32,256]{2,1,0:T(8,128)(2,1)S(1)} collective-permute-done((bf16[2,32,256]{2,1,0:T(8,128)(2,1)S(1)}, bf16[2,32,256]{2,1,0:T(8,128)(2,1)S(1)}, u32[]{:S(2)}, u32[]{:S(2)}) %collective-permute-start.9) | collective-permute-done | bytes 32800 | tf_op jit(solution)/shard_map/ppermute | solution.py:223
  32.2 0.0 collective-permute-done.10.refs_6_
  32.2 0.7 %shard_map.91 = (f32[256,128]{1,0:T(8,128)}, f32[32,256]{1,0:T(8,128)}, f32[32,256]{1,0:T(8,128)}) custom-call(f32[256,128]{1,0:T(8,128)S(1)} %get-tuple-element.20.own_ref, bf16[256,128]{1,0:T(8,128)(2,1)S(1)} %collective-permute-done.4.refs_0_, bf16[256,128]{1,0:T(8,128)(2,1)S(1)} %collective-permute-done.5.refs_1_, ...), custom_call_target="tpu_custom_call" | custom-call | bytes 688128 | tf_op jit(solution)/shard_map/pallas_call | solution.py:33
  (2 shorter events, 0.1 us)
Async XLA Ops:
  0.6 4.0 %copy-start.2 = (bf16[256,128]{1,0:T(8,128)(2,1)S(1)}, bf16[256,128]{1,0:T(8,128)(2,1)}, u32[]{:S(2)}) copy-start(bf16[256,128]{1,0:T(8,128)(2,1)} %param.8) | copy-start | bytes 196612
  0.6 3.9 %copy-start.3 = (bf16[256,128]{1,0:T(8,128)(2,1)S(1)}, bf16[256,128]{1,0:T(8,128)(2,1)}, u32[]{:S(2)}) copy-start(bf16[256,128]{1,0:T(8,128)(2,1)} %param.7) | copy-start | bytes 196612
  1.6 6.5 %collective-permute-start.1 = (bf16[2,256,128]{2,1,0:T(8,128)(2,1)S(1)}, bf16[2,256,128]{2,1,0:T(8,128)(2,1)S(1)}, u32[]{:S(2)}, u32[]{:S(2)}) collective-permute-start(bf16[2,256,128]{2,1,0:T(8,128)(2,1)S(1)} %pad_maximum_fusion.refs_0_), channel_id=1, source_target_pairs={{0,8},{4,12},{8,0},{12,4},{16,24},{20,28},{24,16},{28,20},{1,9},{5... | collective-permute-start | bytes 393224 | tf_op jit(solution)/shard_map/ppermute | solution.py:174
  4.6 6.0 %collective-permute-start = (bf16[2,256,128]{2,1,0:T(8,128)(2,1)S(1)}, bf16[2,256,128]{2,1,0:T(8,128)(2,1)S(1)}, u32[]{:S(2)}, u32[]{:S(2)}) collective-permute-start(bf16[2,256,128]{2,1,0:T(8,128)(2,1)S(1)} %pad_maximum_fusion.refs_0_), channel_id=1, source_target_pairs={{0,4},{4,0},{8,12},{12,8},{16,20},{20,16},{24,28},{28,24},{1,5},{5... | collective-permute-start | bytes 393224 | tf_op jit(solution)/shard_map/ppermute | solution.py:174
  4.6 3.5 %copy-start = (s32[16,16]{1,0:T(8,128)S(1)}, s32[16,16]{1,0:T(8,128)}, u32[]{:S(2)}) copy-start(s32[16,16]{1,0:T(8,128)} %mask_ref.1) | copy-start | bytes 3076
  4.6 3.5 %copy-start.1 = (s32[16]{0:T(128)S(1)}, s32[16]{0:T(128)}, u32[]{:S(2)}) copy-start(s32[16]{0:T(128)} %ids_ref.1) | copy-start | bytes 196
  4.6 6.0 %collective-permute-start.3 = (bf16[2,256,128]{2,1,0:T(8,128)(2,1)S(1)}, bf16[2,256,128]{2,1,0:T(8,128)(2,1)S(1)}, u32[]{:S(2)}, u32[]{:S(2)}) collective-permute-start(bf16[2,256,128]{2,1,0:T(8,128)(2,1)S(1)} %pad_maximum_fusion.1.refs_4_.refs_0_), channel_id=1, source_target_pairs={{0,16},{4,20},{8,24},{12,28},{16,0},{20,4},{24,8},{28,12},{1,17},{... | collective-permute-start | bytes 393224 | tf_op jit(solution)/shard_map/ppermute | solution.py:174
  8.1 2.5 %collective-permute-start.2 = (bf16[2,256,128]{2,1,0:T(8,128)(2,1)S(1)}, bf16[2,256,128]{2,1,0:T(8,128)(2,1)S(1)}, u32[]{:S(2)}, u32[]{:S(2)}) collective-permute-start(bf16[2,256,128]{2,1,0:T(8,128)(2,1)S(1)} %collective-permute-done.1.refs_2_), channel_id=1, source_target_pairs={{0,4},{4,0},{8,12},{12,8},{16,20},{20,16},{24,28},{28,24},{1,5},{5... | collective-permute-start | bytes 393224 | tf_op jit(solution)/shard_map/ppermute | solution.py:174
  17.9 5.8 %collective-permute-start.7 = (bf16[4,2,32,256]{3,2,1,0:T(8,128)(2,1)S(1)}, bf16[4,2,32,256]{3,2,1,0:T(8,128)(2,1)S(1)}, u32[]{:S(2)}, u32[]{:S(2)}) collective-permute-start(bf16[4,2,32,256]{3,2,1,0:T(8,128)(2,1)S(1)} %get-tuple-element.25), channel_id=1, source_target_pairs={{0,16},{4,20},{8,24},{12,28},{16,0},{20,4},{24,8},{28,12},{1,17},{... | collective-permute-start | bytes 393224 | tf_op jit(solution)/shard_map/ppermute | solution.py:174
  21.0 6.4 %collective-permute-start.4 = (bf16[256,128]{1,0:T(8,128)(2,1)S(1)}, bf16[256,128]{1,0:T(8,128)(2,1)S(1)}, u32[]{:S(2)}, u32[]{:S(2)}) collective-permute-start(bf16[256,128]{1,0:T(8,128)(2,1)S(1)} %get-tuple-element.21), channel_id=1, source_target_pairs={{0,4},{4,0},{8,12},{12,8},{16,20},{20,16},{24,28},{28,24},{1,5},{5... | collective-permute-start | bytes 196616 | tf_op jit(solution)/shard_map/ppermute | solution.py:174
  21.1 7.1 %collective-permute-start.5 = (bf16[256,128]{1,0:T(8,128)(2,1)S(1)}, bf16[256,128]{1,0:T(8,128)(2,1)S(1)}, u32[]{:S(2)}, u32[]{:S(2)}) collective-permute-start(bf16[256,128]{1,0:T(8,128)(2,1)S(1)} %get-tuple-element.22), channel_id=1, source_target_pairs={{0,8},{4,12},{8,0},{12,4},{16,24},{20,28},{24,16},{28,20},{1,9},{5... | collective-permute-start | bytes 196616 | tf_op jit(solution)/shard_map/ppermute | solution.py:174
  21.7 6.5 %collective-permute-start.6 = (bf16[256,128]{1,0:T(8,128)(2,1)S(1)}, bf16[256,128]{1,0:T(8,128)(2,1)S(1)}, u32[]{:S(2)}, u32[]{:S(2)}) collective-permute-start(bf16[256,128]{1,0:T(8,128)(2,1)S(1)} %get-tuple-element.23), channel_id=1, source_target_pairs={{0,12},{4,8},{8,4},{12,0},{16,28},{20,24},{24,20},{28,16},{1,13},{... | collective-permute-start | bytes 196616 | tf_op jit(solution)/shard_map/ppermute | solution.py:174
  23.8 6.1 %collective-permute-start.8 = (bf16[2,32,256]{2,1,0:T(8,128)(2,1)S(1)}, bf16[2,32,256]{2,1,0:T(8,128)(2,1)S(1)}, u32[]{:S(2)}, u32[]{:S(2)}) collective-permute-start(bf16[2,32,256]{2,1,0:T(8,128)(2,1)S(1)} %get-tuple-element.27), channel_id=1, source_target_pairs={{0,3},{1,2},{2,1},{3,0},{4,7},{5,6},{6,5},{7,4},{8,11},{9,10},{10,... | collective-permute-start | bytes 98312 | tf_op jit(solution)/shard_map/ppermute | solution.py:223
  27.4 4.8 %collective-permute-start.9 = (bf16[2,32,256]{2,1,0:T(8,128)(2,1)S(1)}, bf16[2,32,256]{2,1,0:T(8,128)(2,1)S(1)}, u32[]{:S(2)}, u32[]{:S(2)}) collective-permute-start(bf16[2,32,256]{2,1,0:T(8,128)(2,1)S(1)} %get-tuple-element.28), channel_id=1, source_target_pairs={{0,2},{1,3},{2,0},{3,1},{4,6},{5,7},{6,4},{7,5},{8,10},{9,11},{10,... | collective-permute-start | bytes 98312 | tf_op jit(solution)/shard_map/ppermute | solution.py:223
  27.4 4.8 %collective-permute-start.10 = (bf16[2,32,256]{2,1,0:T(8,128)(2,1)S(1)}, bf16[2,32,256]{2,1,0:T(8,128)(2,1)S(1)}, u32[]{:S(2)}, u32[]{:S(2)}) collective-permute-start(bf16[2,32,256]{2,1,0:T(8,128)(2,1)S(1)} %get-tuple-element.29), channel_id=1, source_target_pairs={{0,1},{1,0},{2,3},{3,2},{4,5},{5,4},{6,7},{7,6},{8,9},{9,8},{10,11... | collective-permute-start | bytes 98312 | tf_op jit(solution)/shard_map/ppermute | solution.py:223

commit v4 on v3

v4 whole, which is shorter than its diff:
```python
import functools
import math

import jax
import jax.numpy as jnp
from jax import lax
from jax.experimental import pallas as pl
from jax.experimental.pallas import tpu as pltpu
from jax.sharding import PartitionSpec as P

GROUP = 4
SHARE = 4
MASKED = -1e30
FLOOR = -1e20
VMEM_LIMIT = 48 * 1024 * 1024

F32 = jnp.float32
BF16 = jnp.bfloat16


def dot(left, right, left_dim, right_dim):
    return lax.dot_general(
        left, right, (((left_dim,), (right_dim,)), ((), ())), preferred_element_type=F32
    )


def vmem():
    return pl.BlockSpec(memory_space=pltpu.VMEM)


def call(kernel, out_shape, ins, in_specs=None, flops=0, scratch=()):
    size = sum(math.prod(x.shape) * x.dtype.itemsize for x in list(ins) + list(out_shape))
    return pl.pallas_call(
        kernel,
        out_shape=out_shape,
        in_specs=in_specs or [vmem() for _ in ins],
        out_specs=[vmem() for _ in out_shape],
        scratch_shapes=list(scratch),
        compiler_params=pltpu.CompilerParams(vmem_limit_bytes=VMEM_LIMIT),
        cost_estimate=pl.CostEstimate(flops=flops, bytes_accessed=size, transcendentals=0),
    )(*ins)


def limits_kernel(units, half, ids_ref, mask_ref, *limit_refs):
    ctx_index = lax.axis_index("ctx")
    lane = lax.broadcasted_iota(jnp.int32, (1, half), 1)
    for r, limit_ref in enumerate(limit_refs):
        for side in range(2):
            query_block = ids_ref[(ctx_index ^ r) * 2 + side]
            for row in range(2 * units):
                key_block = ids_ref[(ctx_index ^ (row // 2 * SHARE)) * 2 + row % 2]
                linked = mask_ref[query_block, key_block] > 0
                start = jnp.where(linked, (query_block - key_block) * half, -2 * half)
                limit_ref[row : row + 1, side * half : (side + 1) * half] = lane + start


def after_kernel(in_ref, after_ref, out_ref):
    del after_ref
    out_ref[...] = in_ref[...]


def unit_kernel(units, factor, limit_ref, qg_ref, *refs):
    kv_refs, (exp_ref, dprob_ref, stats_ref) = refs[:units], refs[units:]
    unit = qg_ref.shape[1]
    half = unit // 2
    q_rows, g_rows = qg_ref[0], qg_ref[1]
    row = lax.broadcasted_iota(jnp.int32, (half, 1), 0)
    scores = []
    for u in range(units):
        products = dot(kv_refs[u][0], q_rows, 1, 1) * factor
        for part in range(2):
            allowed = limit_ref[u * 2 + part : u * 2 + part + 1, :] >= row
            scores.append(jnp.where(allowed, products[part * half : (part + 1) * half], MASKED))
    top = functools.reduce(jnp.maximum, [jnp.max(s, axis=0, keepdims=True) for s in scores])
    top = jnp.maximum(top, FLOOR)
    total = jnp.zeros_like(top)
    weighted = jnp.zeros_like(top)
    for u in range(units):
        dprobs = dot(kv_refs[u][1], g_rows, 1, 1)
        for part in range(2):
            start = u * unit + part * half
            weights = jnp.exp2(scores[u * 2 + part] - top)
            here = dprobs[part * half : (part + 1) * half]
            exp_ref[start : start + half] = weights
            dprob_ref[start : start + half] = here
            total += jnp.sum(weights, axis=0, keepdims=True)
            weighted += jnp.sum(weights * here, axis=0, keepdims=True)
    stats_ref[0:1, :] = top
    stats_ref[1:2, :] = total
    stats_ref[2:3, :] = weighted


def collect_kernel(*refs):
    for r in range(SHARE):
        refs[-1][r] = refs[r][...]


def merge_stats(left, right):
    top = jnp.maximum(left[0:1], right[0:1])
    first, second = jnp.exp2(left[0:1] - top), jnp.exp2(right[0:1] - top)
    return (
        top,
        left[1:2] * first + right[1:2] * second,
        left[2:3] * first + right[2:3] * second,
    )


def pair_kernel(own_ref, other_ref, out_ref):
    for r in range(SHARE):
        for row, value in enumerate(merge_stats(own_ref[r], other_ref[r ^ 1])):
            out_ref[r, row : row + 1, :] = value


def grads_kernel(u, scale, *refs):
    (own_ref, near_ref, far_ref), refs = refs[:3], refs[3:]
    qg_refs, refs = refs[:SHARE], refs[SHARE:]
    exp_refs, dprob_refs = refs[:SHARE], refs[SHARE : 2 * SHARE]
    ds_ref, out_ref = refs[2 * SHARE :]
    _, unit, width = qg_refs[0].shape
    sub = width // GROUP
    dk, dv = 0.0, 0.0
    for r in range(SHARE):
        top, total, weighted = merge_stats(near_ref[r], far_ref[r ^ 2])
        share = jnp.exp2(own_ref[r, 0:1] - top) / total
        delta = weighted / total
        probs = exp_refs[r][u * unit : (u + 1) * unit] * share
        dprobs = dprob_refs[r][u * unit : (u + 1) * unit]
        dscores = (probs * (dprobs - delta)).astype(BF16)
        ds_ref[:, r * unit : (r + 1) * unit] = dscores
        dv += dot(probs.astype(BF16), qg_refs[r][1], 1, 0)
        dk += dot(dscores, qg_refs[r][0], 1, 0)
    dk_tall = (dk * scale).T.astype(out_ref.dtype)
    dv_tall = dv.T.astype(out_ref.dtype)
    for part in range(GROUP):
        out_ref[part, 0] = dk_tall[part * sub : (part + 1) * sub]
        out_ref[part, 1] = dv_tall[part * sub : (part + 1) * sub]


def merge_kernel(*refs):
    terms, total_ref, (own_ref, *far_refs) = refs[: -GROUP - 1], refs[-1], refs[-GROUP - 1 : -1]
    total_ref[...] = sum(ref[...].astype(F32) for ref in terms)
    lane = lax.axis_index("fsdp") % GROUP
    own_ref[...] = total_ref[lane]
    for h in range(1, GROUP):
        far_refs[h - 1][...] = total_ref[(lane + h) % GROUP].astype(BF16)


def query_kernel(units, scale, *refs):
    ds_refs, kv_refs = refs[:units], refs[units : 2 * units]
    own_ref, far_refs = refs[2 * units], refs[2 * units + 1 :]
    unit = own_ref.shape[0]
    dq = sum(dot(kv_refs[u][0], ds_refs[u][...], 0, 0) for u in range(units))
    dq = (dq * scale).T
    own_ref[...] = dq[:unit]
    for r in range(1, SHARE):
        far_refs[r - 1][...] = dq[r * unit : (r + 1) * unit].astype(BF16)


def sum_kernel(*refs):
    refs[-1][...] = sum(ref[...].astype(F32) for ref in refs[:-1])


def final_kernel(*refs):
    parts, (dk_ref, dv_ref) = refs[:-2], refs[-2:]
    dk_ref[...] = sum(ref[0].astype(F32) for ref in parts)
    dv_ref[...] = sum(ref[1].astype(F32) for ref in parts)


def body(queries, keys, values, out_grad, block_ids, block_mask):
    unit, width = queries.shape
    ctx_size, lanes = lax.axis_size("ctx"), lax.axis_size("fsdp")
    units = ctx_size // SHARE
    rows = SHARE * unit
    sub = width // GROUP
    scale = width ** (-0.5)
    factor = scale * math.log2(math.e)
    if keys.shape[1] != width:
        key_group = lax.axis_index("fsdp") // GROUP
        keys = lax.dynamic_slice_in_dim(keys, key_group * width, width, 1)
        values = lax.dynamic_slice_in_dim(values, key_group * width, width, 1)

    def swap(x, step):
        return lax.ppermute(x, "ctx", [(i, i ^ step) for i in range(ctx_size)])

    qg, kv = jnp.stack([queries, out_grad]), jnp.stack([keys, values])
    far_qg = swap(qg, 2)
    kvs = [kv] + [swap(kv, u * SHARE) for u in range(1, units)]
    limits = call(
        functools.partial(limits_kernel, units, unit // 2),
        [jax.ShapeDtypeStruct((2 * units, unit), jnp.int32)] * SHARE,
        [block_ids, block_mask],
        in_specs=[pl.BlockSpec(memory_space=pltpu.SMEM)] * 2,
    )
    (sent_qg,) = call(after_kernel, [jax.ShapeDtypeStruct(far_qg.shape, BF16)], [far_qg, limits[0]])
    qgs = [qg, swap(qg, 1), far_qg, swap(sent_qg, 1)]

    product = 2 * unit * unit * width
    grid = jax.ShapeDtypeStruct((units * unit, unit), F32)
    results = [
        call(
            functools.partial(unit_kernel, units, factor),
            [grid, grid, jax.ShapeDtypeStruct((3, unit), F32)],
            [limits[r], qgs[r]] + kvs,
            flops=2 * units * product,
        )
        for r in range(SHARE)
    ]
    exps, dprobs, stats = zip(*results)
    (stats,) = call(
        collect_kernel, [jax.ShapeDtypeStruct((SHARE, 3, unit), F32)], list(stats)
    )
    (chip_stats,) = call(
        pair_kernel, [jax.ShapeDtypeStruct(stats.shape, F32)], [stats, swap(stats, 1)]
    )
    operands = [stats, chip_stats, swap(chip_stats, 2)] + qgs + list(exps) + list(dprobs)

    parts = (GROUP, 2, sub, unit)
    scores, shares = [], []
    for u in reversed(range(units)):
        dscores, share = call(
            functools.partial(grads_kernel, u, scale),
            [
                jax.ShapeDtypeStruct((unit, rows), BF16),
                jax.ShapeDtypeStruct(parts, BF16 if u else F32),
            ],
            operands,
            flops=2 * SHARE * product,
        )
        scores.insert(0, dscores)
        shares.insert(0, swap(share, u * SHARE) if u else share)
    own, *far = call(
        functools.partial(query_kernel, units, scale),
        [jax.ShapeDtypeStruct((unit, width), F32)]
        + [jax.ShapeDtypeStruct((unit, width), BF16)] * (SHARE - 1),
        scores + kvs,
        flops=SHARE * units * product,
    )
    far = [swap(x, step + 1) for step, x in enumerate(far)]

    def cross(x, step):
        pairs = [(i, i // GROUP * GROUP + (i + step) % GROUP) for i in range(lanes)]
        return lax.ppermute(x, "fsdp", pairs)

    own_part, *others_part = call(
        merge_kernel,
        [jax.ShapeDtypeStruct(parts[1:], F32)]
        + [jax.ShapeDtypeStruct(parts[1:], BF16)] * (GROUP - 1),
        shares,
        scratch=[pltpu.VMEM(parts, F32)],
    )
    columns = [own_part] + [cross(others_part[h - 1], h) for h in range(1, GROUP)]
    (dq,) = call(sum_kernel, [jax.ShapeDtypeStruct((unit, width), F32)], [own] + far)
    dk, dv = call(final_kernel, [jax.ShapeDtypeStruct((sub, unit), F32)] * 2, columns)
    return dq, dk.T, dv.T


def solution(mesh):
    in_specs = (P("ctx", "fsdp"), P("ctx", None), P("ctx", None), P("ctx", "fsdp"), P(), P())
    out_specs = (P("ctx", "fsdp"), P("ctx", "fsdp"), P("ctx", "fsdp"))
    return jax.shard_map(body, mesh=mesh, in_specs=in_specs, out_specs=out_specs, check_vma=False)
```

time: 33.1 us -> 30.9 us (0.934)
  blocking collectives: 5.25 us -> 0 us
  starting transfers between devices: 12.6 us -> 14.3 us
  waiting for transfers between devices: 8.38 us -> 9.39 us
    all_gather x1 -> x0, blocking collectives: 5.25 us -> none  [body(): all_stats = lax.all_gather(stats, 'ctx', axis_index_groups=groups)]
    ppermute x8 -> x10, waiting for transfers between devices: 4.36 us -> 7.52 us  [swap(): return lax.ppermute(x, 'ctx', [(i, i ^ step) for i in range(ctx_size)])]
    ppermute x3, waiting for transfers between devices: 4.02 us -> 1.88 us  [cross(): return lax.ppermute(x, 'fsdp', pairs)]
    ppermute x3, starting transfers between devices: 4.45 us -> 5.58 us  [cross(): return lax.ppermute(x, 'fsdp', pairs)]
    ppermute x8 -> x10, starting transfers between devices: 8.12 us -> 8.75 us  [swap(): return lax.ppermute(x, 'ctx', [(i, i ^ step) for i in range(ctx_size)])]
    pallas_call x7 -> x14, Pallas kernels: 5.05 us -> 5.27 us  [call(): pl.pallas_call(kernel, out_shape=out_shape, in_specs=in_specs or [vmem()...]
  transfers between devices with their start and end apart: 11 -> 13, of which waited for: 5 -> 7; matrix products, arithmetic and copies ran while one was open for 0% -> 0% of each run, Pallas kernels for 7% -> 12%
where the time goes in v4:
time: 30.9 us; the launch traced here: 30.7 us
  starting transfers between devices  14.3 us (46%)
  waiting for transfers between devices  9.39 us (30%)
  Pallas kernels  5.27 us (17%)
  other arithmetic  0.94 us (3%)
  between operations  0.79 us (3%)
    ppermute x10, starting transfers between devices, swap(): return lax.ppermute(x, 'ctx', [(i, i ^ step) for i in range(ctx_size)])  8.75 us
    ppermute x10, waiting for transfers between devices, swap(): return lax.ppermute(x, 'ctx', [(i, i ^ step) for i in range(ctx_size)])  7.52 us
    ppermute x3, starting transfers between devices, cross(): return lax.ppermute(x, 'fsdp', pairs)  5.58 us
    pallas_call x14, Pallas kernels, call(): pl.pallas_call(kernel, out_shape=out_shape, in_specs=in_specs or [vmem()...  5.27 us
    ppermute x3, waiting for transfers between devices, cross(): return lax.ppermute(x, 'fsdp', pairs)  1.88 us
    another operation x2, other arithmetic, body(): qg, kv = (jnp.stack([queries, out_grad]), jnp.stack([keys, values]))  0.94 us
  transfers between devices with their start and end apart: 13, of which 7 were waited for; matrix products, arithmetic and copies ran while one was open for 0% of the time, Pallas kernels for 12%

profile of v4, /device:TPU:0, one launch (start us, length us, event | category | flops | bytes accessed | tf_op | source)
XLA Modules:
  0.0 30.7 jit_solution(3696984852263418131)
XLA Ops:
  0.6 0.0 copy-start.2
  0.6 0.0 copy-start.3
  0.7 0.9 %pad_maximum_fusion.qg_ref.refs_3_ = bf16[2,256,128]{2,1,0:T(8,128)(2,1)S(1)} fusion(bf16[1,256,128]{2,1,0:T(8,128)(2,1)} %bitcast.6, bf16[1,256,128]{2,1,0:T(8,128)(2,1)} %bitcast.7), kind=kLoop, calls=%fused_computation | loop fusion | flops 65536 | bytes 262144 | tf_op jit(solution)/shard_map/stack | solution.py:185
  1.6 3.0 %collective-permute-start.2 = (bf16[2,256,128]{2,1,0:T(8,128)(2,1)S(1)}, bf16[2,256,128]{2,1,0:T(8,128)(2,1)S(1)}, u32[]{:S(2)}, u32[]{:S(2)}) collective-permute-start(bf16[2,256,128]{2,1,0:T(8,128)(2,1)S(1)} %pad_maximum_fusion.qg_ref.refs_3_), channel_id=1, source_target_pairs={{0,8},{4,12},{8,0},{12,4},{16,24},{20,28},{24,16},{28,20},{1,9},{5... | collective-permute-start | bytes 393224 | tf_op jit(solution)/shard_map/ppermute | solution.py:183
  4.6 0.0 copy-done.2
  4.6 0.0 copy-done.3
  4.6 0.0 copy-start
  4.6 0.0 copy-start.1
  4.6 1.6 %collective-permute-start = (bf16[2,256,128]{2,1,0:T(8,128)(2,1)S(1)}, bf16[2,256,128]{2,1,0:T(8,128)(2,1)S(1)}, u32[]{:S(2)}, u32[]{:S(2)}) collective-permute-start(bf16[2,256,128]{2,1,0:T(8,128)(2,1)S(1)} %pad_maximum_fusion.1.refs_0_.refs_2_), channel_id=1, source_target_pairs={{0,16},{4,20},{8,24},{12,28},{16,0},{20,4},{24,8},{28,12},{1,17},{... | collective-permute-start | bytes 393224 | tf_op jit(solution)/shard_map/ppermute | solution.py:183
  6.2 0.0 collective-permute-start.1
  6.2 0.0 copy-done
  6.2 0.0 copy-done.1
  6.2 0.8 %shard_map.85 = (s32[4,256]{1,0:T(4,128)S(1)}, s32[4,256]{1,0:T(4,128)S(1)}, s32[4,256]{1,0:T(4,128)S(1)}, s32[4,256]{1,0:T(4,128)S(1)}) custom-call(s32[16]{0:T(128)S(1)} %copy-done.1, s32[16,16]{1,0:T(8,128)S(1)} %copy-done), custom_call_target="tpu_custom_call" | custom-call | bytes 17472 | tf_op jit(solution)/shard_map/pallas_call | solution.py:33
  7.0 1.1 %collective-permute-done.2.qg_ref.in_ref.refs_5_ = bf16[2,256,128]{2,1,0:T(8,128)(2,1)S(1)} collective-permute-done((bf16[2,256,128]{2,1,0:T(8,128)(2,1)S(1)}, bf16[2,256,128]{2,1,0:T(8,128)(2,1)S(1)}, u32[]{:S(2)}, u32[]{:S(2)}) %collective-permute-start.2) | collective-permute-done | bytes 131104 | tf_op jit(solution)/shard_map/ppermute | solution.py:183
  8.1 0.1 collective-permute-start.3
  8.2 1.5 %collective-permute-done.refs_1_.refs_3_ = bf16[2,256,128]{2,1,0:T(8,128)(2,1)S(1)} collective-permute-done((bf16[2,256,128]{2,1,0:T(8,128)(2,1)S(1)}, bf16[2,256,128]{2,1,0:T(8,128)(2,1)S(1)}, u32[]{:S(2)}, u32[]{:S(2)}) %collective-permute-start) | collective-permute-done | bytes 131104 | tf_op jit(solution)/shard_map/ppermute | solution.py:183
  9.6 0.4 %shard_map.86 = (f32[512,256]{1,0:T(8,128)S(1)}, f32[512,256]{1,0:T(8,128)S(1)}, f32[3,256]{1,0:T(4,128)S(1)}) custom-call(s32[4,256]{1,0:T(4,128)S(1)} %get-tuple-element.33.limit_ref.after_ref, bf16[2,256,128]{2,1,0:T(8,128)(2,1)S(1)} %pad_maximum_fusion.qg_ref.refs_3_, bf16[2,256,128]{2,1,0:T(8,128)(2,1)S(1)} %pad_maximum_fusion.1.refs_0_.refs_2_, ...), custom_call_target="tpu_custom_call" | custom-call | flops 67108864 | bytes 1448960 | tf_op jit(solution)/shard_map/pallas_call | solution.py:33
  10.0 0.4 %shard_map.88 = (f32[512,256]{1,0:T(8,128)S(1)}, f32[512,256]{1,0:T(8,128)S(1)}, f32[3,256]{1,0:T(4,128)S(1)}) custom-call(s32[4,256]{1,0:T(4,128)S(1)} %get-tuple-element.37.limit_ref, bf16[2,256,128]{2,1,0:T(8,128)(2,1)S(1)} %collective-permute-done.2.qg_ref.in_ref.refs_5_, bf16[2,256,128]{2,1,0:T(8,128)(2,1)S(1)} %pad_maximum_fusion.1.refs_0_.refs_2_, ...), custom_call_target="tpu_custom_call" | custom-call | flops 67108864 | bytes 1448960 | tf_op jit(solution)/shard_map/pallas_call | solution.py:33
  10.4 0.0 collective-permute-done.1.qg_ref.refs_4_
  10.4 0.4 %shard_map.87 = (f32[512,256]{1,0:T(8,128)S(1)}, f32[512,256]{1,0:T(8,128)S(1)}, f32[3,256]{1,0:T(4,128)S(1)}) custom-call(s32[4,256]{1,0:T(4,128)S(1)} %get-tuple-element.35.limit_ref, bf16[2,256,128]{2,1,0:T(8,128)(2,1)S(1)} %collective-permute-done.1.qg_ref.refs_4_, bf16[2,256,128]{2,1,0:T(8,128)(2,1)S(1)} %pad_maximum_fusion.1.refs_0_.refs_2_, ...), custom_call_target="tpu_custom_call" | custom-call | flops 67108864 | bytes 1448960 | tf_op jit(solution)/shard_map/pallas_call | solution.py:33
  10.8 0.0 collective-permute-done.3.qg_ref.refs_6_
  10.8 0.4 %shard_map.90 = (f32[512,256]{1,0:T(8,128)S(1)}, f32[512,256]{1,0:T(8,128)S(1)}, f32[3,256]{1,0:T(4,128)S(1)}) custom-call(s32[4,256]{1,0:T(4,128)S(1)} %get-tuple-element.39.limit_ref, bf16[2,256,128]{2,1,0:T(8,128)(2,1)S(1)} %collective-permute-done.3.qg_ref.refs_6_, bf16[2,256,128]{2,1,0:T(8,128)(2,1)S(1)} %pad_maximum_fusion.1.refs_0_.refs_2_, ...), custom_call_target="tpu_custom_call" | custom-call | flops 67108864 | bytes 1448960 | tf_op jit(solution)/shard_map/pallas_call | solution.py:33
  11.2 0.1 collective-permute-start.4
  11.3 1.2 %collective-permute-done.4.other_ref = f32[4,3,256]{2,1,0:T(4,128)S(1)} collective-permute-done((f32[4,3,256]{2,1,0:T(4,128)S(1)}, f32[4,3,256]{2,1,0:T(4,128)S(1)}, u32[]{:S(2)}, u32[]{:S(2)}) %collective-permute-start.4) | collective-permute-done | bytes 12320 | tf_op jit(solution)/shard_map/ppermute | solution.py:183
  12.5 0.5 %collective-permute-start.5 = (f32[4,3,256]{2,1,0:T(4,128)S(1)}, f32[4,3,256]{2,1,0:T(4,128)S(1)}, u32[]{:S(2)}, u32[]{:S(2)}) collective-permute-start(f32[4,3,256]{2,1,0:T(4,128)S(1)} %shard_map.92.refs_1_), channel_id=1, source_target_pairs={{0,8},{4,12},{8,0},{12,4},{16,24},{20,28},{24,16},{28,20},{1,9},{5... | collective-permute-start | bytes 36872 | tf_op jit(solution)/shard_map/ppermute | solution.py:183
  13.0 3.3 %collective-permute-done.5.refs_2_ = f32[4,3,256]{2,1,0:T(4,128)S(1)} collective-permute-done((f32[4,3,256]{2,1,0:T(4,128)S(1)}, f32[4,3,256]{2,1,0:T(4,128)S(1)}, u32[]{:S(2)}, u32[]{:S(2)}) %collective-permute-start.5) | collective-permute-done | bytes 12320 | tf_op jit(solution)/shard_map/ppermute | solution.py:183
  16.3 0.5 %shard_map.94 = (bf16[256,1024]{1,0:T(8,128)(2,1)S(1)}, bf16[4,2,32,256]{3,2,1,0:T(8,128)(2,1)S(1)}) custom-call(f32[4,3,256]{2,1,0:T(4,128)S(1)} %shard_map.91.own_ref.refs_0_, f32[4,3,256]{2,1,0:T(4,128)S(1)} %shard_map.92.refs_1_, f32[4,3,256]{2,1,0:T(4,128)S(1)} %collective-permute-done.5.refs_2_, ...), custom_call_target="tpu_custom_call" | custom-call | flops 134217728 | bytes 5410816 | tf_op jit(solution)/shard_map/pallas_call | solution.py:33
  16.9 1.6 %collective-permute-start.9 = (bf16[4,2,32,256]{3,2,1,0:T(8,128)(2,1)S(1)}, bf16[4,2,32,256]{3,2,1,0:T(8,128)(2,1)S(1)}, u32[]{:S(2)}, u32[]{:S(2)}) collective-permute-start(bf16[4,2,32,256]{3,2,1,0:T(8,128)(2,1)S(1)} %get-tuple-element.56), channel_id=1, source_target_pairs={{0,16},{4,20},{8,24},{12,28},{16,0},{20,4},{24,8},{28,12},{1,17},{... | collective-permute-start | bytes 393224 | tf_op jit(solution)/shard_map/ppermute | solution.py:183
  18.5 0.6 %shard_map.93 = (bf16[256,1024]{1,0:T(8,128)(2,1)S(1)}, f32[4,2,32,256]{3,2,1,0:T(8,128)S(1)}) custom-call(f32[4,3,256]{2,1,0:T(4,128)S(1)} %shard_map.91.own_ref.refs_0_, f32[4,3,256]{2,1,0:T(4,128)S(1)} %shard_map.92.refs_1_, f32[4,3,256]{2,1,0:T(4,128)S(1)} %collective-permute-done.5.refs_2_, bf16[2,256,128]{2,1,0:T(8,128)(2,1)S(1)} %pad_maximum_fusion.qg_ref.refs_3_, ...), custom_call_target="tpu_custom_call" | custom-call | flops 134217728 | bytes 5541888 | tf_op jit(solution)/shard_map/pallas_call | solution.py:33
  19.0 0.4 %shard_map.95 = (f32[256,128]{1,0:T(8,128)S(1)}, bf16[256,128]{1,0:T(8,128)(2,1)S(1)}, bf16[256,128]{1,0:T(8,128)(2,1)S(1)}, bf16[256,128]{1,0:T(8,128)(2,1)S(1)}) custom-call(bf16[256,1024]{1,0:T(8,128)(2,1)S(1)} %get-tuple-element.49.refs_0_, bf16[256,1024]{1,0:T(8,128)(2,1)S(1)} %get-tuple-element.50.refs_1_, ...), custom_call_target="tpu_custom_call" | custom-call | flops 134217728 | bytes 1638400 | tf_op jit(solution)/shard_map/pallas_call | solution.py:33
  19.5 0.1 collective-permute-start.6
  19.6 0.6 %collective-permute-start.7 = (bf16[256,128]{1,0:T(8,128)(2,1)S(1)}, bf16[256,128]{1,0:T(8,128)(2,1)S(1)}, u32[]{:S(2)}, u32[]{:S(2)}) collective-permute-start(bf16[256,128]{1,0:T(8,128)(2,1)S(1)} %get-tuple-element.53), channel_id=1, source_target_pairs={{0,8},{4,12},{8,0},{12,4},{16,24},{20,28},{24,16},{28,20},{1,9},{5... | collective-permute-start | bytes 196616 | tf_op jit(solution)/shard_map/ppermute | solution.py:183
  20.2 1.3 %collective-permute-start.8 = (bf16[256,128]{1,0:T(8,128)(2,1)S(1)}, bf16[256,128]{1,0:T(8,128)(2,1)S(1)}, u32[]{:S(2)}, u32[]{:S(2)}) collective-permute-start(bf16[256,128]{1,0:T(8,128)(2,1)S(1)} %get-tuple-element.54), channel_id=1, source_target_pairs={{0,12},{4,8},{8,4},{12,0},{16,28},{20,24},{24,20},{28,16},{1,13},{... | collective-permute-start | bytes 196616 | tf_op jit(solution)/shard_map/ppermute | solution.py:183
  21.4 0.5 %collective-permute-done.9.refs_1_ = bf16[4,2,32,256]{3,2,1,0:T(8,128)(2,1)S(1)} collective-permute-done((bf16[4,2,32,256]{3,2,1,0:T(8,128)(2,1)S(1)}, bf16[4,2,32,256]{3,2,1,0:T(8,128)(2,1)S(1)}, u32[]{:S(2)}, u32[]{:S(2)}) %collective-permute-start.9) | collective-permute-done | bytes 131104 | tf_op jit(solution)/shard_map/ppermute | solution.py:183
  21.9 1.6 %collective-permute-start.10 = (bf16[2,32,256]{2,1,0:T(8,128)(2,1)S(1)}, bf16[2,32,256]{2,1,0:T(8,128)(2,1)S(1)}, u32[]{:S(2)}, u32[]{:S(2)}) collective-permute-start(bf16[2,32,256]{2,1,0:T(8,128)(2,1)S(1)} %get-tuple-element.58), channel_id=1, source_target_pairs={{0,1},{1,2},{2,3},{3,0},{4,5},{5,6},{6,7},{7,4},{8,9},{9,10},{10,1... | collective-permute-start | bytes 98312 | tf_op jit(solution)/shard_map/ppermute | solution.py:242
  23.6 2.6 %collective-permute-start.11 = (bf16[2,32,256]{2,1,0:T(8,128)(2,1)S(1)}, bf16[2,32,256]{2,1,0:T(8,128)(2,1)S(1)}, u32[]{:S(2)}, u32[]{:S(2)}) collective-permute-start(bf16[2,32,256]{2,1,0:T(8,128)(2,1)S(1)} %get-tuple-element.59), channel_id=1, source_target_pairs={{0,2},{1,3},{2,0},{3,1},{4,6},{5,7},{6,4},{7,5},{8,10},{9,11},{10,... | collective-permute-start | bytes 98312 | tf_op jit(solution)/shard_map/ppermute | solution.py:242
  26.2 0.0 collective-permute-done.6.refs_1_
  26.2 1.3 %collective-permute-start.12 = (bf16[2,32,256]{2,1,0:T(8,128)(2,1)S(1)}, bf16[2,32,256]{2,1,0:T(8,128)(2,1)S(1)}, u32[]{:S(2)}, u32[]{:S(2)}) collective-permute-start(bf16[2,32,256]{2,1,0:T(8,128)(2,1)S(1)} %get-tuple-element.60), channel_id=1, source_target_pairs={{0,3},{1,0},{2,1},{3,2},{4,7},{5,4},{6,5},{7,6},{8,11},{9,8},{10,9... | collective-permute-start | bytes 98312 | tf_op jit(solution)/shard_map/ppermute | solution.py:242
  27.5 0.0 collective-permute-done.7.refs_2_
  27.5 0.0 collective-permute-done.8.refs_3_
  27.5 0.7 %shard_map.96 = f32[256,128]{1,0:T(8,128)} custom-call(f32[256,128]{1,0:T(8,128)S(1)} %get-tuple-element.51.refs_0_, bf16[256,128]{1,0:T(8,128)(2,1)S(1)} %collective-permute-done.6.refs_1_, bf16[256,128]{1,0:T(8,128)(2,1)S(1)} %collective-permute-done.7.refs_2_, bf16[256,128]{1,0:T(8,128)(2,1)S(1)} %collective-permute-done.8.refs_3_), custom_call_target="tpu_custom_call" | custom-call | bytes 458752 | tf_op jit(solution)/shard_map/pallas_call | solution.py:33
  28.2 0.0 collective-permute-done.10.refs_1_
  28.2 0.5 %collective-permute-done.11.refs_2_ = bf16[2,32,256]{2,1,0:T(8,128)(2,1)S(1)} collective-permute-done((bf16[2,32,256]{2,1,0:T(8,128)(2,1)S(1)}, bf16[2,32,256]{2,1,0:T(8,128)(2,1)S(1)}, u32[]{:S(2)}, u32[]{:S(2)}) %collective-permute-start.11) | collective-permute-done | bytes 32800 | tf_op jit(solution)/shard_map/ppermute | solution.py:242
  28.8 1.3 %collective-permute-done.12.refs_3_ = bf16[2,32,256]{2,1,0:T(8,128)(2,1)S(1)} collective-permute-done((bf16[2,32,256]{2,1,0:T(8,128)(2,1)S(1)}, bf16[2,32,256]{2,1,0:T(8,128)(2,1)S(1)}, u32[]{:S(2)}, u32[]{:S(2)}) %collective-permute-start.12) | collective-permute-done | bytes 32800 | tf_op jit(solution)/shard_map/ppermute | solution.py:242
  30.1 0.6 %shard_map.98 = (f32[32,256]{1,0:T(8,128)}, f32[32,256]{1,0:T(8,128)}) custom-call(f32[2,32,256]{2,1,0:T(8,128)S(1)} %get-tuple-element.57.refs_0_, bf16[2,32,256]{2,1,0:T(8,128)(2,1)S(1)} %collective-permute-done.10.refs_1_, bf16[2,32,256]{2,1,0:T(8,128)(2,1)S(1)} %collective-permute-done.11.refs_2_, bf16[2,32,256]{2,1,0:T(8,128)(2,1)S(1)} %collective-permute-done.12.refs_3_), custom_call_target="tpu_custom_call" | custom-call | bytes 229376 | tf_op jit(solution)/shard_map/pallas_call | solution.py:33
  (5 shorter events, 0.1 us)
Async XLA Ops:
  0.6 3.9 %copy-start.2 = (bf16[256,128]{1,0:T(8,128)(2,1)S(1)}, bf16[256,128]{1,0:T(8,128)(2,1)}, u32[]{:S(2)}) copy-start(bf16[256,128]{1,0:T(8,128)(2,1)} %param.8) | copy-start | bytes 196612
  0.6 3.9 %copy-start.3 = (bf16[256,128]{1,0:T(8,128)(2,1)S(1)}, bf16[256,128]{1,0:T(8,128)(2,1)}, u32[]{:S(2)}) copy-start(bf16[256,128]{1,0:T(8,128)(2,1)} %param.7) | copy-start | bytes 196612
  1.6 6.5 %collective-permute-start.2 = (bf16[2,256,128]{2,1,0:T(8,128)(2,1)S(1)}, bf16[2,256,128]{2,1,0:T(8,128)(2,1)S(1)}, u32[]{:S(2)}, u32[]{:S(2)}) collective-permute-start(bf16[2,256,128]{2,1,0:T(8,128)(2,1)S(1)} %pad_maximum_fusion.qg_ref.refs_3_), channel_id=1, source_target_pairs={{0,8},{4,12},{8,0},{12,4},{16,24},{20,28},{24,16},{28,20},{1,9},{5... | collective-permute-start | bytes 393224 | tf_op jit(solution)/shard_map/ppermute | solution.py:183
  4.6 1.6 %copy-start = (s32[16,16]{1,0:T(8,128)S(1)}, s32[16,16]{1,0:T(8,128)}, u32[]{:S(2)}) copy-start(s32[16,16]{1,0:T(8,128)} %mask_ref.1) | copy-start | bytes 3076
  4.6 1.6 %copy-start.1 = (s32[16]{0:T(128)S(1)}, s32[16]{0:T(128)}, u32[]{:S(2)}) copy-start(s32[16]{0:T(128)} %ids_ref.1) | copy-start | bytes 196
  4.6 5.0 %collective-permute-start = (bf16[2,256,128]{2,1,0:T(8,128)(2,1)S(1)}, bf16[2,256,128]{2,1,0:T(8,128)(2,1)S(1)}, u32[]{:S(2)}, u32[]{:S(2)}) collective-permute-start(bf16[2,256,128]{2,1,0:T(8,128)(2,1)S(1)} %pad_maximum_fusion.1.refs_0_.refs_2_), channel_id=1, source_target_pairs={{0,16},{4,20},{8,24},{12,28},{16,0},{20,4},{24,8},{28,12},{1,17},{... | collective-permute-start | bytes 393224 | tf_op jit(solution)/shard_map/ppermute | solution.py:183
  6.2 4.2 %collective-permute-start.1 = (bf16[2,256,128]{2,1,0:T(8,128)(2,1)S(1)}, bf16[2,256,128]{2,1,0:T(8,128)(2,1)S(1)}, u32[]{:S(2)}, u32[]{:S(2)}) collective-permute-start(bf16[2,256,128]{2,1,0:T(8,128)(2,1)S(1)} %pad_maximum_fusion.qg_ref.refs_3_), channel_id=1, source_target_pairs={{0,4},{4,0},{8,12},{12,8},{16,20},{20,16},{24,28},{28,24},{1,5},{5... | collective-permute-start | bytes 393224 | tf_op jit(solution)/shard_map/ppermute | solution.py:183
  8.1 2.7 %collective-permute-start.3 = (bf16[2,256,128]{2,1,0:T(8,128)(2,1)S(1)}, bf16[2,256,128]{2,1,0:T(8,128)(2,1)S(1)}, u32[]{:S(2)}, u32[]{:S(2)}) collective-permute-start(bf16[2,256,128]{2,1,0:T(8,128)(2,1)S(1)} %shard_map.89), channel_id=1, source_target_pairs={{0,4},{4,0},{8,12},{12,8},{16,20},{20,16},{24,28},{28,24},{1,5},{5... | collective-permute-start | bytes 393224 | tf_op jit(solution)/shard_map/ppermute | solution.py:183
  11.2 1.2 %collective-permute-start.4 = (f32[4,3,256]{2,1,0:T(4,128)S(1)}, f32[4,3,256]{2,1,0:T(4,128)S(1)}, u32[]{:S(2)}, u32[]{:S(2)}) collective-permute-start(f32[4,3,256]{2,1,0:T(4,128)S(1)} %shard_map.91.own_ref.refs_0_), channel_id=1, source_target_pairs={{0,4},{4,0},{8,12},{12,8},{16,20},{20,16},{24,28},{28,24},{1,5},{5... | collective-permute-start | bytes 36872 | tf_op jit(solution)/shard_map/ppermute | solution.py:183
  12.5 3.8 %collective-permute-start.5 = (f32[4,3,256]{2,1,0:T(4,128)S(1)}, f32[4,3,256]{2,1,0:T(4,128)S(1)}, u32[]{:S(2)}, u32[]{:S(2)}) collective-permute-start(f32[4,3,256]{2,1,0:T(4,128)S(1)} %shard_map.92.refs_1_), channel_id=1, source_target_pairs={{0,8},{4,12},{8,0},{12,4},{16,24},{20,28},{24,16},{28,20},{1,9},{5... | collective-permute-start | bytes 36872 | tf_op jit(solution)/shard_map/ppermute | solution.py:183
  16.9 5.0 %collective-permute-start.9 = (bf16[4,2,32,256]{3,2,1,0:T(8,128)(2,1)S(1)}, bf16[4,2,32,256]{3,2,1,0:T(8,128)(2,1)S(1)}, u32[]{:S(2)}, u32[]{:S(2)}) collective-permute-start(bf16[4,2,32,256]{3,2,1,0:T(8,128)(2,1)S(1)} %get-tuple-element.56), channel_id=1, source_target_pairs={{0,16},{4,20},{8,24},{12,28},{16,0},{20,4},{24,8},{28,12},{1,17},{... | collective-permute-start | bytes 393224 | tf_op jit(solution)/shard_map/ppermute | solution.py:183
  19.5 6.7 %collective-permute-start.6 = (bf16[256,128]{1,0:T(8,128)(2,1)S(1)}, bf16[256,128]{1,0:T(8,128)(2,1)S(1)}, u32[]{:S(2)}, u32[]{:S(2)}) collective-permute-start(bf16[256,128]{1,0:T(8,128)(2,1)S(1)} %get-tuple-element.52), channel_id=1, source_target_pairs={{0,4},{4,0},{8,12},{12,8},{16,20},{20,16},{24,28},{28,24},{1,5},{5... | collective-permute-start | bytes 196616 | tf_op jit(solution)/shard_map/ppermute | solution.py:183
  19.6 8.0 %collective-permute-start.7 = (bf16[256,128]{1,0:T(8,128)(2,1)S(1)}, bf16[256,128]{1,0:T(8,128)(2,1)S(1)}, u32[]{:S(2)}, u32[]{:S(2)}) collective-permute-start(bf16[256,128]{1,0:T(8,128)(2,1)S(1)} %get-tuple-element.53), channel_id=1, source_target_pairs={{0,8},{4,12},{8,0},{12,4},{16,24},{20,28},{24,16},{28,20},{1,9},{5... | collective-permute-start | bytes 196616 | tf_op jit(solution)/shard_map/ppermute | solution.py:183
  20.2 7.4 %collective-permute-start.8 = (bf16[256,128]{1,0:T(8,128)(2,1)S(1)}, bf16[256,128]{1,0:T(8,128)(2,1)S(1)}, u32[]{:S(2)}, u32[]{:S(2)}) collective-permute-start(bf16[256,128]{1,0:T(8,128)(2,1)S(1)} %get-tuple-element.54), channel_id=1, source_target_pairs={{0,12},{4,8},{8,4},{12,0},{16,28},{20,24},{24,20},{28,16},{1,13},{... | collective-permute-start | bytes 196616 | tf_op jit(solution)/shard_map/ppermute | solution.py:183
  21.9 6.3 %collective-permute-start.10 = (bf16[2,32,256]{2,1,0:T(8,128)(2,1)S(1)}, bf16[2,32,256]{2,1,0:T(8,128)(2,1)S(1)}, u32[]{:S(2)}, u32[]{:S(2)}) collective-permute-start(bf16[2,32,256]{2,1,0:T(8,128)(2,1)S(1)} %get-tuple-element.58), channel_id=1, source_target_pairs={{0,1},{1,2},{2,3},{3,0},{4,5},{5,6},{6,7},{7,4},{8,9},{9,10},{10,1... | collective-permute-start | bytes 98312 | tf_op jit(solution)/shard_map/ppermute | solution.py:242
  23.6 5.2 %collective-permute-start.11 = (bf16[2,32,256]{2,1,0:T(8,128)(2,1)S(1)}, bf16[2,32,256]{2,1,0:T(8,128)(2,1)S(1)}, u32[]{:S(2)}, u32[]{:S(2)}) collective-permute-start(bf16[2,32,256]{2,1,0:T(8,128)(2,1)S(1)} %get-tuple-element.59), channel_id=1, source_target_pairs={{0,2},{1,3},{2,0},{3,1},{4,6},{5,7},{6,4},{7,5},{8,10},{9,11},{10,... | collective-permute-start | bytes 98312 | tf_op jit(solution)/shard_map/ppermute | solution.py:242
  26.2 3.9 %collective-permute-start.12 = (bf16[2,32,256]{2,1,0:T(8,128)(2,1)S(1)}, bf16[2,32,256]{2,1,0:T(8,128)(2,1)S(1)}, u32[]{:S(2)}, u32[]{:S(2)}) collective-permute-start(bf16[2,32,256]{2,1,0:T(8,128)(2,1)S(1)} %get-tuple-element.60), channel_id=1, source_target_pairs={{0,3},{1,0},{2,1},{3,2},{4,7},{5,4},{6,5},{7,6},{8,11},{9,8},{10,9... | collective-permute-start | bytes 98312 | tf_op jit(solution)/shard_map/ppermute | solution.py:242

commit v5 on v4

--- a/solution.py
+++ b/solution.py
@@ -59,72 +59,65 @@
     out_ref[...] = in_ref[...]
 
 
-def unit_kernel(units, factor, limit_ref, qg_ref, *refs):
-    kv_refs, (exp_ref, dprob_ref, stats_ref) = refs[:units], refs[units:]
-    unit = qg_ref.shape[1]
+def tile_kernel(tiles, factor, *refs):
+    count = len(tiles)
+    limit_refs, qg_refs, kv_refs = (refs[i * count : (i + 1) * count] for i in range(3))
+    exp_refs, dprob_refs, stats_refs = (refs[i * count : (i + 1) * count] for i in range(3, 6))
+    unit = qg_refs[0].shape[1]
     half = unit // 2
-    q_rows, g_rows = qg_ref[0], qg_ref[1]
     row = lax.broadcasted_iota(jnp.int32, (half, 1), 0)
-    scores = []
-    for u in range(units):
-        products = dot(kv_refs[u][0], q_rows, 1, 1) * factor
-        for part in range(2):
-            allowed = limit_ref[u * 2 + part : u * 2 + part + 1, :] >= row
-            scores.append(jnp.where(allowed, products[part * half : (part + 1) * half], MASKED))
-    top = functools.reduce(jnp.maximum, [jnp.max(s, axis=0, keepdims=True) for s in scores])
-    top = jnp.maximum(top, FLOOR)
-    total = jnp.zeros_like(top)
-    weighted = jnp.zeros_like(top)
-    for u in range(units):
-        dprobs = dot(kv_refs[u][1], g_rows, 1, 1)
-        for part in range(2):
-            start = u * unit + part * half
-            weights = jnp.exp2(scores[u * 2 + part] - top)
-            here = dprobs[part * half : (part + 1) * half]
-            exp_ref[start : start + half] = weights
-            dprob_ref[start : start + half] = here
-            total += jnp.sum(weights, axis=0, keepdims=True)
-            weighted += jnp.sum(weights * here, axis=0, keepdims=True)
-    stats_ref[0:1, :] = top
-    stats_ref[1:2, :] = total
-    stats_ref[2:3, :] = weighted
-
-
-def collect_kernel(*refs):
-    for r in range(SHARE):
-        refs[-1][r] = refs[r][...]
+    for i, (_, u) in enumerate(tiles):
+        products = dot(kv_refs[i][0], qg_refs[i][0], 1, 1) * factor
+        scores = jnp.concatenate(
+            [
+                jnp.where(
+                    limit_refs[i][u * 2 + part : u * 2 + part + 1, :] >= row,
+                    products[part * half : (part + 1) * half],
+                    MASKED,
+                )
+                for part in range(2)
+            ],
+            axis=0,
+        )
+        top = jnp.maximum(jnp.max(scores, axis=0, keepdims=True), FLOOR)
+        weights = jnp.exp2(scores - top)
+        dprobs = dot(kv_refs[i][1], qg_refs[i][1], 1, 1)
+        exp_refs[i][...] = weights
+        dprob_refs[i][...] = dprobs
+        stats_refs[i][0:1, :] = top
+        stats_refs[i][1:2, :] = jnp.sum(weights, axis=0, keepdims=True)
+        stats_refs[i][2:3, :] = jnp.sum(weights * dprobs, axis=0, keepdims=True)
 
 
 def merge_stats(left, right):
     top = jnp.maximum(left[0:1], right[0:1])
     first, second = jnp.exp2(left[0:1] - top), jnp.exp2(right[0:1] - top)
-    return (
-        top,
-        left[1:2] * first + right[1:2] * second,
-        left[2:3] * first + right[2:3] * second,
-    )
-
-
-def pair_kernel(own_ref, other_ref, out_ref):
+    return jnp.concatenate(
+        [top, left[1:2] * first + right[1:2] * second, left[2:3] * first + right[2:3] * second],
+        axis=0,
+    )
+
+
+def collect_kernel(units, *refs):
     for r in range(SHARE):
-        for row, value in enumerate(merge_stats(own_ref[r], other_ref[r ^ 1])):
-            out_ref[r, row : row + 1, :] = value
-
-
-def grads_kernel(u, scale, *refs):
-    (own_ref, near_ref, far_ref), refs = refs[:3], refs[3:]
+        stats = functools.reduce(merge_stats, [refs[r * units + u][...] for u in range(units)])
+        refs[-1][r] = stats
+
+
+def grads_kernel(scale, *refs):
+    all_refs, refs = refs[:SHARE], refs[SHARE:]
     qg_refs, refs = refs[:SHARE], refs[SHARE:]
-    exp_refs, dprob_refs = refs[:SHARE], refs[SHARE : 2 * SHARE]
-    ds_ref, out_ref = refs[2 * SHARE :]
+    exp_refs, dprob_refs, stats_refs = (refs[i * SHARE : (i + 1) * SHARE] for i in range(3))
+    ds_ref, out_ref = refs[3 * SHARE :]
     _, unit, width = qg_refs[0].shape
     sub = width // GROUP
     dk, dv = 0.0, 0.0
     for r in range(SHARE):
-        top, total, weighted = merge_stats(near_ref[r], far_ref[r ^ 2])
-        share = jnp.exp2(own_ref[r, 0:1] - top) / total
-        delta = weighted / total
-        probs = exp_refs[r][u * unit : (u + 1) * unit] * share
-        dprobs = dprob_refs[r][u * unit : (u + 1) * unit]
+        whole = functools.reduce(merge_stats, [all_refs[s][r ^ s] for s in range(SHARE)])
+        share = jnp.exp2(stats_refs[r][0:1] - whole[0:1]) / whole[1:2]
+        delta = whole[2:3] / whole[1:2]
+        probs = exp_refs[r][...] * share
+        dprobs = dprob_refs[r][...]
         dscores = (probs * (dprobs - delta)).astype(BF16)
         ds_ref[:, r * unit : (r + 1) * unit] = dscores
         dv += dot(probs.astype(BF16), qg_refs[r][1], 1, 0)
@@ -195,35 +188,41 @@
     qgs = [qg, swap(qg, 1), far_qg, swap(sent_qg, 1)]
 
     product = 2 * unit * unit * width
-    grid = jax.ShapeDtypeStruct((units * unit, unit), F32)
-    results = [
-        call(
-            functools.partial(unit_kernel, units, factor),
-            [grid, grid, jax.ShapeDtypeStruct((3, unit), F32)],
-            [limits[r], qgs[r]] + kvs,
-            flops=2 * units * product,
+    grid = jax.ShapeDtypeStruct((unit, unit), F32)
+    rows_out = jax.ShapeDtypeStruct((3, unit), F32)
+    results = {}
+
+    def run_tiles(tiles):
+        outs = call(
+            functools.partial(tile_kernel, tiles, factor),
+            [grid] * (2 * len(tiles)) + [rows_out] * len(tiles),
+            [limits[r] for r, _ in tiles] + [qgs[r] for r, _ in tiles] + [kvs[u] for _, u in tiles],
+            flops=2 * product * len(tiles),
         )
-        for r in range(SHARE)
-    ]
-    exps, dprobs, stats = zip(*results)
+        for i, tile in enumerate(tiles):
+            results[tile] = outs[i :: len(tiles)]
+
+    run_tiles([(0, 0), (2, 0)])
+    run_tiles([(r, u) for u in range(1, units) for r in (0, 2)])
+    run_tiles([(r, u) for u in range(units) for r in (1, 3)])
     (stats,) = call(
-        collect_kernel, [jax.ShapeDtypeStruct((SHARE, 3, unit), F32)], list(stats)
-    )
-    (chip_stats,) = call(
-        pair_kernel, [jax.ShapeDtypeStruct(stats.shape, F32)], [stats, swap(stats, 1)]
-    )
-    operands = [stats, chip_stats, swap(chip_stats, 2)] + qgs + list(exps) + list(dprobs)
+        functools.partial(collect_kernel, units),
+        [jax.ShapeDtypeStruct((SHARE, 3, unit), F32)],
+        [results[r, u][2] for r in range(SHARE) for u in range(units)],
+    )
+    came = {step: swap(stats, step) for step in (3, 2, 1)}
+    both_stats = [stats] + [came[step] for step in range(1, SHARE)]
 
     parts = (GROUP, 2, sub, unit)
     scores, shares = [], []
     for u in reversed(range(units)):
         dscores, share = call(
-            functools.partial(grads_kernel, u, scale),
+            functools.partial(grads_kernel, scale),
             [
                 jax.ShapeDtypeStruct((unit, rows), BF16),
                 jax.ShapeDtypeStruct(parts, BF16 if u else F32),
             ],
-            operands,
+            both_stats + qgs + [results[r, u][i] for i in range(3) for r in range(SHARE)],
             flops=2 * SHARE * product,
         )
         scores.insert(0, dscores)

time: 30.9 us -> 30 us (0.971)
  waiting for transfers between devices: 9.39 us -> 7.31 us
  starting transfers between devices: 14.3 us -> 15.7 us
    ppermute x10 -> x11, waiting for transfers between devices: 7.52 us -> 5.44 us  [swap(): return lax.ppermute(x, 'ctx', [(i, i ^ step) for i in range(ctx_size)])]
    ppermute x10 -> x11, starting transfers between devices: 8.75 us -> 10.1 us  [swap(): return lax.ppermute(x, 'ctx', [(i, i ^ step) for i in range(ctx_size)])]
    pallas_call x14 -> x12, Pallas kernels: 5.27 us -> 5.17 us  [call(): pl.pallas_call(kernel, out_shape=out_shape, in_specs=in_specs or [vmem()...]
  transfers between devices with their start and end apart: 13 -> 14, of which waited for: 7 -> 7; matrix products, arithmetic and copies ran while one was open for 0% -> 0% of each run, Pallas kernels for 12% -> 11%
where the time goes in v5:
time: 30 us; the launch traced here: 29.9 us
  starting transfers between devices  15.7 us (52%)
  waiting for transfers between devices  7.31 us (24%)
  Pallas kernels  5.17 us (17%)
  other arithmetic  0.94 us (3%)
  between operations  0.77 us (3%)
    ppermute x11, starting transfers between devices, swap(): return lax.ppermute(x, 'ctx', [(i, i ^ step) for i in range(ctx_size)])  10.1 us
    ppermute x3, starting transfers between devices, cross(): return lax.ppermute(x, 'fsdp', pairs)  5.57 us
    ppermute x11, waiting for transfers between devices, swap(): return lax.ppermute(x, 'ctx', [(i, i ^ step) for i in range(ctx_size)])  5.44 us
    pallas_call x12, Pallas kernels, call(): pl.pallas_call(kernel, out_shape=out_shape, in_specs=in_specs or [vmem()...  5.17 us
    ppermute x3, waiting for transfers between devices, cross(): return lax.ppermute(x, 'fsdp', pairs)  1.88 us
    another operation x2, other arithmetic, body(): qg, kv = (jnp.stack([queries, out_grad]), jnp.stack([keys, values]))  0.94 us
  transfers between devices with their start and end apart: 14, of which 7 were waited for; matrix products, arithmetic and copies ran while one was open for 0% of the time, Pallas kernels for 11%

profile of v5, /device:TPU:0, one launch (start us, length us, event | category | flops | bytes accessed | tf_op | source)
XLA Modules:
  0.0 29.9 jit_solution(3578764501082235711)
XLA Ops:
  0.6 0.0 copy-start.2
  0.6 0.0 copy-start.3
  0.7 0.9 %pad_maximum_fusion.refs_2_.refs_4_ = bf16[2,256,128]{2,1,0:T(8,128)(2,1)S(1)} fusion(bf16[1,256,128]{2,1,0:T(8,128)(2,1)} %bitcast.6, bf16[1,256,128]{2,1,0:T(8,128)(2,1)} %bitcast.7), kind=kLoop, calls=%fused_computation | loop fusion | flops 65536 | bytes 262144 | tf_op jit(solution)/shard_map/stack | solution.py:178
  1.6 3.0 %collective-permute-start = (bf16[2,256,128]{2,1,0:T(8,128)(2,1)S(1)}, bf16[2,256,128]{2,1,0:T(8,128)(2,1)S(1)}, u32[]{:S(2)}, u32[]{:S(2)}) collective-permute-start(bf16[2,256,128]{2,1,0:T(8,128)(2,1)S(1)} %pad_maximum_fusion.refs_2_.refs_4_), channel_id=1, source_target_pairs={{0,8},{4,12},{8,0},{12,4},{16,24},{20,28},{24,16},{28,20},{1,9},{5... | collective-permute-start | bytes 393224 | tf_op jit(solution)/shard_map/ppermute | solution.py:176
  4.6 0.0 copy-done.2
  4.6 0.0 copy-done.3
  4.6 0.0 copy-start
  4.6 0.0 copy-start.1
  4.6 1.6 %collective-permute-start.1 = (bf16[2,256,128]{2,1,0:T(8,128)(2,1)S(1)}, bf16[2,256,128]{2,1,0:T(8,128)(2,1)S(1)}, u32[]{:S(2)}, u32[]{:S(2)}) collective-permute-start(bf16[2,256,128]{2,1,0:T(8,128)(2,1)S(1)} %pad_maximum_fusion.1.refs_4_.refs_5_.refs_8_.refs_9_.refs_2_), channel_id=1, source_target_pairs={{0,16},{4,20},{8,24},{12,28},{16,0},{20,4},{24,8},{28,12},{1,17},{... | collective-permute-start | bytes 393224 | tf_op jit(solution)/shard_map/ppermute | solution.py:176
  6.2 0.0 collective-permute-start.2
  6.2 0.0 copy-done
  6.2 0.0 copy-done.1
  6.2 0.8 %shard_map.85 = (s32[4,256]{1,0:T(4,128)S(1)}, s32[4,256]{1,0:T(4,128)S(1)}, s32[4,256]{1,0:T(4,128)S(1)}, s32[4,256]{1,0:T(4,128)S(1)}) custom-call(s32[16]{0:T(128)S(1)} %copy-done.1, s32[16,16]{1,0:T(8,128)S(1)} %copy-done), custom_call_target="tpu_custom_call" | custom-call | bytes 17472 | tf_op jit(solution)/shard_map/pallas_call | solution.py:33
  7.0 1.1 %collective-permute-done.refs_3_.in_ref.refs_6_ = bf16[2,256,128]{2,1,0:T(8,128)(2,1)S(1)} collective-permute-done((bf16[2,256,128]{2,1,0:T(8,128)(2,1)S(1)}, bf16[2,256,128]{2,1,0:T(8,128)(2,1)S(1)}, u32[]{:S(2)}, u32[]{:S(2)}) %collective-permute-start) | collective-permute-done | bytes 131104 | tf_op jit(solution)/shard_map/ppermute | solution.py:176
  8.1 0.1 collective-permute-start.3
  8.2 0.4 %shard_map.86 = (f32[256,256]{1,0:T(8,128)S(1)}, f32[256,256]{1,0:T(8,128)S(1)}, f32[256,256]{1,0:T(8,128)S(1)}, f32[256,256]{1,0:T(8,128)S(1)}, f32[3,256]{1,0:T(4,128)S(1)}, /*index=5*/f32[3,256]{1,0:T(4,128)S(1)}) custom-call(s32[4,256]{1,0:T(4,128)S(1)} %get-tuple-element.45.refs_0_.after_ref, s32[4,256]{1,0:T(4,128)S(1)} %get-tuple-element.46.refs_1_, ...), custom_call_target="tpu_custom_call" | custom-call | flops 67108864 | bytes 1587200 | tf_op jit(solution)/shard_map/pallas_call | solution.py:33
  8.6 1.1 %collective-permute-done.1.refs_4_.refs_5_.refs_10_.refs_11_.refs_3_ = bf16[2,256,128]{2,1,0:T(8,128)(2,1)S(1)} collective-permute-done((bf16[2,256,128]{2,1,0:T(8,128)(2,1)S(1)}, bf16[2,256,128]{2,1,0:T(8,128)(2,1)S(1)}, u32[]{:S(2)}, u32[]{:S(2)}) %collective-permute-start.1) | collective-permute-done | bytes 131104 | tf_op jit(solution)/shard_map/ppermute | solution.py:176
  9.6 0.4 %shard_map.87 = (f32[256,256]{1,0:T(8,128)S(1)}, f32[256,256]{1,0:T(8,128)S(1)}, f32[256,256]{1,0:T(8,128)S(1)}, f32[256,256]{1,0:T(8,128)S(1)}, f32[3,256]{1,0:T(4,128)S(1)}, /*index=5*/f32[3,256]{1,0:T(4,128)S(1)}) custom-call(s32[4,256]{1,0:T(4,128)S(1)} %get-tuple-element.45.refs_0_.after_ref, s32[4,256]{1,0:T(4,128)S(1)} %get-tuple-element.46.refs_1_, ...), custom_call_target="tpu_custom_call" | custom-call | flops 67108864 | bytes 1587200 | tf_op jit(solution)/shard_map/pallas_call | solution.py:33
  10.1 0.0 collective-permute-done.2.refs_4_.refs_6_.refs_5_
  10.1 0.0 collective-permute-done.3.refs_5_.refs_7_
  10.1 0.6 %shard_map.89 = (f32[256,256]{1,0:T(8,128)S(1)}, f32[256,256]{1,0:T(8,128)S(1)}, f32[256,256]{1,0:T(8,128)S(1)}, f32[256,256]{1,0:T(8,128)S(1)}, f32[256,256]{1,...) custom-call(s32[4,256]{1,0:T(4,128)S(1)} %get-tuple-element.49.refs_, ...), custom_call_target="tpu_custom_call" | custom-call | flops 134217728 | bytes 3174400 | tf_op jit(solution)/shard_map/pallas_call | solution.py:33
  10.7 1.0 %collective-permute-start.6 = (f32[4,3,256]{2,1,0:T(4,128)S(1)}, f32[4,3,256]{2,1,0:T(4,128)S(1)}, u32[]{:S(2)}, u32[]{:S(2)}) collective-permute-start(f32[4,3,256]{2,1,0:T(4,128)S(1)} %shard_map.90.refs_0_), channel_id=1, source_target_pairs={{0,12},{4,8},{8,4},{12,0},{16,28},{20,24},{24,20},{28,16},{1,13},{... | collective-permute-start | bytes 36872 | tf_op jit(solution)/shard_map/ppermute | solution.py:176
  11.7 0.3 %collective-permute-start.5 = (f32[4,3,256]{2,1,0:T(4,128)S(1)}, f32[4,3,256]{2,1,0:T(4,128)S(1)}, u32[]{:S(2)}, u32[]{:S(2)}) collective-permute-start(f32[4,3,256]{2,1,0:T(4,128)S(1)} %shard_map.90.refs_0_), channel_id=1, source_target_pairs={{0,8},{4,12},{8,0},{12,4},{16,24},{20,28},{24,16},{28,20},{1,9},{5... | collective-permute-start | bytes 36872 | tf_op jit(solution)/shard_map/ppermute | solution.py:176
  12.0 0.6 %collective-permute-start.4 = (f32[4,3,256]{2,1,0:T(4,128)S(1)}, f32[4,3,256]{2,1,0:T(4,128)S(1)}, u32[]{:S(2)}, u32[]{:S(2)}) collective-permute-start(f32[4,3,256]{2,1,0:T(4,128)S(1)} %shard_map.90.refs_0_), channel_id=1, source_target_pairs={{0,4},{4,0},{8,12},{12,8},{16,20},{20,16},{24,28},{28,24},{1,5},{5... | collective-permute-start | bytes 36872 | tf_op jit(solution)/shard_map/ppermute | solution.py:176
  12.6 1.3 %collective-permute-done.6.refs_3_ = f32[4,3,256]{2,1,0:T(4,128)S(1)} collective-permute-done((f32[4,3,256]{2,1,0:T(4,128)S(1)}, f32[4,3,256]{2,1,0:T(4,128)S(1)}, u32[]{:S(2)}, u32[]{:S(2)}) %collective-permute-start.6) | collective-permute-done | bytes 12320 | tf_op jit(solution)/shard_map/ppermute | solution.py:176
  13.9 1.5 %collective-permute-done.5.refs_2_ = f32[4,3,256]{2,1,0:T(4,128)S(1)} collective-permute-done((f32[4,3,256]{2,1,0:T(4,128)S(1)}, f32[4,3,256]{2,1,0:T(4,128)S(1)}, u32[]{:S(2)}, u32[]{:S(2)}) %collective-permute-start.5) | collective-permute-done | bytes 12320 | tf_op jit(solution)/shard_map/ppermute | solution.py:176
  15.4 0.0 collective-permute-done.4.refs_1_
  15.4 0.6 %shard_map.92 = (bf16[256,1024]{1,0:T(8,128)(2,1)S(1)}, bf16[4,2,32,256]{3,2,1,0:T(8,128)(2,1)S(1)}) custom-call(f32[4,3,256]{2,1,0:T(4,128)S(1)} %shard_map.90.refs_0_, f32[4,3,256]{2,1,0:T(4,128)S(1)} %collective-permute-done.4.refs_1_, f32[4,3,256]{2,1,0:T(4,128)S(1)} %collective-permute-done.5.refs_2_, f32[4,3,256]{2,1,0:T(4,128)S(1)} %collective-permute-done.6.refs_3_, ...), custom_call_target="tpu_custom_call" | custom-call | flops 134217728 | bytes 3338240 | tf_op jit(solution)/shard_map/pallas_call | solution.py:33
  16.0 1.6 %collective-permute-start.10 = (bf16[4,2,32,256]{3,2,1,0:T(8,128)(2,1)S(1)}, bf16[4,2,32,256]{3,2,1,0:T(8,128)(2,1)S(1)}, u32[]{:S(2)}, u32[]{:S(2)}) collective-permute-start(bf16[4,2,32,256]{3,2,1,0:T(8,128)(2,1)S(1)} %get-tuple-element.80), channel_id=1, source_target_pairs={{0,16},{4,20},{8,24},{12,28},{16,0},{20,4},{24,8},{28,12},{1,17},{... | collective-permute-start | bytes 393224 | tf_op jit(solution)/shard_map/ppermute | solution.py:176
  17.6 0.6 %shard_map.91 = (bf16[256,1024]{1,0:T(8,128)(2,1)S(1)}, f32[4,2,32,256]{3,2,1,0:T(8,128)S(1)}) custom-call(f32[4,3,256]{2,1,0:T(4,128)S(1)} %shard_map.90.refs_0_, f32[4,3,256]{2,1,0:T(4,128)S(1)} %collective-permute-done.4.refs_1_, f32[4,3,256]{2,1,0:T(4,128)S(1)} %collective-permute-done.5.refs_2_, f32[4,3,256]{2,1,0:T(4,128)S(1)} %collective-permute-done.6.refs_3_, ...), custom_call_target="tpu_custom_call" | custom-call | flops 134217728 | bytes 3469312 | tf_op jit(solution)/shard_map/pallas_call | solution.py:33
  18.2 0.4 %shard_map.93 = (f32[256,128]{1,0:T(8,128)S(1)}, bf16[256,128]{1,0:T(8,128)(2,1)S(1)}, bf16[256,128]{1,0:T(8,128)(2,1)S(1)}, bf16[256,128]{1,0:T(8,128)(2,1)S(1)}) custom-call(bf16[256,1024]{1,0:T(8,128)(2,1)S(1)} %get-tuple-element.65.refs_0_, bf16[256,1024]{1,0:T(8,128)(2,1)S(1)} %get-tuple-element.74.refs_1_, ...), custom_call_target="tpu_custom_call" | custom-call | flops 134217728 | bytes 1638400 | tf_op jit(solution)/shard_map/pallas_call | solution.py:33
  18.6 0.1 collective-permute-start.7
  18.7 0.6 %collective-permute-start.8 = (bf16[256,128]{1,0:T(8,128)(2,1)S(1)}, bf16[256,128]{1,0:T(8,128)(2,1)S(1)}, u32[]{:S(2)}, u32[]{:S(2)}) collective-permute-start(bf16[256,128]{1,0:T(8,128)(2,1)S(1)} %get-tuple-element.77), channel_id=1, source_target_pairs={{0,8},{4,12},{8,0},{12,4},{16,24},{20,28},{24,16},{28,20},{1,9},{5... | collective-permute-start | bytes 196616 | tf_op jit(solution)/shard_map/ppermute | solution.py:176
  19.3 1.3 %collective-permute-start.9 = (bf16[256,128]{1,0:T(8,128)(2,1)S(1)}, bf16[256,128]{1,0:T(8,128)(2,1)S(1)}, u32[]{:S(2)}, u32[]{:S(2)}) collective-permute-start(bf16[256,128]{1,0:T(8,128)(2,1)S(1)} %get-tuple-element.78), channel_id=1, source_target_pairs={{0,12},{4,8},{8,4},{12,0},{16,28},{20,24},{24,20},{28,16},{1,13},{... | collective-permute-start | bytes 196616 | tf_op jit(solution)/shard_map/ppermute | solution.py:176
  20.6 0.5 %collective-permute-done.10.refs_1_ = bf16[4,2,32,256]{3,2,1,0:T(8,128)(2,1)S(1)} collective-permute-done((bf16[4,2,32,256]{3,2,1,0:T(8,128)(2,1)S(1)}, bf16[4,2,32,256]{3,2,1,0:T(8,128)(2,1)S(1)}, u32[]{:S(2)}, u32[]{:S(2)}) %collective-permute-start.10) | collective-permute-done | bytes 131104 | tf_op jit(solution)/shard_map/ppermute | solution.py:176
  21.1 1.6 %collective-permute-start.11 = (bf16[2,32,256]{2,1,0:T(8,128)(2,1)S(1)}, bf16[2,32,256]{2,1,0:T(8,128)(2,1)S(1)}, u32[]{:S(2)}, u32[]{:S(2)}) collective-permute-start(bf16[2,32,256]{2,1,0:T(8,128)(2,1)S(1)} %get-tuple-element.82), channel_id=1, source_target_pairs={{0,1},{1,2},{2,3},{3,0},{4,5},{5,6},{6,7},{7,4},{8,9},{9,10},{10,1... | collective-permute-start | bytes 98312 | tf_op jit(solution)/shard_map/ppermute | solution.py:241
  22.7 2.6 %collective-permute-start.12 = (bf16[2,32,256]{2,1,0:T(8,128)(2,1)S(1)}, bf16[2,32,256]{2,1,0:T(8,128)(2,1)S(1)}, u32[]{:S(2)}, u32[]{:S(2)}) collective-permute-start(bf16[2,32,256]{2,1,0:T(8,128)(2,1)S(1)} %get-tuple-element.83), channel_id=1, source_target_pairs={{0,2},{1,3},{2,0},{3,1},{4,6},{5,7},{6,4},{7,5},{8,10},{9,11},{10,... | collective-permute-start | bytes 98312 | tf_op jit(solution)/shard_map/ppermute | solution.py:241
  25.3 0.0 collective-permute-done.7.refs_1_
  25.3 1.3 %collective-permute-start.13 = (bf16[2,32,256]{2,1,0:T(8,128)(2,1)S(1)}, bf16[2,32,256]{2,1,0:T(8,128)(2,1)S(1)}, u32[]{:S(2)}, u32[]{:S(2)}) collective-permute-start(bf16[2,32,256]{2,1,0:T(8,128)(2,1)S(1)} %get-tuple-element.84), channel_id=1, source_target_pairs={{0,3},{1,0},{2,1},{3,2},{4,7},{5,4},{6,5},{7,6},{8,11},{9,8},{10,9... | collective-permute-start | bytes 98312 | tf_op jit(solution)/shard_map/ppermute | solution.py:241
  26.7 0.0 collective-permute-done.8.refs_2_
  26.7 0.0 collective-permute-done.9.refs_3_
  26.7 0.7 %shard_map.94 = f32[256,128]{1,0:T(8,128)} custom-call(f32[256,128]{1,0:T(8,128)S(1)} %get-tuple-element.75.refs_0_, bf16[256,128]{1,0:T(8,128)(2,1)S(1)} %collective-permute-done.7.refs_1_, bf16[256,128]{1,0:T(8,128)(2,1)S(1)} %collective-permute-done.8.refs_2_, bf16[256,128]{1,0:T(8,128)(2,1)S(1)} %collective-permute-done.9.refs_3_), custom_call_target="tpu_custom_call" | custom-call | bytes 458752 | tf_op jit(solution)/shard_map/pallas_call | solution.py:33
  27.4 0.0 collective-permute-done.11.refs_1_
  27.4 0.6 %collective-permute-done.12.refs_2_ = bf16[2,32,256]{2,1,0:T(8,128)(2,1)S(1)} collective-permute-done((bf16[2,32,256]{2,1,0:T(8,128)(2,1)S(1)}, bf16[2,32,256]{2,1,0:T(8,128)(2,1)S(1)}, u32[]{:S(2)}, u32[]{:S(2)}) %collective-permute-start.12) | collective-permute-done | bytes 32800 | tf_op jit(solution)/shard_map/ppermute | solution.py:241
  27.9 1.3 %collective-permute-done.13.refs_3_ = bf16[2,32,256]{2,1,0:T(8,128)(2,1)S(1)} collective-permute-done((bf16[2,32,256]{2,1,0:T(8,128)(2,1)S(1)}, bf16[2,32,256]{2,1,0:T(8,128)(2,1)S(1)}, u32[]{:S(2)}, u32[]{:S(2)}) %collective-permute-start.13) | collective-permute-done | bytes 32800 | tf_op jit(solution)/shard_map/ppermute | solution.py:241
  29.2 0.6 %shard_map.96 = (f32[32,256]{1,0:T(8,128)}, f32[32,256]{1,0:T(8,128)}) custom-call(f32[2,32,256]{2,1,0:T(8,128)S(1)} %get-tuple-element.81.refs_0_, bf16[2,32,256]{2,1,0:T(8,128)(2,1)S(1)} %collective-permute-done.11.refs_1_, bf16[2,32,256]{2,1,0:T(8,128)(2,1)S(1)} %collective-permute-done.12.refs_2_, bf16[2,32,256]{2,1,0:T(8,128)(2,1)S(1)} %collective-permute-done.13.refs_3_), custom_call_target="tpu_custom_call" | custom-call | bytes 229376 | tf_op jit(solution)/shard_map/pallas_call | solution.py:33
  (4 shorter events, 0.1 us)
Async XLA Ops:
  0.6 3.9 %copy-start.2 = (bf16[256,128]{1,0:T(8,128)(2,1)S(1)}, bf16[256,128]{1,0:T(8,128)(2,1)}, u32[]{:S(2)}) copy-start(bf16[256,128]{1,0:T(8,128)(2,1)} %param.8) | copy-start | bytes 196612
  0.6 3.9 %copy-start.3 = (bf16[256,128]{1,0:T(8,128)(2,1)S(1)}, bf16[256,128]{1,0:T(8,128)(2,1)}, u32[]{:S(2)}) copy-start(bf16[256,128]{1,0:T(8,128)(2,1)} %param.7) | copy-start | bytes 196612
  1.6 6.5 %collective-permute-start = (bf16[2,256,128]{2,1,0:T(8,128)(2,1)S(1)}, bf16[2,256,128]{2,1,0:T(8,128)(2,1)S(1)}, u32[]{:S(2)}, u32[]{:S(2)}) collective-permute-start(bf16[2,256,128]{2,1,0:T(8,128)(2,1)S(1)} %pad_maximum_fusion.refs_2_.refs_4_), channel_id=1, source_target_pairs={{0,8},{4,12},{8,0},{12,4},{16,24},{20,28},{24,16},{28,20},{1,9},{5... | collective-permute-start | bytes 393224 | tf_op jit(solution)/shard_map/ppermute | solution.py:176
  4.6 1.6 %copy-start = (s32[16,16]{1,0:T(8,128)S(1)}, s32[16,16]{1,0:T(8,128)}, u32[]{:S(2)}) copy-start(s32[16,16]{1,0:T(8,128)} %mask_ref.1) | copy-start | bytes 3076
  4.6 1.6 %copy-start.1 = (s32[16]{0:T(128)S(1)}, s32[16]{0:T(128)}, u32[]{:S(2)}) copy-start(s32[16]{0:T(128)} %ids_ref.1) | copy-start | bytes 196
  4.6 5.0 %collective-permute-start.1 = (bf16[2,256,128]{2,1,0:T(8,128)(2,1)S(1)}, bf16[2,256,128]{2,1,0:T(8,128)(2,1)S(1)}, u32[]{:S(2)}, u32[]{:S(2)}) collective-permute-start(bf16[2,256,128]{2,1,0:T(8,128)(2,1)S(1)} %pad_maximum_fusion.1.refs_4_.refs_5_.refs_8_.refs_9_.refs_2_), channel_id=1, source_target_pairs={{0,16},{4,20},{8,24},{12,28},{16,0},{20,4},{24,8},{28,12},{1,17},{... | collective-permute-start | bytes 393224 | tf_op jit(solution)/shard_map/ppermute | solution.py:176
  6.2 3.9 %collective-permute-start.2 = (bf16[2,256,128]{2,1,0:T(8,128)(2,1)S(1)}, bf16[2,256,128]{2,1,0:T(8,128)(2,1)S(1)}, u32[]{:S(2)}, u32[]{:S(2)}) collective-permute-start(bf16[2,256,128]{2,1,0:T(8,128)(2,1)S(1)} %pad_maximum_fusion.refs_2_.refs_4_), channel_id=1, source_target_pairs={{0,4},{4,0},{8,12},{12,8},{16,20},{20,16},{24,28},{28,24},{1,5},{5... | collective-permute-start | bytes 393224 | tf_op jit(solution)/shard_map/ppermute | solution.py:176
  8.1 2.0 %collective-permute-start.3 = (bf16[2,256,128]{2,1,0:T(8,128)(2,1)S(1)}, bf16[2,256,128]{2,1,0:T(8,128)(2,1)S(1)}, u32[]{:S(2)}, u32[]{:S(2)}) collective-permute-start(bf16[2,256,128]{2,1,0:T(8,128)(2,1)S(1)} %shard_map.88), channel_id=1, source_target_pairs={{0,4},{4,0},{8,12},{12,8},{16,20},{20,16},{24,28},{28,24},{1,5},{5... | collective-permute-start | bytes 393224 | tf_op jit(solution)/shard_map/ppermute | solution.py:176
  10.7 3.2 %collective-permute-start.6 = (f32[4,3,256]{2,1,0:T(4,128)S(1)}, f32[4,3,256]{2,1,0:T(4,128)S(1)}, u32[]{:S(2)}, u32[]{:S(2)}) collective-permute-start(f32[4,3,256]{2,1,0:T(4,128)S(1)} %shard_map.90.refs_0_), channel_id=1, source_target_pairs={{0,12},{4,8},{8,4},{12,0},{16,28},{20,24},{24,20},{28,16},{1,13},{... | collective-permute-start | bytes 36872 | tf_op jit(solution)/shard_map/ppermute | solution.py:176
  11.7 3.8 %collective-permute-start.5 = (f32[4,3,256]{2,1,0:T(4,128)S(1)}, f32[4,3,256]{2,1,0:T(4,128)S(1)}, u32[]{:S(2)}, u32[]{:S(2)}) collective-permute-start(f32[4,3,256]{2,1,0:T(4,128)S(1)} %shard_map.90.refs_0_), channel_id=1, source_target_pairs={{0,8},{4,12},{8,0},{12,4},{16,24},{20,28},{24,16},{28,20},{1,9},{5... | collective-permute-start | bytes 36872 | tf_op jit(solution)/shard_map/ppermute | solution.py:176
  12.0 3.4 %collective-permute-start.4 = (f32[4,3,256]{2,1,0:T(4,128)S(1)}, f32[4,3,256]{2,1,0:T(4,128)S(1)}, u32[]{:S(2)}, u32[]{:S(2)}) collective-permute-start(f32[4,3,256]{2,1,0:T(4,128)S(1)} %shard_map.90.refs_0_), channel_id=1, source_target_pairs={{0,4},{4,0},{8,12},{12,8},{16,20},{20,16},{24,28},{28,24},{1,5},{5... | collective-permute-start | bytes 36872 | tf_op jit(solution)/shard_map/ppermute | solution.py:176
  16.0 5.0 %collective-permute-start.10 = (bf16[4,2,32,256]{3,2,1,0:T(8,128)(2,1)S(1)}, bf16[4,2,32,256]{3,2,1,0:T(8,128)(2,1)S(1)}, u32[]{:S(2)}, u32[]{:S(2)}) collective-permute-start(bf16[4,2,32,256]{3,2,1,0:T(8,128)(2,1)S(1)} %get-tuple-element.80), channel_id=1, source_target_pairs={{0,16},{4,20},{8,24},{12,28},{16,0},{20,4},{24,8},{28,12},{1,17},{... | collective-permute-start | bytes 393224 | tf_op jit(solution)/shard_map/ppermute | solution.py:176
  18.6 6.7 %collective-permute-start.7 = (bf16[256,128]{1,0:T(8,128)(2,1)S(1)}, bf16[256,128]{1,0:T(8,128)(2,1)S(1)}, u32[]{:S(2)}, u32[]{:S(2)}) collective-permute-start(bf16[256,128]{1,0:T(8,128)(2,1)S(1)} %get-tuple-element.76), channel_id=1, source_target_pairs={{0,4},{4,0},{8,12},{12,8},{16,20},{20,16},{24,28},{28,24},{1,5},{5... | collective-permute-start | bytes 196616 | tf_op jit(solution)/shard_map/ppermute | solution.py:176
  18.7 8.0 %collective-permute-start.8 = (bf16[256,128]{1,0:T(8,128)(2,1)S(1)}, bf16[256,128]{1,0:T(8,128)(2,1)S(1)}, u32[]{:S(2)}, u32[]{:S(2)}) collective-permute-start(bf16[256,128]{1,0:T(8,128)(2,1)S(1)} %get-tuple-element.77), channel_id=1, source_target_pairs={{0,8},{4,12},{8,0},{12,4},{16,24},{20,28},{24,16},{28,20},{1,9},{5... | collective-permute-start | bytes 196616 | tf_op jit(solution)/shard_map/ppermute | solution.py:176
  19.3 7.4 %collective-permute-start.9 = (bf16[256,128]{1,0:T(8,128)(2,1)S(1)}, bf16[256,128]{1,0:T(8,128)(2,1)S(1)}, u32[]{:S(2)}, u32[]{:S(2)}) collective-permute-start(bf16[256,128]{1,0:T(8,128)(2,1)S(1)} %get-tuple-element.78), channel_id=1, source_target_pairs={{0,12},{4,8},{8,4},{12,0},{16,28},{20,24},{24,20},{28,16},{1,13},{... | collective-permute-start | bytes 196616 | tf_op jit(solution)/shard_map/ppermute | solution.py:176
  21.1 6.3 %collective-permute-start.11 = (bf16[2,32,256]{2,1,0:T(8,128)(2,1)S(1)}, bf16[2,32,256]{2,1,0:T(8,128)(2,1)S(1)}, u32[]{:S(2)}, u32[]{:S(2)}) collective-permute-start(bf16[2,32,256]{2,1,0:T(8,128)(2,1)S(1)} %get-tuple-element.82), channel_id=1, source_target_pairs={{0,1},{1,2},{2,3},{3,0},{4,5},{5,6},{6,7},{7,4},{8,9},{9,10},{10,1... | collective-permute-start | bytes 98312 | tf_op jit(solution)/shard_map/ppermute | solution.py:241
  22.7 5.2 %collective-permute-start.12 = (bf16[2,32,256]{2,1,0:T(8,128)(2,1)S(1)}, bf16[2,32,256]{2,1,0:T(8,128)(2,1)S(1)}, u32[]{:S(2)}, u32[]{:S(2)}) collective-permute-start(bf16[2,32,256]{2,1,0:T(8,128)(2,1)S(1)} %get-tuple-element.83), channel_id=1, source_target_pairs={{0,2},{1,3},{2,0},{3,1},{4,6},{5,7},{6,4},{7,5},{8,10},{9,11},{10,... | collective-permute-start | bytes 98312 | tf_op jit(solution)/shard_map/ppermute | solution.py:241
  25.3 3.9 %collective-permute-start.13 = (bf16[2,32,256]{2,1,0:T(8,128)(2,1)S(1)}, bf16[2,32,256]{2,1,0:T(8,128)(2,1)S(1)}, u32[]{:S(2)}, u32[]{:S(2)}) collective-permute-start(bf16[2,32,256]{2,1,0:T(8,128)(2,1)S(1)} %get-tuple-element.84), channel_id=1, source_target_pairs={{0,3},{1,0},{2,1},{3,2},{4,7},{5,4},{6,5},{7,6},{8,11},{9,8},{10,9... | collective-permute-start | bytes 98312 | tf_op jit(solution)/shard_map/ppermute | solution.py:241

commit v6 on v5

--- a/solution.py
+++ b/solution.py
@@ -129,13 +129,23 @@
         out_ref[part, 1] = dv_tall[part * sub : (part + 1) * sub]
 
 
+TARGETS = ((2, 3, 1, 0), (3, 2, 0, 1), (1, 0, 3, 2))
+
+
+def target(lane, h):
+    place = TARGETS[h - 1][0]
+    for i in range(1, GROUP):
+        place = jnp.where(lane == i, TARGETS[h - 1][i], place)
+    return place
+
+
 def merge_kernel(*refs):
     terms, total_ref, (own_ref, *far_refs) = refs[: -GROUP - 1], refs[-1], refs[-GROUP - 1 : -1]
     total_ref[...] = sum(ref[...].astype(F32) for ref in terms)
     lane = lax.axis_index("fsdp") % GROUP
     own_ref[...] = total_ref[lane]
     for h in range(1, GROUP):
-        far_refs[h - 1][...] = total_ref[(lane + h) % GROUP].astype(BF16)
+        far_refs[h - 1][...] = total_ref[target(lane, h)].astype(BF16)
 
 
 def query_kernel(units, scale, *refs):
@@ -237,7 +247,7 @@
     far = [swap(x, step + 1) for step, x in enumerate(far)]
 
     def cross(x, step):
-        pairs = [(i, i // GROUP * GROUP + (i + step) % GROUP) for i in range(lanes)]
+        pairs = [(i, i // GROUP * GROUP + TARGETS[step - 1][i % GROUP]) for i in range(lanes)]
         return lax.ppermute(x, "fsdp", pairs)
 
     own_part, *others_part = call(

time: 30 us -> 29.7 us (0.990)
  starting transfers between devices: 15.7 us -> 14.3 us
  waiting for transfers between devices: 7.31 us -> 8.32 us
    ppermute x3, starting transfers between devices: 5.57 us -> 4.22 us  [cross(): return lax.ppermute(x, 'fsdp', pairs)]
    ppermute x3, waiting for transfers between devices: 1.88 us -> 2.89 us  [cross(): return lax.ppermute(x, 'fsdp', pairs)]
  transfers between devices with their start and end apart: 14 -> 14, of which waited for: 7 -> 8; matrix products, arithmetic and copies ran while one was open for 0% -> 0% of each run, Pallas kernels for 11% -> 11%
where the time goes in v6:
time: 29.7 us; the launch traced here: 29.5 us
  starting transfers between devices  14.3 us (48%)
  waiting for transfers between devices  8.32 us (28%)
  Pallas kernels  5.17 us (17%)
  other arithmetic  0.94 us (3%)
  between operations  0.77 us (3%)
    ppermute x11, starting transfers between devices, swap(): return lax.ppermute(x, 'ctx', [(i, i ^ step) for i in range(ctx_size)])  10.1 us
    ppermute x11, waiting for transfers between devices, swap(): return lax.ppermute(x, 'ctx', [(i, i ^ step) for i in range(ctx_size)])  5.44 us
    pallas_call x12, Pallas kernels, call(): pl.pallas_call(kernel, out_shape=out_shape, in_specs=in_specs or [vmem()...  5.17 us
    ppermute x3, starting transfers between devices, cross(): return lax.ppermute(x, 'fsdp', pairs)  4.22 us
    ppermute x3, waiting for transfers between devices, cross(): return lax.ppermute(x, 'fsdp', pairs)  2.89 us
    another operation x2, other arithmetic, body(): qg, kv = (jnp.stack([queries, out_grad]), jnp.stack([keys, values]))  0.94 us
  transfers between devices with their start and end apart: 14, of which 8 were waited for; matrix products, arithmetic and copies ran while one was open for 0% of the time, Pallas kernels for 11%

profile of v6, /device:TPU:0, one launch (start us, length us, event | category | flops | bytes accessed | tf_op | source)
XLA Modules:
  0.0 29.5 jit_solution(6237070805483911616)
XLA Ops:
  0.6 0.0 copy-start.2
  0.6 0.0 copy-start.3
  0.7 0.9 %pad_maximum_fusion.refs_2_.refs_4_ = bf16[2,256,128]{2,1,0:T(8,128)(2,1)S(1)} fusion(bf16[1,256,128]{2,1,0:T(8,128)(2,1)} %bitcast.6, bf16[1,256,128]{2,1,0:T(8,128)(2,1)} %bitcast.7), kind=kLoop, calls=%fused_computation | loop fusion | flops 65536 | bytes 262144 | tf_op jit(solution)/shard_map/stack | solution.py:188
  1.6 3.0 %collective-permute-start = (bf16[2,256,128]{2,1,0:T(8,128)(2,1)S(1)}, bf16[2,256,128]{2,1,0:T(8,128)(2,1)S(1)}, u32[]{:S(2)}, u32[]{:S(2)}) collective-permute-start(bf16[2,256,128]{2,1,0:T(8,128)(2,1)S(1)} %pad_maximum_fusion.refs_2_.refs_4_), channel_id=1, source_target_pairs={{0,8},{4,12},{8,0},{12,4},{16,24},{20,28},{24,16},{28,20},{1,9},{5... | collective-permute-start | bytes 393224 | tf_op jit(solution)/shard_map/ppermute | solution.py:186
  4.6 0.0 copy-done.2
  4.6 0.0 copy-done.3
  4.6 0.0 copy-start
  4.6 0.0 copy-start.1
  4.6 1.6 %collective-permute-start.1 = (bf16[2,256,128]{2,1,0:T(8,128)(2,1)S(1)}, bf16[2,256,128]{2,1,0:T(8,128)(2,1)S(1)}, u32[]{:S(2)}, u32[]{:S(2)}) collective-permute-start(bf16[2,256,128]{2,1,0:T(8,128)(2,1)S(1)} %pad_maximum_fusion.1.refs_4_.refs_5_.refs_8_.refs_9_.refs_2_), channel_id=1, source_target_pairs={{0,16},{4,20},{8,24},{12,28},{16,0},{20,4},{24,8},{28,12},{1,17},{... | collective-permute-start | bytes 393224 | tf_op jit(solution)/shard_map/ppermute | solution.py:186
  6.2 0.0 collective-permute-start.2
  6.2 0.0 copy-done
  6.2 0.0 copy-done.1
  6.2 0.8 %shard_map.85 = (s32[4,256]{1,0:T(4,128)S(1)}, s32[4,256]{1,0:T(4,128)S(1)}, s32[4,256]{1,0:T(4,128)S(1)}, s32[4,256]{1,0:T(4,128)S(1)}) custom-call(s32[16]{0:T(128)S(1)} %copy-done.1, s32[16,16]{1,0:T(8,128)S(1)} %copy-done), custom_call_target="tpu_custom_call" | custom-call | bytes 17472 | tf_op jit(solution)/shard_map/pallas_call | solution.py:33
  7.0 1.1 %collective-permute-done.refs_3_.in_ref.refs_6_ = bf16[2,256,128]{2,1,0:T(8,128)(2,1)S(1)} collective-permute-done((bf16[2,256,128]{2,1,0:T(8,128)(2,1)S(1)}, bf16[2,256,128]{2,1,0:T(8,128)(2,1)S(1)}, u32[]{:S(2)}, u32[]{:S(2)}) %collective-permute-start) | collective-permute-done | bytes 131104 | tf_op jit(solution)/shard_map/ppermute | solution.py:186
  8.1 0.1 collective-permute-start.3
  8.2 0.4 %shard_map.86 = (f32[256,256]{1,0:T(8,128)S(1)}, f32[256,256]{1,0:T(8,128)S(1)}, f32[256,256]{1,0:T(8,128)S(1)}, f32[256,256]{1,0:T(8,128)S(1)}, f32[3,256]{1,0:T(4,128)S(1)}, /*index=5*/f32[3,256]{1,0:T(4,128)S(1)}) custom-call(s32[4,256]{1,0:T(4,128)S(1)} %get-tuple-element.45.refs_0_.after_ref, s32[4,256]{1,0:T(4,128)S(1)} %get-tuple-element.46.refs_1_, ...), custom_call_target="tpu_custom_call" | custom-call | flops 67108864 | bytes 1587200 | tf_op jit(solution)/shard_map/pallas_call | solution.py:33
  8.6 1.1 %collective-permute-done.1.refs_4_.refs_5_.refs_10_.refs_11_.refs_3_ = bf16[2,256,128]{2,1,0:T(8,128)(2,1)S(1)} collective-permute-done((bf16[2,256,128]{2,1,0:T(8,128)(2,1)S(1)}, bf16[2,256,128]{2,1,0:T(8,128)(2,1)S(1)}, u32[]{:S(2)}, u32[]{:S(2)}) %collective-permute-start.1) | collective-permute-done | bytes 131104 | tf_op jit(solution)/shard_map/ppermute | solution.py:186
  9.6 0.4 %shard_map.87 = (f32[256,256]{1,0:T(8,128)S(1)}, f32[256,256]{1,0:T(8,128)S(1)}, f32[256,256]{1,0:T(8,128)S(1)}, f32[256,256]{1,0:T(8,128)S(1)}, f32[3,256]{1,0:T(4,128)S(1)}, /*index=5*/f32[3,256]{1,0:T(4,128)S(1)}) custom-call(s32[4,256]{1,0:T(4,128)S(1)} %get-tuple-element.45.refs_0_.after_ref, s32[4,256]{1,0:T(4,128)S(1)} %get-tuple-element.46.refs_1_, ...), custom_call_target="tpu_custom_call" | custom-call | flops 67108864 | bytes 1587200 | tf_op jit(solution)/shard_map/pallas_call | solution.py:33
  10.1 0.0 collective-permute-done.2.refs_4_.refs_6_.refs_5_
  10.1 0.0 collective-permute-done.3.refs_5_.refs_7_
  10.1 0.6 %shard_map.89 = (f32[256,256]{1,0:T(8,128)S(1)}, f32[256,256]{1,0:T(8,128)S(1)}, f32[256,256]{1,0:T(8,128)S(1)}, f32[256,256]{1,0:T(8,128)S(1)}, f32[256,256]{1,...) custom-call(s32[4,256]{1,0:T(4,128)S(1)} %get-tuple-element.49.refs_, ...), custom_call_target="tpu_custom_call" | custom-call | flops 134217728 | bytes 3174400 | tf_op jit(solution)/shard_map/pallas_call | solution.py:33
  10.7 1.0 %collective-permute-start.6 = (f32[4,3,256]{2,1,0:T(4,128)S(1)}, f32[4,3,256]{2,1,0:T(4,128)S(1)}, u32[]{:S(2)}, u32[]{:S(2)}) collective-permute-start(f32[4,3,256]{2,1,0:T(4,128)S(1)} %shard_map.90.refs_0_), channel_id=1, source_target_pairs={{0,12},{4,8},{8,4},{12,0},{16,28},{20,24},{24,20},{28,16},{1,13},{... | collective-permute-start | bytes 36872 | tf_op jit(solution)/shard_map/ppermute | solution.py:186
  11.7 0.3 %collective-permute-start.5 = (f32[4,3,256]{2,1,0:T(4,128)S(1)}, f32[4,3,256]{2,1,0:T(4,128)S(1)}, u32[]{:S(2)}, u32[]{:S(2)}) collective-permute-start(f32[4,3,256]{2,1,0:T(4,128)S(1)} %shard_map.90.refs_0_), channel_id=1, source_target_pairs={{0,8},{4,12},{8,0},{12,4},{16,24},{20,28},{24,16},{28,20},{1,9},{5... | collective-permute-start | bytes 36872 | tf_op jit(solution)/shard_map/ppermute | solution.py:186
  12.0 0.6 %collective-permute-start.4 = (f32[4,3,256]{2,1,0:T(4,128)S(1)}, f32[4,3,256]{2,1,0:T(4,128)S(1)}, u32[]{:S(2)}, u32[]{:S(2)}) collective-permute-start(f32[4,3,256]{2,1,0:T(4,128)S(1)} %shard_map.90.refs_0_), channel_id=1, source_target_pairs={{0,4},{4,0},{8,12},{12,8},{16,20},{20,16},{24,28},{28,24},{1,5},{5... | collective-permute-start | bytes 36872 | tf_op jit(solution)/shard_map/ppermute | solution.py:186
  12.6 1.3 %collective-permute-done.6.refs_3_ = f32[4,3,256]{2,1,0:T(4,128)S(1)} collective-permute-done((f32[4,3,256]{2,1,0:T(4,128)S(1)}, f32[4,3,256]{2,1,0:T(4,128)S(1)}, u32[]{:S(2)}, u32[]{:S(2)}) %collective-permute-start.6) | collective-permute-done | bytes 12320 | tf_op jit(solution)/shard_map/ppermute | solution.py:186
  13.9 1.5 %collective-permute-done.5.refs_2_ = f32[4,3,256]{2,1,0:T(4,128)S(1)} collective-permute-done((f32[4,3,256]{2,1,0:T(4,128)S(1)}, f32[4,3,256]{2,1,0:T(4,128)S(1)}, u32[]{:S(2)}, u32[]{:S(2)}) %collective-permute-start.5) | collective-permute-done | bytes 12320 | tf_op jit(solution)/shard_map/ppermute | solution.py:186
  15.4 0.0 collective-permute-done.4.refs_1_
  15.4 0.6 %shard_map.92 = (bf16[256,1024]{1,0:T(8,128)(2,1)S(1)}, bf16[4,2,32,256]{3,2,1,0:T(8,128)(2,1)S(1)}) custom-call(f32[4,3,256]{2,1,0:T(4,128)S(1)} %shard_map.90.refs_0_, f32[4,3,256]{2,1,0:T(4,128)S(1)} %collective-permute-done.4.refs_1_, f32[4,3,256]{2,1,0:T(4,128)S(1)} %collective-permute-done.5.refs_2_, f32[4,3,256]{2,1,0:T(4,128)S(1)} %collective-permute-done.6.refs_3_, ...), custom_call_target="tpu_custom_call" | custom-call | flops 134217728 | bytes 3338240 | tf_op jit(solution)/shard_map/pallas_call | solution.py:33
  16.0 1.6 %collective-permute-start.10 = (bf16[4,2,32,256]{3,2,1,0:T(8,128)(2,1)S(1)}, bf16[4,2,32,256]{3,2,1,0:T(8,128)(2,1)S(1)}, u32[]{:S(2)}, u32[]{:S(2)}) collective-permute-start(bf16[4,2,32,256]{3,2,1,0:T(8,128)(2,1)S(1)} %get-tuple-element.80), channel_id=1, source_target_pairs={{0,16},{4,20},{8,24},{12,28},{16,0},{20,4},{24,8},{28,12},{1,17},{... | collective-permute-start | bytes 393224 | tf_op jit(solution)/shard_map/ppermute | solution.py:186
  17.6 0.6 %shard_map.91 = (bf16[256,1024]{1,0:T(8,128)(2,1)S(1)}, f32[4,2,32,256]{3,2,1,0:T(8,128)S(1)}) custom-call(f32[4,3,256]{2,1,0:T(4,128)S(1)} %shard_map.90.refs_0_, f32[4,3,256]{2,1,0:T(4,128)S(1)} %collective-permute-done.4.refs_1_, f32[4,3,256]{2,1,0:T(4,128)S(1)} %collective-permute-done.5.refs_2_, f32[4,3,256]{2,1,0:T(4,128)S(1)} %collective-permute-done.6.refs_3_, ...), custom_call_target="tpu_custom_call" | custom-call | flops 134217728 | bytes 3469312 | tf_op jit(solution)/shard_map/pallas_call | solution.py:33
  18.2 0.4 %shard_map.93 = (f32[256,128]{1,0:T(8,128)S(1)}, bf16[256,128]{1,0:T(8,128)(2,1)S(1)}, bf16[256,128]{1,0:T(8,128)(2,1)S(1)}, bf16[256,128]{1,0:T(8,128)(2,1)S(1)}) custom-call(bf16[256,1024]{1,0:T(8,128)(2,1)S(1)} %get-tuple-element.65.refs_0_, bf16[256,1024]{1,0:T(8,128)(2,1)S(1)} %get-tuple-element.74.refs_1_, ...), custom_call_target="tpu_custom_call" | custom-call | flops 134217728 | bytes 1638400 | tf_op jit(solution)/shard_map/pallas_call | solution.py:33
  18.6 0.1 collective-permute-start.7
  18.7 0.6 %collective-permute-start.8 = (bf16[256,128]{1,0:T(8,128)(2,1)S(1)}, bf16[256,128]{1,0:T(8,128)(2,1)S(1)}, u32[]{:S(2)}, u32[]{:S(2)}) collective-permute-start(bf16[256,128]{1,0:T(8,128)(2,1)S(1)} %get-tuple-element.77), channel_id=1, source_target_pairs={{0,8},{4,12},{8,0},{12,4},{16,24},{20,28},{24,16},{28,20},{1,9},{5... | collective-permute-start | bytes 196616 | tf_op jit(solution)/shard_map/ppermute | solution.py:186
  19.3 1.3 %collective-permute-start.9 = (bf16[256,128]{1,0:T(8,128)(2,1)S(1)}, bf16[256,128]{1,0:T(8,128)(2,1)S(1)}, u32[]{:S(2)}, u32[]{:S(2)}) collective-permute-start(bf16[256,128]{1,0:T(8,128)(2,1)S(1)} %get-tuple-element.78), channel_id=1, source_target_pairs={{0,12},{4,8},{8,4},{12,0},{16,28},{20,24},{24,20},{28,16},{1,13},{... | collective-permute-start | bytes 196616 | tf_op jit(solution)/shard_map/ppermute | solution.py:186
  20.6 0.5 %collective-permute-done.10.refs_1_ = bf16[4,2,32,256]{3,2,1,0:T(8,128)(2,1)S(1)} collective-permute-done((bf16[4,2,32,256]{3,2,1,0:T(8,128)(2,1)S(1)}, bf16[4,2,32,256]{3,2,1,0:T(8,128)(2,1)S(1)}, u32[]{:S(2)}, u32[]{:S(2)}) %collective-permute-start.10) | collective-permute-done | bytes 131104 | tf_op jit(solution)/shard_map/ppermute | solution.py:186
  21.1 2.6 %collective-permute-start.11 = (bf16[2,32,256]{2,1,0:T(8,128)(2,1)S(1)}, bf16[2,32,256]{2,1,0:T(8,128)(2,1)S(1)}, u32[]{:S(2)}, u32[]{:S(2)}) collective-permute-start(bf16[2,32,256]{2,1,0:T(8,128)(2,1)S(1)} %get-tuple-element.82), channel_id=1, source_target_pairs={{0,2},{1,3},{2,1},{3,0},{4,6},{5,7},{6,5},{7,4},{8,10},{9,11},{10,... | collective-permute-start | bytes 98312 | tf_op jit(solution)/shard_map/ppermute | solution.py:251
  23.7 1.2 %collective-permute-start.12 = (bf16[2,32,256]{2,1,0:T(8,128)(2,1)S(1)}, bf16[2,32,256]{2,1,0:T(8,128)(2,1)S(1)}, u32[]{:S(2)}, u32[]{:S(2)}) collective-permute-start(bf16[2,32,256]{2,1,0:T(8,128)(2,1)S(1)} %get-tuple-element.83), channel_id=1, source_target_pairs={{0,3},{1,2},{2,0},{3,1},{4,7},{5,6},{6,4},{7,5},{8,11},{9,10},{10,... | collective-permute-start | bytes 98312 | tf_op jit(solution)/shard_map/ppermute | solution.py:251
  25.0 0.0 collective-permute-done.7.refs_1_
  25.0 0.3 %collective-permute-start.13 = (bf16[2,32,256]{2,1,0:T(8,128)(2,1)S(1)}, bf16[2,32,256]{2,1,0:T(8,128)(2,1)S(1)}, u32[]{:S(2)}, u32[]{:S(2)}) collective-permute-start(bf16[2,32,256]{2,1,0:T(8,128)(2,1)S(1)} %get-tuple-element.84), channel_id=1, source_target_pairs={{0,1},{1,0},{2,3},{3,2},{4,5},{5,4},{6,7},{7,6},{8,9},{9,8},{10,11... | collective-permute-start | bytes 98312 | tf_op jit(solution)/shard_map/ppermute | solution.py:251
  25.3 0.0 collective-permute-done.8.refs_2_
  25.3 0.0 collective-permute-done.9.refs_3_
  25.3 0.7 %shard_map.94 = f32[256,128]{1,0:T(8,128)} custom-call(f32[256,128]{1,0:T(8,128)S(1)} %get-tuple-element.75.refs_0_, bf16[256,128]{1,0:T(8,128)(2,1)S(1)} %collective-permute-done.7.refs_1_, bf16[256,128]{1,0:T(8,128)(2,1)S(1)} %collective-permute-done.8.refs_2_, bf16[256,128]{1,0:T(8,128)(2,1)S(1)} %collective-permute-done.9.refs_3_), custom_call_target="tpu_custom_call" | custom-call | bytes 458752 | tf_op jit(solution)/shard_map/pallas_call | solution.py:33
  26.0 0.8 %collective-permute-done.11.refs_1_ = bf16[2,32,256]{2,1,0:T(8,128)(2,1)S(1)} collective-permute-done((bf16[2,32,256]{2,1,0:T(8,128)(2,1)S(1)}, bf16[2,32,256]{2,1,0:T(8,128)(2,1)S(1)}, u32[]{:S(2)}, u32[]{:S(2)}) %collective-permute-start.11) | collective-permute-done | bytes 32800 | tf_op jit(solution)/shard_map/ppermute | solution.py:251
  26.9 1.7 %collective-permute-done.12.refs_2_ = bf16[2,32,256]{2,1,0:T(8,128)(2,1)S(1)} collective-permute-done((bf16[2,32,256]{2,1,0:T(8,128)(2,1)S(1)}, bf16[2,32,256]{2,1,0:T(8,128)(2,1)S(1)}, u32[]{:S(2)}, u32[]{:S(2)}) %collective-permute-start.12) | collective-permute-done | bytes 32800 | tf_op jit(solution)/shard_map/ppermute | solution.py:251
  28.6 0.4 %collective-permute-done.13.refs_3_ = bf16[2,32,256]{2,1,0:T(8,128)(2,1)S(1)} collective-permute-done((bf16[2,32,256]{2,1,0:T(8,128)(2,1)S(1)}, bf16[2,32,256]{2,1,0:T(8,128)(2,1)S(1)}, u32[]{:S(2)}, u32[]{:S(2)}) %collective-permute-start.13) | collective-permute-done | bytes 32800 | tf_op jit(solution)/shard_map/ppermute | solution.py:251
  28.9 0.6 %shard_map.96 = (f32[32,256]{1,0:T(8,128)}, f32[32,256]{1,0:T(8,128)}) custom-call(f32[2,32,256]{2,1,0:T(8,128)S(1)} %get-tuple-element.81.refs_0_, bf16[2,32,256]{2,1,0:T(8,128)(2,1)S(1)} %collective-permute-done.11.refs_1_, bf16[2,32,256]{2,1,0:T(8,128)(2,1)S(1)} %collective-permute-done.12.refs_2_, bf16[2,32,256]{2,1,0:T(8,128)(2,1)S(1)} %collective-permute-done.13.refs_3_), custom_call_target="tpu_custom_call" | custom-call | bytes 229376 | tf_op jit(solution)/shard_map/pallas_call | solution.py:33
  (4 shorter events, 0.1 us)
Async XLA Ops:
  0.6 3.9 %copy-start.2 = (bf16[256,128]{1,0:T(8,128)(2,1)S(1)}, bf16[256,128]{1,0:T(8,128)(2,1)}, u32[]{:S(2)}) copy-start(bf16[256,128]{1,0:T(8,128)(2,1)} %param.8) | copy-start | bytes 196612
  0.6 3.9 %copy-start.3 = (bf16[256,128]{1,0:T(8,128)(2,1)S(1)}, bf16[256,128]{1,0:T(8,128)(2,1)}, u32[]{:S(2)}) copy-start(bf16[256,128]{1,0:T(8,128)(2,1)} %param.7) | copy-start | bytes 196612
  1.6 6.5 %collective-permute-start = (bf16[2,256,128]{2,1,0:T(8,128)(2,1)S(1)}, bf16[2,256,128]{2,1,0:T(8,128)(2,1)S(1)}, u32[]{:S(2)}, u32[]{:S(2)}) collective-permute-start(bf16[2,256,128]{2,1,0:T(8,128)(2,1)S(1)} %pad_maximum_fusion.refs_2_.refs_4_), channel_id=1, source_target_pairs={{0,8},{4,12},{8,0},{12,4},{16,24},{20,28},{24,16},{28,20},{1,9},{5... | collective-permute-start | bytes 393224 | tf_op jit(solution)/shard_map/ppermute | solution.py:186
  4.6 1.6 %copy-start = (s32[16,16]{1,0:T(8,128)S(1)}, s32[16,16]{1,0:T(8,128)}, u32[]{:S(2)}) copy-start(s32[16,16]{1,0:T(8,128)} %mask_ref.1) | copy-start | bytes 3076
  4.6 1.6 %copy-start.1 = (s32[16]{0:T(128)S(1)}, s32[16]{0:T(128)}, u32[]{:S(2)}) copy-start(s32[16]{0:T(128)} %ids_ref.1) | copy-start | bytes 196
  4.6 5.0 %collective-permute-start.1 = (bf16[2,256,128]{2,1,0:T(8,128)(2,1)S(1)}, bf16[2,256,128]{2,1,0:T(8,128)(2,1)S(1)}, u32[]{:S(2)}, u32[]{:S(2)}) collective-permute-start(bf16[2,256,128]{2,1,0:T(8,128)(2,1)S(1)} %pad_maximum_fusion.1.refs_4_.refs_5_.refs_8_.refs_9_.refs_2_), channel_id=1, source_target_pairs={{0,16},{4,20},{8,24},{12,28},{16,0},{20,4},{24,8},{28,12},{1,17},{... | collective-permute-start | bytes 393224 | tf_op jit(solution)/shard_map/ppermute | solution.py:186
  6.2 3.9 %collective-permute-start.2 = (bf16[2,256,128]{2,1,0:T(8,128)(2,1)S(1)}, bf16[2,256,128]{2,1,0:T(8,128)(2,1)S(1)}, u32[]{:S(2)}, u32[]{:S(2)}) collective-permute-start(bf16[2,256,128]{2,1,0:T(8,128)(2,1)S(1)} %pad_maximum_fusion.refs_2_.refs_4_), channel_id=1, source_target_pairs={{0,4},{4,0},{8,12},{12,8},{16,20},{20,16},{24,28},{28,24},{1,5},{5... | collective-permute-start | bytes 393224 | tf_op jit(solution)/shard_map/ppermute | solution.py:186
  8.1 2.0 %collective-permute-start.3 = (bf16[2,256,128]{2,1,0:T(8,128)(2,1)S(1)}, bf16[2,256,128]{2,1,0:T(8,128)(2,1)S(1)}, u32[]{:S(2)}, u32[]{:S(2)}) collective-permute-start(bf16[2,256,128]{2,1,0:T(8,128)(2,1)S(1)} %shard_map.88), channel_id=1, source_target_pairs={{0,4},{4,0},{8,12},{12,8},{16,20},{20,16},{24,28},{28,24},{1,5},{5... | collective-permute-start | bytes 393224 | tf_op jit(solution)/shard_map/ppermute | solution.py:186
  10.7 3.2 %collective-permute-start.6 = (f32[4,3,256]{2,1,0:T(4,128)S(1)}, f32[4,3,256]{2,1,0:T(4,128)S(1)}, u32[]{:S(2)}, u32[]{:S(2)}) collective-permute-start(f32[4,3,256]{2,1,0:T(4,128)S(1)} %shard_map.90.refs_0_), channel_id=1, source_target_pairs={{0,12},{4,8},{8,4},{12,0},{16,28},{20,24},{24,20},{28,16},{1,13},{... | collective-permute-start | bytes 36872 | tf_op jit(solution)/shard_map/ppermute | solution.py:186
  11.7 3.8 %collective-permute-start.5 = (f32[4,3,256]{2,1,0:T(4,128)S(1)}, f32[4,3,256]{2,1,0:T(4,128)S(1)}, u32[]{:S(2)}, u32[]{:S(2)}) collective-permute-start(f32[4,3,256]{2,1,0:T(4,128)S(1)} %shard_map.90.refs_0_), channel_id=1, source_target_pairs={{0,8},{4,12},{8,0},{12,4},{16,24},{20,28},{24,16},{28,20},{1,9},{5... | collective-permute-start | bytes 36872 | tf_op jit(solution)/shard_map/ppermute | solution.py:186
  12.0 3.4 %collective-permute-start.4 = (f32[4,3,256]{2,1,0:T(4,128)S(1)}, f32[4,3,256]{2,1,0:T(4,128)S(1)}, u32[]{:S(2)}, u32[]{:S(2)}) collective-permute-start(f32[4,3,256]{2,1,0:T(4,128)S(1)} %shard_map.90.refs_0_), channel_id=1, source_target_pairs={{0,4},{4,0},{8,12},{12,8},{16,20},{20,16},{24,28},{28,24},{1,5},{5... | collective-permute-start | bytes 36872 | tf_op jit(solution)/shard_map/ppermute | solution.py:186
  16.0 5.0 %collective-permute-start.10 = (bf16[4,2,32,256]{3,2,1,0:T(8,128)(2,1)S(1)}, bf16[4,2,32,256]{3,2,1,0:T(8,128)(2,1)S(1)}, u32[]{:S(2)}, u32[]{:S(2)}) collective-permute-start(bf16[4,2,32,256]{3,2,1,0:T(8,128)(2,1)S(1)} %get-tuple-element.80), channel_id=1, source_target_pairs={{0,16},{4,20},{8,24},{12,28},{16,0},{20,4},{24,8},{28,12},{1,17},{... | collective-permute-start | bytes 393224 | tf_op jit(solution)/shard_map/ppermute | solution.py:186
  18.6 6.3 %collective-permute-start.7 = (bf16[256,128]{1,0:T(8,128)(2,1)S(1)}, bf16[256,128]{1,0:T(8,128)(2,1)S(1)}, u32[]{:S(2)}, u32[]{:S(2)}) collective-permute-start(bf16[256,128]{1,0:T(8,128)(2,1)S(1)} %get-tuple-element.76), channel_id=1, source_target_pairs={{0,4},{4,0},{8,12},{12,8},{16,20},{20,16},{24,28},{28,24},{1,5},{5... | collective-permute-start | bytes 196616 | tf_op jit(solution)/shard_map/ppermute | solution.py:186
  18.7 6.6 %collective-permute-start.8 = (bf16[256,128]{1,0:T(8,128)(2,1)S(1)}, bf16[256,128]{1,0:T(8,128)(2,1)S(1)}, u32[]{:S(2)}, u32[]{:S(2)}) collective-permute-start(bf16[256,128]{1,0:T(8,128)(2,1)S(1)} %get-tuple-element.77), channel_id=1, source_target_pairs={{0,8},{4,12},{8,0},{12,4},{16,24},{20,28},{24,16},{28,20},{1,9},{5... | collective-permute-start | bytes 196616 | tf_op jit(solution)/shard_map/ppermute | solution.py:186
  19.3 6.0 %collective-permute-start.9 = (bf16[256,128]{1,0:T(8,128)(2,1)S(1)}, bf16[256,128]{1,0:T(8,128)(2,1)S(1)}, u32[]{:S(2)}, u32[]{:S(2)}) collective-permute-start(bf16[256,128]{1,0:T(8,128)(2,1)S(1)} %get-tuple-element.78), channel_id=1, source_target_pairs={{0,12},{4,8},{8,4},{12,0},{16,28},{20,24},{24,20},{28,16},{1,13},{... | collective-permute-start | bytes 196616 | tf_op jit(solution)/shard_map/ppermute | solution.py:186
  21.1 5.8 %collective-permute-start.11 = (bf16[2,32,256]{2,1,0:T(8,128)(2,1)S(1)}, bf16[2,32,256]{2,1,0:T(8,128)(2,1)S(1)}, u32[]{:S(2)}, u32[]{:S(2)}) collective-permute-start(bf16[2,32,256]{2,1,0:T(8,128)(2,1)S(1)} %get-tuple-element.82), channel_id=1, source_target_pairs={{0,2},{1,3},{2,1},{3,0},{4,6},{5,7},{6,5},{7,4},{8,10},{9,11},{10,... | collective-permute-start | bytes 98312 | tf_op jit(solution)/shard_map/ppermute | solution.py:251
  23.7 4.8 %collective-permute-start.12 = (bf16[2,32,256]{2,1,0:T(8,128)(2,1)S(1)}, bf16[2,32,256]{2,1,0:T(8,128)(2,1)S(1)}, u32[]{:S(2)}, u32[]{:S(2)}) collective-permute-start(bf16[2,32,256]{2,1,0:T(8,128)(2,1)S(1)} %get-tuple-element.83), channel_id=1, source_target_pairs={{0,3},{1,2},{2,0},{3,1},{4,7},{5,6},{6,4},{7,5},{8,11},{9,10},{10,... | collective-permute-start | bytes 98312 | tf_op jit(solution)/shard_map/ppermute | solution.py:251
  25.0 3.9 %collective-permute-start.13 = (bf16[2,32,256]{2,1,0:T(8,128)(2,1)S(1)}, bf16[2,32,256]{2,1,0:T(8,128)(2,1)S(1)}, u32[]{:S(2)}, u32[]{:S(2)}) collective-permute-start(bf16[2,32,256]{2,1,0:T(8,128)(2,1)S(1)} %get-tuple-element.84), channel_id=1, source_target_pairs={{0,1},{1,0},{2,3},{3,2},{4,5},{5,4},{6,7},{7,6},{8,9},{9,8},{10,11... | collective-permute-start | bytes 98312 | tf_op jit(solution)/shard_map/ppermute | solution.py:251

commit v7 on v5

--- a/solution.py
+++ b/solution.py
@@ -129,13 +129,28 @@
         out_ref[part, 1] = dv_tall[part * sub : (part + 1) * sub]
 
 
+TARGETS = (
+    ((2, 3, 1, 0), (3, 2, 0, 1), (1, 0, 3, 2)),
+    ((1, 3, 0, 2), (3, 2, 1, 0), (2, 0, 3, 1)),
+)
+
+
+def target(core, lane, h):
+    place = 0
+    for side in range(2):
+        for i in range(GROUP):
+            here = (lane == i) & (core == side)
+            place = jnp.where(here, TARGETS[side][h - 1][i], place)
+    return place
+
+
 def merge_kernel(*refs):
     terms, total_ref, (own_ref, *far_refs) = refs[: -GROUP - 1], refs[-1], refs[-GROUP - 1 : -1]
     total_ref[...] = sum(ref[...].astype(F32) for ref in terms)
-    lane = lax.axis_index("fsdp") % GROUP
+    lane, core = lax.axis_index("fsdp") % GROUP, lax.axis_index("ctx") % 2
     own_ref[...] = total_ref[lane]
     for h in range(1, GROUP):
-        far_refs[h - 1][...] = total_ref[(lane + h) % GROUP].astype(BF16)
+        far_refs[h - 1][...] = total_ref[target(core, lane, h)].astype(BF16)
 
 
 def query_kernel(units, scale, *refs):
@@ -203,8 +218,8 @@
             results[tile] = outs[i :: len(tiles)]
 
     run_tiles([(0, 0), (2, 0)])
-    run_tiles([(r, u) for u in range(1, units) for r in (0, 2)])
-    run_tiles([(r, u) for u in range(units) for r in (1, 3)])
+    run_tiles([(r, u) for u in range(1, units) for r in (0, 2)] + [(1, u) for u in range(units)])
+    run_tiles([(3, u) for u in range(units)])
     (stats,) = call(
         functools.partial(collect_kernel, units),
         [jax.ShapeDtypeStruct((SHARE, 3, unit), F32)],
@@ -237,8 +252,12 @@
     far = [swap(x, step + 1) for step, x in enumerate(far)]
 
     def cross(x, step):
-        pairs = [(i, i // GROUP * GROUP + (i + step) % GROUP) for i in range(lanes)]
-        return lax.ppermute(x, "fsdp", pairs)
+        pairs = [
+            (c * lanes + i, c * lanes + i // GROUP * GROUP + TARGETS[c % 2][step - 1][i % GROUP])
+            for c in range(ctx_size)
+            for i in range(lanes)
+        ]
+        return lax.ppermute(x, ("ctx", "fsdp"), pairs)
 
     own_part, *others_part = call(
         merge_kernel,

time: 30 us -> 29.6 us (0.987)
  starting transfers between devices: 15.7 us -> 14.3 us
  waiting for transfers between devices: 7.31 us -> 8.18 us
    ppermute x3, starting transfers between devices: 5.57 us -> 4.22 us  [cross(): return lax.ppermute(x, ('ctx', 'fsdp'), pairs)]
    ppermute x3, waiting for transfers between devices: 1.88 us -> 2.89 us  [cross(): return lax.ppermute(x, ('ctx', 'fsdp'), pairs)]
  transfers between devices with their start and end apart: 14 -> 14, of which waited for: 7 -> 8; matrix products, arithmetic and copies ran while one was open for 0% -> 0% of each run, Pallas kernels for 11% -> 12%
where the time goes in v7:
time: 29.6 us; the launch traced here: 29.4 us
  starting transfers between devices  14.3 us (48%)
  waiting for transfers between devices  8.18 us (28%)
  Pallas kernels  5.19 us (18%)
  other arithmetic  0.94 us (3%)
  between operations  0.76 us (3%)
    ppermute x11, starting transfers between devices, swap(): return lax.ppermute(x, 'ctx', [(i, i ^ step) for i in range(ctx_size)])  10.1 us
    ppermute x11, waiting for transfers between devices, swap(): return lax.ppermute(x, 'ctx', [(i, i ^ step) for i in range(ctx_size)])  5.3 us
    pallas_call x12, Pallas kernels, call(): pl.pallas_call(kernel, out_shape=out_shape, in_specs=in_specs or [vmem()...  5.19 us
    ppermute x3, starting transfers between devices, cross(): return lax.ppermute(x, ('ctx', 'fsdp'), pairs)  4.22 us
    ppermute x3, waiting for transfers between devices, cross(): return lax.ppermute(x, ('ctx', 'fsdp'), pairs)  2.89 us
    another operation x2, other arithmetic, body(): qg, kv = (jnp.stack([queries, out_grad]), jnp.stack([keys, values]))  0.94 us
  transfers between devices with their start and end apart: 14, of which 8 were waited for; matrix products, arithmetic and copies ran while one was open for 0% of the time, Pallas kernels for 12%

profile of v7, /device:TPU:0, one launch (start us, length us, event | category | flops | bytes accessed | tf_op | source)
XLA Modules:
  0.0 29.4 jit_solution(3197521431288994474)
XLA Ops:
  0.6 0.0 copy-start.2
  0.6 0.0 copy-start.3
  0.7 0.9 %pad_maximum_fusion.refs_2_.refs_4_ = bf16[2,256,128]{2,1,0:T(8,128)(2,1)S(1)} fusion(bf16[1,256,128]{2,1,0:T(8,128)(2,1)} %bitcast.6, bf16[1,256,128]{2,1,0:T(8,128)(2,1)} %bitcast.7), kind=kLoop, calls=%fused_computation | loop fusion | flops 65536 | bytes 262144 | tf_op jit(solution)/shard_map/stack | solution.py:193
  1.6 3.0 %collective-permute-start = (bf16[2,256,128]{2,1,0:T(8,128)(2,1)S(1)}, bf16[2,256,128]{2,1,0:T(8,128)(2,1)S(1)}, u32[]{:S(2)}, u32[]{:S(2)}) collective-permute-start(bf16[2,256,128]{2,1,0:T(8,128)(2,1)S(1)} %pad_maximum_fusion.refs_2_.refs_4_), channel_id=1, source_target_pairs={{0,8},{4,12},{8,0},{12,4},{16,24},{20,28},{24,16},{28,20},{1,9},{5... | collective-permute-start | bytes 393224 | tf_op jit(solution)/shard_map/ppermute | solution.py:191
  4.6 0.0 copy-done.2
  4.6 0.0 copy-done.3
  4.6 0.0 copy-start
  4.6 0.0 copy-start.1
  4.6 1.6 %collective-permute-start.2 = (bf16[2,256,128]{2,1,0:T(8,128)(2,1)S(1)}, bf16[2,256,128]{2,1,0:T(8,128)(2,1)S(1)}, u32[]{:S(2)}, u32[]{:S(2)}) collective-permute-start(bf16[2,256,128]{2,1,0:T(8,128)(2,1)S(1)} %pad_maximum_fusion.1.refs_4_.refs_5_.refs_10_.refs_2_), channel_id=1, source_target_pairs={{0,16},{4,20},{8,24},{12,28},{16,0},{20,4},{24,8},{28,12},{1,17},{... | collective-permute-start | bytes 393224 | tf_op jit(solution)/shard_map/ppermute | solution.py:191
  6.2 0.0 collective-permute-start.1
  6.2 0.0 copy-done
  6.2 0.0 copy-done.1
  6.2 0.8 %shard_map.85 = (s32[4,256]{1,0:T(4,128)S(1)}, s32[4,256]{1,0:T(4,128)S(1)}, s32[4,256]{1,0:T(4,128)S(1)}, s32[4,256]{1,0:T(4,128)S(1)}) custom-call(s32[16]{0:T(128)S(1)} %copy-done.1, s32[16,16]{1,0:T(8,128)S(1)} %copy-done), custom_call_target="tpu_custom_call" | custom-call | bytes 17472 | tf_op jit(solution)/shard_map/pallas_call | solution.py:33
  7.0 1.1 %collective-permute-done.refs_3_.refs_5_.in_ref.refs_6_ = bf16[2,256,128]{2,1,0:T(8,128)(2,1)S(1)} collective-permute-done((bf16[2,256,128]{2,1,0:T(8,128)(2,1)S(1)}, bf16[2,256,128]{2,1,0:T(8,128)(2,1)S(1)}, u32[]{:S(2)}, u32[]{:S(2)}) %collective-permute-start) | collective-permute-done | bytes 131104 | tf_op jit(solution)/shard_map/ppermute | solution.py:191
  8.1 0.1 collective-permute-start.3
  8.2 0.4 %shard_map.86 = (f32[256,256]{1,0:T(8,128)S(1)}, f32[256,256]{1,0:T(8,128)S(1)}, f32[256,256]{1,0:T(8,128)S(1)}, f32[256,256]{1,0:T(8,128)S(1)}, f32[3,256]{1,0:T(4,128)S(1)}, /*index=5*/f32[3,256]{1,0:T(4,128)S(1)}) custom-call(s32[4,256]{1,0:T(4,128)S(1)} %get-tuple-element.45.refs_0_.after_ref, s32[4,256]{1,0:T(4,128)S(1)} %get-tuple-element.46.refs_1_, ...), custom_call_target="tpu_custom_call" | custom-call | flops 67108864 | bytes 1587200 | tf_op jit(solution)/shard_map/pallas_call | solution.py:33
  8.6 1.1 %collective-permute-done.2.refs_8_.refs_9_.refs_11_.refs_5_.refs_3_ = bf16[2,256,128]{2,1,0:T(8,128)(2,1)S(1)} collective-permute-done((bf16[2,256,128]{2,1,0:T(8,128)(2,1)S(1)}, bf16[2,256,128]{2,1,0:T(8,128)(2,1)S(1)}, u32[]{:S(2)}, u32[]{:S(2)}) %collective-permute-start.2) | collective-permute-done | bytes 131104 | tf_op jit(solution)/shard_map/ppermute | solution.py:191
  9.6 0.0 collective-permute-done.1.refs_6_.refs_7_.refs_5_
  9.7 0.6 %shard_map.87 = (f32[256,256]{1,0:T(8,128)S(1)}, f32[256,256]{1,0:T(8,128)S(1)}, f32[256,256]{1,0:T(8,128)S(1)}, f32[256,256]{1,0:T(8,128)S(1)}, f32[256,256]{1,...) custom-call(s32[4,256]{1,0:T(4,128)S(1)} %get-tuple-element.45.refs_, ...), custom_call_target="tpu_custom_call" | custom-call | flops 134217728 | bytes 3174400 | tf_op jit(solution)/shard_map/pallas_call | solution.py:33
  10.3 0.0 collective-permute-done.3.refs_2_.refs_3_.refs_7_
  10.3 0.4 %shard_map.89 = (f32[256,256]{1,0:T(8,128)S(1)}, f32[256,256]{1,0:T(8,128)S(1)}, f32[256,256]{1,0:T(8,128)S(1)}, f32[256,256]{1,0:T(8,128)S(1)}, f32[3,256]{1,0:T(4,128)S(1)}, /*index=5*/f32[3,256]{1,0:T(4,128)S(1)}) custom-call(s32[4,256]{1,0:T(4,128)S(1)} %get-tuple-element.54.refs_0_.refs_1_, s32[4,256]{1,0:T(4,128)S(1)} %get-tuple-element.54.refs_0_.refs_1_, ...), custom_call_target="tpu_custom_call" | custom-call | flops 67108864 | bytes 1587200 | tf_op jit(solution)/shard_map/pallas_call | solution.py:33
  10.7 0.9 %collective-permute-start.6 = (f32[4,3,256]{2,1,0:T(4,128)S(1)}, f32[4,3,256]{2,1,0:T(4,128)S(1)}, u32[]{:S(2)}, u32[]{:S(2)}) collective-permute-start(f32[4,3,256]{2,1,0:T(4,128)S(1)} %shard_map.90.refs_0_), channel_id=1, source_target_pairs={{0,12},{4,8},{8,4},{12,0},{16,28},{20,24},{24,20},{28,16},{1,13},{... | collective-permute-start | bytes 36872 | tf_op jit(solution)/shard_map/ppermute | solution.py:191
  11.6 0.3 collective-permute-start.5
  11.8 0.8 %collective-permute-start.4 = (f32[4,3,256]{2,1,0:T(4,128)S(1)}, f32[4,3,256]{2,1,0:T(4,128)S(1)}, u32[]{:S(2)}, u32[]{:S(2)}) collective-permute-start(f32[4,3,256]{2,1,0:T(4,128)S(1)} %shard_map.90.refs_0_), channel_id=1, source_target_pairs={{0,4},{4,0},{8,12},{12,8},{16,20},{20,16},{24,28},{28,24},{1,5},{5... | collective-permute-start | bytes 36872 | tf_op jit(solution)/shard_map/ppermute | solution.py:191
  12.6 1.3 %collective-permute-done.6.refs_3_ = f32[4,3,256]{2,1,0:T(4,128)S(1)} collective-permute-done((f32[4,3,256]{2,1,0:T(4,128)S(1)}, f32[4,3,256]{2,1,0:T(4,128)S(1)}, u32[]{:S(2)}, u32[]{:S(2)}) %collective-permute-start.6) | collective-permute-done | bytes 12320 | tf_op jit(solution)/shard_map/ppermute | solution.py:191
  13.9 1.4 %collective-permute-done.5.refs_2_ = f32[4,3,256]{2,1,0:T(4,128)S(1)} collective-permute-done((f32[4,3,256]{2,1,0:T(4,128)S(1)}, f32[4,3,256]{2,1,0:T(4,128)S(1)}, u32[]{:S(2)}, u32[]{:S(2)}) %collective-permute-start.5) | collective-permute-done | bytes 12320 | tf_op jit(solution)/shard_map/ppermute | solution.py:191
  15.3 0.0 collective-permute-done.4.refs_1_
  15.3 0.6 %shard_map.92 = (bf16[256,1024]{1,0:T(8,128)(2,1)S(1)}, bf16[4,2,32,256]{3,2,1,0:T(8,128)(2,1)S(1)}) custom-call(f32[4,3,256]{2,1,0:T(4,128)S(1)} %shard_map.90.refs_0_, f32[4,3,256]{2,1,0:T(4,128)S(1)} %collective-permute-done.4.refs_1_, f32[4,3,256]{2,1,0:T(4,128)S(1)} %collective-permute-done.5.refs_2_, f32[4,3,256]{2,1,0:T(4,128)S(1)} %collective-permute-done.6.refs_3_, ...), custom_call_target="tpu_custom_call" | custom-call | flops 134217728 | bytes 3338240 | tf_op jit(solution)/shard_map/pallas_call | solution.py:33
  15.9 1.6 %collective-permute-start.10 = (bf16[4,2,32,256]{3,2,1,0:T(8,128)(2,1)S(1)}, bf16[4,2,32,256]{3,2,1,0:T(8,128)(2,1)S(1)}, u32[]{:S(2)}, u32[]{:S(2)}) collective-permute-start(bf16[4,2,32,256]{3,2,1,0:T(8,128)(2,1)S(1)} %get-tuple-element.80), channel_id=1, source_target_pairs={{0,16},{4,20},{8,24},{12,28},{16,0},{20,4},{24,8},{28,12},{1,17},{... | collective-permute-start | bytes 393224 | tf_op jit(solution)/shard_map/ppermute | solution.py:191
  17.5 0.6 %shard_map.91 = (bf16[256,1024]{1,0:T(8,128)(2,1)S(1)}, f32[4,2,32,256]{3,2,1,0:T(8,128)S(1)}) custom-call(f32[4,3,256]{2,1,0:T(4,128)S(1)} %shard_map.90.refs_0_, f32[4,3,256]{2,1,0:T(4,128)S(1)} %collective-permute-done.4.refs_1_, f32[4,3,256]{2,1,0:T(4,128)S(1)} %collective-permute-done.5.refs_2_, f32[4,3,256]{2,1,0:T(4,128)S(1)} %collective-permute-done.6.refs_3_, ...), custom_call_target="tpu_custom_call" | custom-call | flops 134217728 | bytes 3469312 | tf_op jit(solution)/shard_map/pallas_call | solution.py:33
  18.1 0.4 %shard_map.93 = (f32[256,128]{1,0:T(8,128)S(1)}, bf16[256,128]{1,0:T(8,128)(2,1)S(1)}, bf16[256,128]{1,0:T(8,128)(2,1)S(1)}, bf16[256,128]{1,0:T(8,128)(2,1)S(1)}) custom-call(bf16[256,1024]{1,0:T(8,128)(2,1)S(1)} %get-tuple-element.65.refs_0_, bf16[256,1024]{1,0:T(8,128)(2,1)S(1)} %get-tuple-element.74.refs_1_, ...), custom_call_target="tpu_custom_call" | custom-call | flops 134217728 | bytes 1638400 | tf_op jit(solution)/shard_map/pallas_call | solution.py:33
  18.5 0.1 collective-permute-start.7
  18.6 0.6 %collective-permute-start.8 = (bf16[256,128]{1,0:T(8,128)(2,1)S(1)}, bf16[256,128]{1,0:T(8,128)(2,1)S(1)}, u32[]{:S(2)}, u32[]{:S(2)}) collective-permute-start(bf16[256,128]{1,0:T(8,128)(2,1)S(1)} %get-tuple-element.77), channel_id=1, source_target_pairs={{0,8},{4,12},{8,0},{12,4},{16,24},{20,28},{24,16},{28,20},{1,9},{5... | collective-permute-start | bytes 196616 | tf_op jit(solution)/shard_map/ppermute | solution.py:191
  19.2 1.2 %collective-permute-start.9 = (bf16[256,128]{1,0:T(8,128)(2,1)S(1)}, bf16[256,128]{1,0:T(8,128)(2,1)S(1)}, u32[]{:S(2)}, u32[]{:S(2)}) collective-permute-start(bf16[256,128]{1,0:T(8,128)(2,1)S(1)} %get-tuple-element.78), channel_id=1, source_target_pairs={{0,12},{4,8},{8,4},{12,0},{16,28},{20,24},{24,20},{28,16},{1,13},{... | collective-permute-start | bytes 196616 | tf_op jit(solution)/shard_map/ppermute | solution.py:191
  20.4 0.5 %collective-permute-done.10.refs_1_ = bf16[4,2,32,256]{3,2,1,0:T(8,128)(2,1)S(1)} collective-permute-done((bf16[4,2,32,256]{3,2,1,0:T(8,128)(2,1)S(1)}, bf16[4,2,32,256]{3,2,1,0:T(8,128)(2,1)S(1)}, u32[]{:S(2)}, u32[]{:S(2)}) %collective-permute-start.10) | collective-permute-done | bytes 131104 | tf_op jit(solution)/shard_map/ppermute | solution.py:191
  21.0 2.6 %collective-permute-start.11 = (bf16[2,32,256]{2,1,0:T(8,128)(2,1)S(1)}, bf16[2,32,256]{2,1,0:T(8,128)(2,1)S(1)}, u32[]{:S(2)}, u32[]{:S(2)}) collective-permute-start(bf16[2,32,256]{2,1,0:T(8,128)(2,1)S(1)} %get-tuple-element.82), channel_id=1, source_target_pairs={{0,2},{1,3},{2,1},{3,0},{4,5},{5,7},{6,4},{7,6},{8,10},{9,11},{10,... | collective-permute-start | bytes 98312 | tf_op jit(solution)/shard_map/ppermute | solution.py:260
  23.6 1.2 %collective-permute-start.12 = (bf16[2,32,256]{2,1,0:T(8,128)(2,1)S(1)}, bf16[2,32,256]{2,1,0:T(8,128)(2,1)S(1)}, u32[]{:S(2)}, u32[]{:S(2)}) collective-permute-start(bf16[2,32,256]{2,1,0:T(8,128)(2,1)S(1)} %get-tuple-element.83), channel_id=1, source_target_pairs={{0,3},{1,2},{2,0},{3,1},{4,7},{5,6},{6,5},{7,4},{8,11},{9,10},{10,... | collective-permute-start | bytes 98312 | tf_op jit(solution)/shard_map/ppermute | solution.py:260
  24.8 0.0 collective-permute-done.7.refs_1_
  24.8 0.3 %collective-permute-start.13 = (bf16[2,32,256]{2,1,0:T(8,128)(2,1)S(1)}, bf16[2,32,256]{2,1,0:T(8,128)(2,1)S(1)}, u32[]{:S(2)}, u32[]{:S(2)}) collective-permute-start(bf16[2,32,256]{2,1,0:T(8,128)(2,1)S(1)} %get-tuple-element.84), channel_id=1, source_target_pairs={{0,1},{1,0},{2,3},{3,2},{4,6},{5,4},{6,7},{7,5},{8,9},{9,8},{10,11... | collective-permute-start | bytes 98312 | tf_op jit(solution)/shard_map/ppermute | solution.py:260
  25.2 0.0 collective-permute-done.8.refs_2_
  25.2 0.0 collective-permute-done.9.refs_3_
  25.2 0.7 %shard_map.94 = f32[256,128]{1,0:T(8,128)} custom-call(f32[256,128]{1,0:T(8,128)S(1)} %get-tuple-element.75.refs_0_, bf16[256,128]{1,0:T(8,128)(2,1)S(1)} %collective-permute-done.7.refs_1_, bf16[256,128]{1,0:T(8,128)(2,1)S(1)} %collective-permute-done.8.refs_2_, bf16[256,128]{1,0:T(8,128)(2,1)S(1)} %collective-permute-done.9.refs_3_), custom_call_target="tpu_custom_call" | custom-call | bytes 458752 | tf_op jit(solution)/shard_map/pallas_call | solution.py:33
  25.9 1.0 %collective-permute-done.11.refs_1_ = bf16[2,32,256]{2,1,0:T(8,128)(2,1)S(1)} collective-permute-done((bf16[2,32,256]{2,1,0:T(8,128)(2,1)S(1)}, bf16[2,32,256]{2,1,0:T(8,128)(2,1)S(1)}, u32[]{:S(2)}, u32[]{:S(2)}) %collective-permute-start.11) | collective-permute-done | bytes 32800 | tf_op jit(solution)/shard_map/ppermute | solution.py:260
  26.9 1.5 %collective-permute-done.12.refs_2_ = bf16[2,32,256]{2,1,0:T(8,128)(2,1)S(1)} collective-permute-done((bf16[2,32,256]{2,1,0:T(8,128)(2,1)S(1)}, bf16[2,32,256]{2,1,0:T(8,128)(2,1)S(1)}, u32[]{:S(2)}, u32[]{:S(2)}) %collective-permute-start.12) | collective-permute-done | bytes 32800 | tf_op jit(solution)/shard_map/ppermute | solution.py:260
  28.4 0.4 %collective-permute-done.13.refs_3_ = bf16[2,32,256]{2,1,0:T(8,128)(2,1)S(1)} collective-permute-done((bf16[2,32,256]{2,1,0:T(8,128)(2,1)S(1)}, bf16[2,32,256]{2,1,0:T(8,128)(2,1)S(1)}, u32[]{:S(2)}, u32[]{:S(2)}) %collective-permute-start.13) | collective-permute-done | bytes 32800 | tf_op jit(solution)/shard_map/ppermute | solution.py:260
  28.8 0.6 %shard_map.96 = (f32[32,256]{1,0:T(8,128)}, f32[32,256]{1,0:T(8,128)}) custom-call(f32[2,32,256]{2,1,0:T(8,128)S(1)} %get-tuple-element.81.refs_0_, bf16[2,32,256]{2,1,0:T(8,128)(2,1)S(1)} %collective-permute-done.11.refs_1_, bf16[2,32,256]{2,1,0:T(8,128)(2,1)S(1)} %collective-permute-done.12.refs_2_, bf16[2,32,256]{2,1,0:T(8,128)(2,1)S(1)} %collective-permute-done.13.refs_3_), custom_call_target="tpu_custom_call" | custom-call | bytes 229376 | tf_op jit(solution)/shard_map/pallas_call | solution.py:33
  (4 shorter events, 0.1 us)
Async XLA Ops:
  0.6 3.9 %copy-start.2 = (bf16[256,128]{1,0:T(8,128)(2,1)S(1)}, bf16[256,128]{1,0:T(8,128)(2,1)}, u32[]{:S(2)}) copy-start(bf16[256,128]{1,0:T(8,128)(2,1)} %param.8) | copy-start | bytes 196612
  0.6 3.9 %copy-start.3 = (bf16[256,128]{1,0:T(8,128)(2,1)S(1)}, bf16[256,128]{1,0:T(8,128)(2,1)}, u32[]{:S(2)}) copy-start(bf16[256,128]{1,0:T(8,128)(2,1)} %param.7) | copy-start | bytes 196612
  1.6 6.5 %collective-permute-start = (bf16[2,256,128]{2,1,0:T(8,128)(2,1)S(1)}, bf16[2,256,128]{2,1,0:T(8,128)(2,1)S(1)}, u32[]{:S(2)}, u32[]{:S(2)}) collective-permute-start(bf16[2,256,128]{2,1,0:T(8,128)(2,1)S(1)} %pad_maximum_fusion.refs_2_.refs_4_), channel_id=1, source_target_pairs={{0,8},{4,12},{8,0},{12,4},{16,24},{20,28},{24,16},{28,20},{1,9},{5... | collective-permute-start | bytes 393224 | tf_op jit(solution)/shard_map/ppermute | solution.py:191
  4.6 1.6 %copy-start = (s32[16,16]{1,0:T(8,128)S(1)}, s32[16,16]{1,0:T(8,128)}, u32[]{:S(2)}) copy-start(s32[16,16]{1,0:T(8,128)} %mask_ref.1) | copy-start | bytes 3076
  4.6 1.6 %copy-start.1 = (s32[16]{0:T(128)S(1)}, s32[16]{0:T(128)}, u32[]{:S(2)}) copy-start(s32[16]{0:T(128)} %ids_ref.1) | copy-start | bytes 196
  4.6 5.0 %collective-permute-start.2 = (bf16[2,256,128]{2,1,0:T(8,128)(2,1)S(1)}, bf16[2,256,128]{2,1,0:T(8,128)(2,1)S(1)}, u32[]{:S(2)}, u32[]{:S(2)}) collective-permute-start(bf16[2,256,128]{2,1,0:T(8,128)(2,1)S(1)} %pad_maximum_fusion.1.refs_4_.refs_5_.refs_10_.refs_2_), channel_id=1, source_target_pairs={{0,16},{4,20},{8,24},{12,28},{16,0},{20,4},{24,8},{28,12},{1,17},{... | collective-permute-start | bytes 393224 | tf_op jit(solution)/shard_map/ppermute | solution.py:191
  6.2 3.5 %collective-permute-start.1 = (bf16[2,256,128]{2,1,0:T(8,128)(2,1)S(1)}, bf16[2,256,128]{2,1,0:T(8,128)(2,1)S(1)}, u32[]{:S(2)}, u32[]{:S(2)}) collective-permute-start(bf16[2,256,128]{2,1,0:T(8,128)(2,1)S(1)} %pad_maximum_fusion.refs_2_.refs_4_), channel_id=1, source_target_pairs={{0,4},{4,0},{8,12},{12,8},{16,20},{20,16},{24,28},{28,24},{1,5},{5... | collective-permute-start | bytes 393224 | tf_op jit(solution)/shard_map/ppermute | solution.py:191
  8.1 2.2 %collective-permute-start.3 = (bf16[2,256,128]{2,1,0:T(8,128)(2,1)S(1)}, bf16[2,256,128]{2,1,0:T(8,128)(2,1)S(1)}, u32[]{:S(2)}, u32[]{:S(2)}) collective-permute-start(bf16[2,256,128]{2,1,0:T(8,128)(2,1)S(1)} %shard_map.88), channel_id=1, source_target_pairs={{0,4},{4,0},{8,12},{12,8},{16,20},{20,16},{24,28},{28,24},{1,5},{5... | collective-permute-start | bytes 393224 | tf_op jit(solution)/shard_map/ppermute | solution.py:191
  10.7 3.2 %collective-permute-start.6 = (f32[4,3,256]{2,1,0:T(4,128)S(1)}, f32[4,3,256]{2,1,0:T(4,128)S(1)}, u32[]{:S(2)}, u32[]{:S(2)}) collective-permute-start(f32[4,3,256]{2,1,0:T(4,128)S(1)} %shard_map.90.refs_0_), channel_id=1, source_target_pairs={{0,12},{4,8},{8,4},{12,0},{16,28},{20,24},{24,20},{28,16},{1,13},{... | collective-permute-start | bytes 36872 | tf_op jit(solution)/shard_map/ppermute | solution.py:191
  11.6 3.7 %collective-permute-start.5 = (f32[4,3,256]{2,1,0:T(4,128)S(1)}, f32[4,3,256]{2,1,0:T(4,128)S(1)}, u32[]{:S(2)}, u32[]{:S(2)}) collective-permute-start(f32[4,3,256]{2,1,0:T(4,128)S(1)} %shard_map.90.refs_0_), channel_id=1, source_target_pairs={{0,8},{4,12},{8,0},{12,4},{16,24},{20,28},{24,16},{28,20},{1,9},{5... | collective-permute-start | bytes 36872 | tf_op jit(solution)/shard_map/ppermute | solution.py:191
  11.8 3.5 %collective-permute-start.4 = (f32[4,3,256]{2,1,0:T(4,128)S(1)}, f32[4,3,256]{2,1,0:T(4,128)S(1)}, u32[]{:S(2)}, u32[]{:S(2)}) collective-permute-start(f32[4,3,256]{2,1,0:T(4,128)S(1)} %shard_map.90.refs_0_), channel_id=1, source_target_pairs={{0,4},{4,0},{8,12},{12,8},{16,20},{20,16},{24,28},{28,24},{1,5},{5... | collective-permute-start | bytes 36872 | tf_op jit(solution)/shard_map/ppermute | solution.py:191
  15.9 5.0 %collective-permute-start.10 = (bf16[4,2,32,256]{3,2,1,0:T(8,128)(2,1)S(1)}, bf16[4,2,32,256]{3,2,1,0:T(8,128)(2,1)S(1)}, u32[]{:S(2)}, u32[]{:S(2)}) collective-permute-start(bf16[4,2,32,256]{3,2,1,0:T(8,128)(2,1)S(1)} %get-tuple-element.80), channel_id=1, source_target_pairs={{0,16},{4,20},{8,24},{12,28},{16,0},{20,4},{24,8},{28,12},{1,17},{... | collective-permute-start | bytes 393224 | tf_op jit(solution)/shard_map/ppermute | solution.py:191
  18.5 6.3 %collective-permute-start.7 = (bf16[256,128]{1,0:T(8,128)(2,1)S(1)}, bf16[256,128]{1,0:T(8,128)(2,1)S(1)}, u32[]{:S(2)}, u32[]{:S(2)}) collective-permute-start(bf16[256,128]{1,0:T(8,128)(2,1)S(1)} %get-tuple-element.76), channel_id=1, source_target_pairs={{0,4},{4,0},{8,12},{12,8},{16,20},{20,16},{24,28},{28,24},{1,5},{5... | collective-permute-start | bytes 196616 | tf_op jit(solution)/shard_map/ppermute | solution.py:191
  18.6 6.6 %collective-permute-start.8 = (bf16[256,128]{1,0:T(8,128)(2,1)S(1)}, bf16[256,128]{1,0:T(8,128)(2,1)S(1)}, u32[]{:S(2)}, u32[]{:S(2)}) collective-permute-start(bf16[256,128]{1,0:T(8,128)(2,1)S(1)} %get-tuple-element.77), channel_id=1, source_target_pairs={{0,8},{4,12},{8,0},{12,4},{16,24},{20,28},{24,16},{28,20},{1,9},{5... | collective-permute-start | bytes 196616 | tf_op jit(solution)/shard_map/ppermute | solution.py:191
  19.2 6.0 %collective-permute-start.9 = (bf16[256,128]{1,0:T(8,128)(2,1)S(1)}, bf16[256,128]{1,0:T(8,128)(2,1)S(1)}, u32[]{:S(2)}, u32[]{:S(2)}) collective-permute-start(bf16[256,128]{1,0:T(8,128)(2,1)S(1)} %get-tuple-element.78), channel_id=1, source_target_pairs={{0,12},{4,8},{8,4},{12,0},{16,28},{20,24},{24,20},{28,16},{1,13},{... | collective-permute-start | bytes 196616 | tf_op jit(solution)/shard_map/ppermute | solution.py:191
  21.0 5.9 %collective-permute-start.11 = (bf16[2,32,256]{2,1,0:T(8,128)(2,1)S(1)}, bf16[2,32,256]{2,1,0:T(8,128)(2,1)S(1)}, u32[]{:S(2)}, u32[]{:S(2)}) collective-permute-start(bf16[2,32,256]{2,1,0:T(8,128)(2,1)S(1)} %get-tuple-element.82), channel_id=1, source_target_pairs={{0,2},{1,3},{2,1},{3,0},{4,5},{5,7},{6,4},{7,6},{8,10},{9,11},{10,... | collective-permute-start | bytes 98312 | tf_op jit(solution)/shard_map/ppermute | solution.py:260
  23.6 4.8 %collective-permute-start.12 = (bf16[2,32,256]{2,1,0:T(8,128)(2,1)S(1)}, bf16[2,32,256]{2,1,0:T(8,128)(2,1)S(1)}, u32[]{:S(2)}, u32[]{:S(2)}) collective-permute-start(bf16[2,32,256]{2,1,0:T(8,128)(2,1)S(1)} %get-tuple-element.83), channel_id=1, source_target_pairs={{0,3},{1,2},{2,0},{3,1},{4,7},{5,6},{6,5},{7,4},{8,11},{9,10},{10,... | collective-permute-start | bytes 98312 | tf_op jit(solution)/shard_map/ppermute | solution.py:260
  24.8 3.9 %collective-permute-start.13 = (bf16[2,32,256]{2,1,0:T(8,128)(2,1)S(1)}, bf16[2,32,256]{2,1,0:T(8,128)(2,1)S(1)}, u32[]{:S(2)}, u32[]{:S(2)}) collective-permute-start(bf16[2,32,256]{2,1,0:T(8,128)(2,1)S(1)} %get-tuple-element.84), channel_id=1, source_target_pairs={{0,1},{1,0},{2,3},{3,2},{4,6},{5,4},{6,7},{7,5},{8,9},{9,8},{10,11... | collective-permute-start | bytes 98312 | tf_op jit(solution)/shard_map/ppermute | solution.py:260

commit v8 on v7

--- a/solution.py
+++ b/solution.py
@@ -79,14 +79,14 @@
             ],
             axis=0,
         )
-        top = jnp.maximum(jnp.max(scores, axis=0, keepdims=True), FLOOR)
-        weights = jnp.exp2(scores - top)
+        top = jnp.maximum(jnp.max(scores.reshape(-1, 8, unit), axis=0), FLOOR)
+        weights = jnp.exp2(scores.reshape(-1, 8, unit) - top)
         dprobs = dot(kv_refs[i][1], qg_refs[i][1], 1, 1)
-        exp_refs[i][...] = weights
+        exp_refs[i][...] = weights.reshape(unit, unit)
         dprob_refs[i][...] = dprobs
-        stats_refs[i][0:1, :] = top
-        stats_refs[i][1:2, :] = jnp.sum(weights, axis=0, keepdims=True)
-        stats_refs[i][2:3, :] = jnp.sum(weights * dprobs, axis=0, keepdims=True)
+        stats_refs[i][0] = top
+        stats_refs[i][1] = jnp.sum(weights, axis=0)
+        stats_refs[i][2] = jnp.sum(weights * dprobs.reshape(-1, 8, unit), axis=0)
 
 
 def merge_stats(left, right):
@@ -100,8 +100,23 @@
 
 def collect_kernel(units, *refs):
     for r in range(SHARE):
-        stats = functools.reduce(merge_stats, [refs[r * units + u][...] for u in range(units)])
-        refs[-1][r] = stats
+        parts = [refs[r * units + u] for u in range(units)]
+        tops = functools.reduce(jnp.maximum, [ref[0] for ref in parts])
+        top = jnp.max(tops, axis=0, keepdims=True)
+        factors = [jnp.exp2(ref[0] - top) for ref in parts]
+        refs[-1][r, 0:1, :] = top
+        for row in (1, 2):
+            total = sum(ref[row] * factor for ref, factor in zip(parts, factors))
+            refs[-1][r, row : row + 1, :] = jnp.sum(total, axis=0, keepdims=True)
+
+
+def last_tiles_kernel(tiles, others, factor, units, *refs):
+    count = len(tiles)
+    ins, refs = refs[: 3 * count], refs[3 * count :]
+    other_refs, outs, collected_ref = refs[: len(others)], refs[len(others) : -1], refs[-1]
+    tile_kernel(tiles, factor, *ins, *outs)
+    stats = dict(zip(others, other_refs)) | dict(zip(tiles, outs[2 * count :]))
+    collect_kernel(units, *[stats[r, u] for r in range(SHARE) for u in range(units)], collected_ref)
 
 
 def grads_kernel(scale, *refs):
@@ -114,9 +129,9 @@
     dk, dv = 0.0, 0.0
     for r in range(SHARE):
         whole = functools.reduce(merge_stats, [all_refs[s][r ^ s] for s in range(SHARE)])
-        share = jnp.exp2(stats_refs[r][0:1] - whole[0:1]) / whole[1:2]
+        share = jnp.exp2(stats_refs[r][0] - whole[0:1]) / whole[1:2]
         delta = whole[2:3] / whole[1:2]
-        probs = exp_refs[r][...] * share
+        probs = (exp_refs[r][...].reshape(-1, 8, unit) * share).reshape(unit, unit)
         dprobs = dprob_refs[r][...]
         dscores = (probs * (dprobs - delta)).astype(BF16)
         ds_ref[:, r * unit : (r + 1) * unit] = dscores
@@ -204,7 +219,7 @@
 
     product = 2 * unit * unit * width
     grid = jax.ShapeDtypeStruct((unit, unit), F32)
-    rows_out = jax.ShapeDtypeStruct((3, unit), F32)
+    rows_out = jax.ShapeDtypeStruct((3, 8, unit), F32)
     results = {}
 
     def run_tiles(tiles):
@@ -219,12 +234,20 @@
 
     run_tiles([(0, 0), (2, 0)])
     run_tiles([(r, u) for u in range(1, units) for r in (0, 2)] + [(1, u) for u in range(units)])
-    run_tiles([(3, u) for u in range(units)])
-    (stats,) = call(
-        functools.partial(collect_kernel, units),
-        [jax.ShapeDtypeStruct((SHARE, 3, unit), F32)],
-        [results[r, u][2] for r in range(SHARE) for u in range(units)],
-    )
+    last, others = [(3, u) for u in range(units)], list(results)
+    *outs, stats = call(
+        functools.partial(last_tiles_kernel, last, others, factor, units),
+        [grid] * (2 * len(last))
+        + [rows_out] * len(last)
+        + [jax.ShapeDtypeStruct((SHARE, 3, unit), F32)],
+        [limits[r] for r, _ in last]
+        + [qgs[r] for r, _ in last]
+        + [kvs[u] for _, u in last]
+        + [results[tile][2] for tile in others],
+        flops=2 * product * len(last),
+    )
+    for i, tile in enumerate(last):
+        results[tile] = outs[i :: len(last)]
     came = {step: swap(stats, step) for step in (3, 2, 1)}
     both_stats = [stats] + [came[step] for step in range(1, SHARE)]
 

time: 29.6 us -> 29.5 us (level)
    pallas_call x12 -> x11, Pallas kernels: 5.19 us -> 5.12 us  [call(): pl.pallas_call(kernel, out_shape=out_shape, in_specs=in_specs or [vmem()...]
where the time goes in v8:
time: 29.5 us; the launch traced here: 29.4 us
  starting transfers between devices  14.3 us (48%)
  waiting for transfers between devices  8.19 us (28%)
  Pallas kernels  5.12 us (17%)
  other arithmetic  0.94 us (3%)
  between operations  0.76 us (3%)
    ppermute x11, starting transfers between devices, swap(): return lax.ppermute(x, 'ctx', [(i, i ^ step) for i in range(ctx_size)])  10.1 us
    ppermute x11, waiting for transfers between devices, swap(): return lax.ppermute(x, 'ctx', [(i, i ^ step) for i in range(ctx_size)])  5.3 us
    pallas_call x11, Pallas kernels, call(): pl.pallas_call(kernel, out_shape=out_shape, in_specs=in_specs or [vmem()...  5.12 us
    ppermute x3, starting transfers between devices, cross(): return lax.ppermute(x, ('ctx', 'fsdp'), pairs)  4.22 us
    ppermute x3, waiting for transfers between devices, cross(): return lax.ppermute(x, ('ctx', 'fsdp'), pairs)  2.89 us
    another operation x2, other arithmetic, body(): qg, kv = (jnp.stack([queries, out_grad]), jnp.stack([keys, values]))  0.94 us
  transfers between devices with their start and end apart: 14, of which 8 were waited for; matrix products, arithmetic and copies ran while one was open for 0% of the time, Pallas kernels for 12%

profile of v8, /device:TPU:0, one launch (start us, length us, event | category | flops | bytes accessed | tf_op | source)
XLA Modules:
  0.0 29.4 jit_solution(12947901280427408779)
XLA Ops:
  0.6 0.0 copy-start.2
  0.6 0.0 copy-start.3
  0.7 0.9 %pad_maximum_fusion.refs_2_.refs_4_ = bf16[2,256,128]{2,1,0:T(8,128)(2,1)S(1)} fusion(bf16[1,256,128]{2,1,0:T(8,128)(2,1)} %bitcast.6, bf16[1,256,128]{2,1,0:T(8,128)(2,1)} %bitcast.7), kind=kLoop, calls=%fused_computation | loop fusion | flops 65536 | bytes 262144 | tf_op jit(solution)/shard_map/stack | solution.py:208
  1.6 3.0 %collective-permute-start = (bf16[2,256,128]{2,1,0:T(8,128)(2,1)S(1)}, bf16[2,256,128]{2,1,0:T(8,128)(2,1)S(1)}, u32[]{:S(2)}, u32[]{:S(2)}) collective-permute-start(bf16[2,256,128]{2,1,0:T(8,128)(2,1)S(1)} %pad_maximum_fusion.refs_2_.refs_4_), channel_id=1, source_target_pairs={{0,8},{4,12},{8,0},{12,4},{16,24},{20,28},{24,16},{28,20},{1,9},{5... | collective-permute-start | bytes 393224 | tf_op jit(solution)/shard_map/ppermute | solution.py:206
  4.6 0.0 copy-done.2
  4.6 0.0 copy-done.3
  4.6 0.0 copy-start
  4.6 0.0 copy-start.1
  4.6 1.6 %collective-permute-start.2 = (bf16[2,256,128]{2,1,0:T(8,128)(2,1)S(1)}, bf16[2,256,128]{2,1,0:T(8,128)(2,1)S(1)}, u32[]{:S(2)}, u32[]{:S(2)}) collective-permute-start(bf16[2,256,128]{2,1,0:T(8,128)(2,1)S(1)} %pad_maximum_fusion.1.refs_4_.refs_5_.refs_10_.refs_2_), channel_id=1, source_target_pairs={{0,16},{4,20},{8,24},{12,28},{16,0},{20,4},{24,8},{28,12},{1,17},{... | collective-permute-start | bytes 393224 | tf_op jit(solution)/shard_map/ppermute | solution.py:206
  6.2 0.0 collective-permute-start.3
  6.2 0.0 copy-done
  6.2 0.0 copy-done.1
  6.2 0.8 %shard_map.85 = (s32[4,256]{1,0:T(4,128)S(1)}, s32[4,256]{1,0:T(4,128)S(1)}, s32[4,256]{1,0:T(4,128)S(1)}, s32[4,256]{1,0:T(4,128)S(1)}) custom-call(s32[16]{0:T(128)S(1)} %copy-done.1, s32[16,16]{1,0:T(8,128)S(1)} %copy-done), custom_call_target="tpu_custom_call" | custom-call | bytes 17472 | tf_op jit(solution)/shard_map/pallas_call | solution.py:33
  7.0 1.1 %collective-permute-done.in_ref.refs_3_.refs_5_.refs_6_ = bf16[2,256,128]{2,1,0:T(8,128)(2,1)S(1)} collective-permute-done((bf16[2,256,128]{2,1,0:T(8,128)(2,1)S(1)}, bf16[2,256,128]{2,1,0:T(8,128)(2,1)S(1)}, u32[]{:S(2)}, u32[]{:S(2)}) %collective-permute-start) | collective-permute-done | bytes 131104 | tf_op jit(solution)/shard_map/ppermute | solution.py:206
  8.1 0.1 collective-permute-start.1
  8.2 0.4 %shard_map.87 = (f32[256,256]{1,0:T(8,128)S(1)}, f32[256,256]{1,0:T(8,128)S(1)}, f32[256,256]{1,0:T(8,128)S(1)}, f32[256,256]{1,0:T(8,128)S(1)}, f32[3,8,256]{2,1,0:T(8,128)S(1)}, /*index=5*/f32[3,8,256]{2,1,0:T(8,128)S(1)}) custom-call(s32[4,256]{1,0:T(4,128)S(1)} %get-tuple-element.47.after_ref.refs_0_, s32[4,256]{1,0:T(4,128)S(1)} %get-tuple-element.48.refs_1_, ...), custom_call_target="tpu_custom_call" | custom-call | flops 67108864 | bytes 1630208 | tf_op jit(solution)/shard_map/pallas_call | solution.py:33
  8.6 1.1 %collective-permute-done.2.refs_8_.refs_9_.refs_11_.refs_5_.refs_3_ = bf16[2,256,128]{2,1,0:T(8,128)(2,1)S(1)} collective-permute-done((bf16[2,256,128]{2,1,0:T(8,128)(2,1)S(1)}, bf16[2,256,128]{2,1,0:T(8,128)(2,1)S(1)}, u32[]{:S(2)}, u32[]{:S(2)}) %collective-permute-start.2) | collective-permute-done | bytes 131104 | tf_op jit(solution)/shard_map/ppermute | solution.py:206
  9.6 0.0 collective-permute-done.3.refs_6_.refs_7_.refs_5_
  9.7 0.6 %shard_map.88 = (f32[256,256]{1,0:T(8,128)S(1)}, f32[256,256]{1,0:T(8,128)S(1)}, f32[256,256]{1,0:T(8,128)S(1)}, f32[256,256]{1,0:T(8,128)S(1)}, f32[256,256]{1,...) custom-call(s32[4,256]{1,0:T(4,128)S(1)} %get-tuple-element.47.after, ...), custom_call_target="tpu_custom_call" | custom-call | flops 134217728 | bytes 3260416 | tf_op jit(solution)/shard_map/pallas_call | solution.py:33
  10.2 0.0 collective-permute-done.1.refs_2_.refs_3_.refs_7_
  10.2 0.4 %shard_map.89 = (f32[256,256]{1,0:T(8,128)S(1)}, f32[256,256]{1,0:T(8,128)S(1)}, f32[256,256]{1,0:T(8,128)S(1)}, f32[256,256]{1,0:T(8,128)S(1)}, f32[3,8,256]{2,...) custom-call(s32[4,256]{1,0:T(4,128)S(1)} %get-tuple-element.46.refs_0_.refs_1_, ...), custom_call_target="tpu_custom_call" | custom-call | flops 67108864 | bytes 1789952 | tf_op jit(solution)/shard_map/pallas_call | solution.py:33
  10.7 0.8 %collective-permute-start.6 = (f32[4,3,256]{2,1,0:T(4,128)S(1)}, f32[4,3,256]{2,1,0:T(4,128)S(1)}, u32[]{:S(2)}, u32[]{:S(2)}) collective-permute-start(f32[4,3,256]{2,1,0:T(4,128)S(1)} %get-tuple-element.56.refs_0_), channel_id=1, source_target_pairs={{0,12},{4,8},{8,4},{12,0},{16,28},{20,24},{24,20},{28,16},{1,13},{... | collective-permute-start | bytes 36872 | tf_op jit(solution)/shard_map/ppermute | solution.py:206
  11.5 0.3 %collective-permute-start.5 = (f32[4,3,256]{2,1,0:T(4,128)S(1)}, f32[4,3,256]{2,1,0:T(4,128)S(1)}, u32[]{:S(2)}, u32[]{:S(2)}) collective-permute-start(f32[4,3,256]{2,1,0:T(4,128)S(1)} %get-tuple-element.56.refs_0_), channel_id=1, source_target_pairs={{0,8},{4,12},{8,0},{12,4},{16,24},{20,28},{24,16},{28,20},{1,9},{5... | collective-permute-start | bytes 36872 | tf_op jit(solution)/shard_map/ppermute | solution.py:206
  11.8 0.8 %collective-permute-start.4 = (f32[4,3,256]{2,1,0:T(4,128)S(1)}, f32[4,3,256]{2,1,0:T(4,128)S(1)}, u32[]{:S(2)}, u32[]{:S(2)}) collective-permute-start(f32[4,3,256]{2,1,0:T(4,128)S(1)} %get-tuple-element.56.refs_0_), channel_id=1, source_target_pairs={{0,4},{4,0},{8,12},{12,8},{16,20},{20,16},{24,28},{28,24},{1,5},{5... | collective-permute-start | bytes 36872 | tf_op jit(solution)/shard_map/ppermute | solution.py:206
  12.6 1.3 %collective-permute-done.6.refs_3_ = f32[4,3,256]{2,1,0:T(4,128)S(1)} collective-permute-done((f32[4,3,256]{2,1,0:T(4,128)S(1)}, f32[4,3,256]{2,1,0:T(4,128)S(1)}, u32[]{:S(2)}, u32[]{:S(2)}) %collective-permute-start.6) | collective-permute-done | bytes 12320 | tf_op jit(solution)/shard_map/ppermute | solution.py:206
  13.9 1.3 %collective-permute-done.5.refs_2_ = f32[4,3,256]{2,1,0:T(4,128)S(1)} collective-permute-done((f32[4,3,256]{2,1,0:T(4,128)S(1)}, f32[4,3,256]{2,1,0:T(4,128)S(1)}, u32[]{:S(2)}, u32[]{:S(2)}) %collective-permute-start.5) | collective-permute-done | bytes 12320 | tf_op jit(solution)/shard_map/ppermute | solution.py:206
  15.2 0.0 collective-permute-done.4.refs_1_
  15.2 0.6 %shard_map.91 = (bf16[256,1024]{1,0:T(8,128)(2,1)S(1)}, bf16[4,2,32,256]{3,2,1,0:T(8,128)(2,1)S(1)}) custom-call(f32[4,3,256]{2,1,0:T(4,128)S(1)} %get-tuple-element.56.refs_0_, f32[4,3,256]{2,1,0:T(4,128)S(1)} %collective-permute-done.4.refs_1_, f32[4,3,256]{2,1,0:T(4,128)S(1)} %collective-permute-done.5.refs_2_, ...), custom_call_target="tpu_custom_call" | custom-call | flops 134217728 | bytes 3424256 | tf_op jit(solution)/shard_map/pallas_call | solution.py:33
  15.8 1.6 %collective-permute-start.10 = (bf16[4,2,32,256]{3,2,1,0:T(8,128)(2,1)S(1)}, bf16[4,2,32,256]{3,2,1,0:T(8,128)(2,1)S(1)}, u32[]{:S(2)}, u32[]{:S(2)}) collective-permute-start(bf16[4,2,32,256]{3,2,1,0:T(8,128)(2,1)S(1)} %get-tuple-element.82), channel_id=1, source_target_pairs={{0,16},{4,20},{8,24},{12,28},{16,0},{20,4},{24,8},{28,12},{1,17},{... | collective-permute-start | bytes 393224 | tf_op jit(solution)/shard_map/ppermute | solution.py:206
  17.4 0.6 %shard_map.90 = (bf16[256,1024]{1,0:T(8,128)(2,1)S(1)}, f32[4,2,32,256]{3,2,1,0:T(8,128)S(1)}) custom-call(f32[4,3,256]{2,1,0:T(4,128)S(1)} %get-tuple-element.56.refs_0_, f32[4,3,256]{2,1,0:T(4,128)S(1)} %collective-permute-done.4.refs_1_, f32[4,3,256]{2,1,0:T(4,128)S(1)} %collective-permute-done.5.refs_2_, ...), custom_call_target="tpu_custom_call" | custom-call | flops 134217728 | bytes 3555328 | tf_op jit(solution)/shard_map/pallas_call | solution.py:33
  18.0 0.4 %shard_map.92 = (f32[256,128]{1,0:T(8,128)S(1)}, bf16[256,128]{1,0:T(8,128)(2,1)S(1)}, bf16[256,128]{1,0:T(8,128)(2,1)S(1)}, bf16[256,128]{1,0:T(8,128)(2,1)S(1)}) custom-call(bf16[256,1024]{1,0:T(8,128)(2,1)S(1)} %get-tuple-element.66.refs_0_, bf16[256,1024]{1,0:T(8,128)(2,1)S(1)} %get-tuple-element.76.refs_1_, ...), custom_call_target="tpu_custom_call" | custom-call | flops 134217728 | bytes 1638400 | tf_op jit(solution)/shard_map/pallas_call | solution.py:33
  18.4 0.1 collective-permute-start.7
  18.5 0.6 %collective-permute-start.8 = (bf16[256,128]{1,0:T(8,128)(2,1)S(1)}, bf16[256,128]{1,0:T(8,128)(2,1)S(1)}, u32[]{:S(2)}, u32[]{:S(2)}) collective-permute-start(bf16[256,128]{1,0:T(8,128)(2,1)S(1)} %get-tuple-element.79), channel_id=1, source_target_pairs={{0,8},{4,12},{8,0},{12,4},{16,24},{20,28},{24,16},{28,20},{1,9},{5... | collective-permute-start | bytes 196616 | tf_op jit(solution)/shard_map/ppermute | solution.py:206
  19.2 1.2 %collective-permute-start.9 = (bf16[256,128]{1,0:T(8,128)(2,1)S(1)}, bf16[256,128]{1,0:T(8,128)(2,1)S(1)}, u32[]{:S(2)}, u32[]{:S(2)}) collective-permute-start(bf16[256,128]{1,0:T(8,128)(2,1)S(1)} %get-tuple-element.80), channel_id=1, source_target_pairs={{0,12},{4,8},{8,4},{12,0},{16,28},{20,24},{24,20},{28,16},{1,13},{... | collective-permute-start | bytes 196616 | tf_op jit(solution)/shard_map/ppermute | solution.py:206
  20.4 0.5 %collective-permute-done.10.refs_1_ = bf16[4,2,32,256]{3,2,1,0:T(8,128)(2,1)S(1)} collective-permute-done((bf16[4,2,32,256]{3,2,1,0:T(8,128)(2,1)S(1)}, bf16[4,2,32,256]{3,2,1,0:T(8,128)(2,1)S(1)}, u32[]{:S(2)}, u32[]{:S(2)}) %collective-permute-start.10) | collective-permute-done | bytes 131104 | tf_op jit(solution)/shard_map/ppermute | solution.py:206
  20.9 2.6 %collective-permute-start.11 = (bf16[2,32,256]{2,1,0:T(8,128)(2,1)S(1)}, bf16[2,32,256]{2,1,0:T(8,128)(2,1)S(1)}, u32[]{:S(2)}, u32[]{:S(2)}) collective-permute-start(bf16[2,32,256]{2,1,0:T(8,128)(2,1)S(1)} %get-tuple-element.84), channel_id=1, source_target_pairs={{0,2},{1,3},{2,1},{3,0},{4,5},{5,7},{6,4},{7,6},{8,10},{9,11},{10,... | collective-permute-start | bytes 98312 | tf_op jit(solution)/shard_map/ppermute | solution.py:283
  23.6 1.2 %collective-permute-start.12 = (bf16[2,32,256]{2,1,0:T(8,128)(2,1)S(1)}, bf16[2,32,256]{2,1,0:T(8,128)(2,1)S(1)}, u32[]{:S(2)}, u32[]{:S(2)}) collective-permute-start(bf16[2,32,256]{2,1,0:T(8,128)(2,1)S(1)} %get-tuple-element.85), channel_id=1, source_target_pairs={{0,3},{1,2},{2,0},{3,1},{4,7},{5,6},{6,5},{7,4},{8,11},{9,10},{10,... | collective-permute-start | bytes 98312 | tf_op jit(solution)/shard_map/ppermute | solution.py:283
  24.8 0.0 collective-permute-done.7.refs_1_
  24.8 0.3 %collective-permute-start.13 = (bf16[2,32,256]{2,1,0:T(8,128)(2,1)S(1)}, bf16[2,32,256]{2,1,0:T(8,128)(2,1)S(1)}, u32[]{:S(2)}, u32[]{:S(2)}) collective-permute-start(bf16[2,32,256]{2,1,0:T(8,128)(2,1)S(1)} %get-tuple-element.86), channel_id=1, source_target_pairs={{0,1},{1,0},{2,3},{3,2},{4,6},{5,4},{6,7},{7,5},{8,9},{9,8},{10,11... | collective-permute-start | bytes 98312 | tf_op jit(solution)/shard_map/ppermute | solution.py:283
  25.1 0.0 collective-permute-done.8.refs_2_
  25.1 0.0 collective-permute-done.9.refs_3_
  25.1 0.7 %shard_map.93 = f32[256,128]{1,0:T(8,128)} custom-call(f32[256,128]{1,0:T(8,128)S(1)} %get-tuple-element.77.refs_0_, bf16[256,128]{1,0:T(8,128)(2,1)S(1)} %collective-permute-done.7.refs_1_, bf16[256,128]{1,0:T(8,128)(2,1)S(1)} %collective-permute-done.8.refs_2_, bf16[256,128]{1,0:T(8,128)(2,1)S(1)} %collective-permute-done.9.refs_3_), custom_call_target="tpu_custom_call" | custom-call | bytes 458752 | tf_op jit(solution)/shard_map/pallas_call | solution.py:33
  25.8 1.0 %collective-permute-done.11.refs_1_ = bf16[2,32,256]{2,1,0:T(8,128)(2,1)S(1)} collective-permute-done((bf16[2,32,256]{2,1,0:T(8,128)(2,1)S(1)}, bf16[2,32,256]{2,1,0:T(8,128)(2,1)S(1)}, u32[]{:S(2)}, u32[]{:S(2)}) %collective-permute-start.11) | collective-permute-done | bytes 32800 | tf_op jit(solution)/shard_map/ppermute | solution.py:283
  26.8 1.5 %collective-permute-done.12.refs_2_ = bf16[2,32,256]{2,1,0:T(8,128)(2,1)S(1)} collective-permute-done((bf16[2,32,256]{2,1,0:T(8,128)(2,1)S(1)}, bf16[2,32,256]{2,1,0:T(8,128)(2,1)S(1)}, u32[]{:S(2)}, u32[]{:S(2)}) %collective-permute-start.12) | collective-permute-done | bytes 32800 | tf_op jit(solution)/shard_map/ppermute | solution.py:283
  28.4 0.4 %collective-permute-done.13.refs_3_ = bf16[2,32,256]{2,1,0:T(8,128)(2,1)S(1)} collective-permute-done((bf16[2,32,256]{2,1,0:T(8,128)(2,1)S(1)}, bf16[2,32,256]{2,1,0:T(8,128)(2,1)S(1)}, u32[]{:S(2)}, u32[]{:S(2)}) %collective-permute-start.13) | collective-permute-done | bytes 32800 | tf_op jit(solution)/shard_map/ppermute | solution.py:283
  28.7 0.6 %shard_map.95 = (f32[32,256]{1,0:T(8,128)}, f32[32,256]{1,0:T(8,128)}) custom-call(f32[2,32,256]{2,1,0:T(8,128)S(1)} %get-tuple-element.83.refs_0_, bf16[2,32,256]{2,1,0:T(8,128)(2,1)S(1)} %collective-permute-done.11.refs_1_, bf16[2,32,256]{2,1,0:T(8,128)(2,1)S(1)} %collective-permute-done.12.refs_2_, bf16[2,32,256]{2,1,0:T(8,128)(2,1)S(1)} %collective-permute-done.13.refs_3_), custom_call_target="tpu_custom_call" | custom-call | bytes 229376 | tf_op jit(solution)/shard_map/pallas_call | solution.py:33
  (3 shorter events, 0.1 us)
Async XLA Ops:
  0.6 3.9 %copy-start.2 = (bf16[256,128]{1,0:T(8,128)(2,1)S(1)}, bf16[256,128]{1,0:T(8,128)(2,1)}, u32[]{:S(2)}) copy-start(bf16[256,128]{1,0:T(8,128)(2,1)} %param.8) | copy-start | bytes 196612
  0.6 3.9 %copy-start.3 = (bf16[256,128]{1,0:T(8,128)(2,1)S(1)}, bf16[256,128]{1,0:T(8,128)(2,1)}, u32[]{:S(2)}) copy-start(bf16[256,128]{1,0:T(8,128)(2,1)} %param.7) | copy-start | bytes 196612
  1.6 6.5 %collective-permute-start = (bf16[2,256,128]{2,1,0:T(8,128)(2,1)S(1)}, bf16[2,256,128]{2,1,0:T(8,128)(2,1)S(1)}, u32[]{:S(2)}, u32[]{:S(2)}) collective-permute-start(bf16[2,256,128]{2,1,0:T(8,128)(2,1)S(1)} %pad_maximum_fusion.refs_2_.refs_4_), channel_id=1, source_target_pairs={{0,8},{4,12},{8,0},{12,4},{16,24},{20,28},{24,16},{28,20},{1,9},{5... | collective-permute-start | bytes 393224 | tf_op jit(solution)/shard_map/ppermute | solution.py:206
  4.6 1.6 %copy-start = (s32[16,16]{1,0:T(8,128)S(1)}, s32[16,16]{1,0:T(8,128)}, u32[]{:S(2)}) copy-start(s32[16,16]{1,0:T(8,128)} %mask_ref.1) | copy-start | bytes 3076
  4.6 1.6 %copy-start.1 = (s32[16]{0:T(128)S(1)}, s32[16]{0:T(128)}, u32[]{:S(2)}) copy-start(s32[16]{0:T(128)} %ids_ref.1) | copy-start | bytes 196
  4.6 5.0 %collective-permute-start.2 = (bf16[2,256,128]{2,1,0:T(8,128)(2,1)S(1)}, bf16[2,256,128]{2,1,0:T(8,128)(2,1)S(1)}, u32[]{:S(2)}, u32[]{:S(2)}) collective-permute-start(bf16[2,256,128]{2,1,0:T(8,128)(2,1)S(1)} %pad_maximum_fusion.1.refs_4_.refs_5_.refs_10_.refs_2_), channel_id=1, source_target_pairs={{0,16},{4,20},{8,24},{12,28},{16,0},{20,4},{24,8},{28,12},{1,17},{... | collective-permute-start | bytes 393224 | tf_op jit(solution)/shard_map/ppermute | solution.py:206
  6.2 3.5 %collective-permute-start.3 = (bf16[2,256,128]{2,1,0:T(8,128)(2,1)S(1)}, bf16[2,256,128]{2,1,0:T(8,128)(2,1)S(1)}, u32[]{:S(2)}, u32[]{:S(2)}) collective-permute-start(bf16[2,256,128]{2,1,0:T(8,128)(2,1)S(1)} %pad_maximum_fusion.refs_2_.refs_4_), channel_id=1, source_target_pairs={{0,4},{4,0},{8,12},{12,8},{16,20},{20,16},{24,28},{28,24},{1,5},{5... | collective-permute-start | bytes 393224 | tf_op jit(solution)/shard_map/ppermute | solution.py:206
  8.1 2.1 %collective-permute-start.1 = (bf16[2,256,128]{2,1,0:T(8,128)(2,1)S(1)}, bf16[2,256,128]{2,1,0:T(8,128)(2,1)S(1)}, u32[]{:S(2)}, u32[]{:S(2)}) collective-permute-start(bf16[2,256,128]{2,1,0:T(8,128)(2,1)S(1)} %shard_map.86), channel_id=1, source_target_pairs={{0,4},{4,0},{8,12},{12,8},{16,20},{20,16},{24,28},{28,24},{1,5},{5... | collective-permute-start | bytes 393224 | tf_op jit(solution)/shard_map/ppermute | solution.py:206
  10.7 3.2 %collective-permute-start.6 = (f32[4,3,256]{2,1,0:T(4,128)S(1)}, f32[4,3,256]{2,1,0:T(4,128)S(1)}, u32[]{:S(2)}, u32[]{:S(2)}) collective-permute-start(f32[4,3,256]{2,1,0:T(4,128)S(1)} %get-tuple-element.56.refs_0_), channel_id=1, source_target_pairs={{0,12},{4,8},{8,4},{12,0},{16,28},{20,24},{24,20},{28,16},{1,13},{... | collective-permute-start | bytes 36872 | tf_op jit(solution)/shard_map/ppermute | solution.py:206
  11.5 3.7 %collective-permute-start.5 = (f32[4,3,256]{2,1,0:T(4,128)S(1)}, f32[4,3,256]{2,1,0:T(4,128)S(1)}, u32[]{:S(2)}, u32[]{:S(2)}) collective-permute-start(f32[4,3,256]{2,1,0:T(4,128)S(1)} %get-tuple-element.56.refs_0_), channel_id=1, source_target_pairs={{0,8},{4,12},{8,0},{12,4},{16,24},{20,28},{24,16},{28,20},{1,9},{5... | collective-permute-start | bytes 36872 | tf_op jit(solution)/shard_map/ppermute | solution.py:206
  11.8 3.4 %collective-permute-start.4 = (f32[4,3,256]{2,1,0:T(4,128)S(1)}, f32[4,3,256]{2,1,0:T(4,128)S(1)}, u32[]{:S(2)}, u32[]{:S(2)}) collective-permute-start(f32[4,3,256]{2,1,0:T(4,128)S(1)} %get-tuple-element.56.refs_0_), channel_id=1, source_target_pairs={{0,4},{4,0},{8,12},{12,8},{16,20},{20,16},{24,28},{28,24},{1,5},{5... | collective-permute-start | bytes 36872 | tf_op jit(solution)/shard_map/ppermute | solution.py:206
  15.8 5.0 %collective-permute-start.10 = (bf16[4,2,32,256]{3,2,1,0:T(8,128)(2,1)S(1)}, bf16[4,2,32,256]{3,2,1,0:T(8,128)(2,1)S(1)}, u32[]{:S(2)}, u32[]{:S(2)}) collective-permute-start(bf16[4,2,32,256]{3,2,1,0:T(8,128)(2,1)S(1)} %get-tuple-element.82), channel_id=1, source_target_pairs={{0,16},{4,20},{8,24},{12,28},{16,0},{20,4},{24,8},{28,12},{1,17},{... | collective-permute-start | bytes 393224 | tf_op jit(solution)/shard_map/ppermute | solution.py:206
  18.4 6.3 %collective-permute-start.7 = (bf16[256,128]{1,0:T(8,128)(2,1)S(1)}, bf16[256,128]{1,0:T(8,128)(2,1)S(1)}, u32[]{:S(2)}, u32[]{:S(2)}) collective-permute-start(bf16[256,128]{1,0:T(8,128)(2,1)S(1)} %get-tuple-element.78), channel_id=1, source_target_pairs={{0,4},{4,0},{8,12},{12,8},{16,20},{20,16},{24,28},{28,24},{1,5},{5... | collective-permute-start | bytes 196616 | tf_op jit(solution)/shard_map/ppermute | solution.py:206
  18.5 6.6 %collective-permute-start.8 = (bf16[256,128]{1,0:T(8,128)(2,1)S(1)}, bf16[256,128]{1,0:T(8,128)(2,1)S(1)}, u32[]{:S(2)}, u32[]{:S(2)}) collective-permute-start(bf16[256,128]{1,0:T(8,128)(2,1)S(1)} %get-tuple-element.79), channel_id=1, source_target_pairs={{0,8},{4,12},{8,0},{12,4},{16,24},{20,28},{24,16},{28,20},{1,9},{5... | collective-permute-start | bytes 196616 | tf_op jit(solution)/shard_map/ppermute | solution.py:206
  19.2 6.0 %collective-permute-start.9 = (bf16[256,128]{1,0:T(8,128)(2,1)S(1)}, bf16[256,128]{1,0:T(8,128)(2,1)S(1)}, u32[]{:S(2)}, u32[]{:S(2)}) collective-permute-start(bf16[256,128]{1,0:T(8,128)(2,1)S(1)} %get-tuple-element.80), channel_id=1, source_target_pairs={{0,12},{4,8},{8,4},{12,0},{16,28},{20,24},{24,20},{28,16},{1,13},{... | collective-permute-start | bytes 196616 | tf_op jit(solution)/shard_map/ppermute | solution.py:206
  20.9 5.9 %collective-permute-start.11 = (bf16[2,32,256]{2,1,0:T(8,128)(2,1)S(1)}, bf16[2,32,256]{2,1,0:T(8,128)(2,1)S(1)}, u32[]{:S(2)}, u32[]{:S(2)}) collective-permute-start(bf16[2,32,256]{2,1,0:T(8,128)(2,1)S(1)} %get-tuple-element.84), channel_id=1, source_target_pairs={{0,2},{1,3},{2,1},{3,0},{4,5},{5,7},{6,4},{7,6},{8,10},{9,11},{10,... | collective-permute-start | bytes 98312 | tf_op jit(solution)/shard_map/ppermute | solution.py:283
  23.6 4.8 %collective-permute-start.12 = (bf16[2,32,256]{2,1,0:T(8,128)(2,1)S(1)}, bf16[2,32,256]{2,1,0:T(8,128)(2,1)S(1)}, u32[]{:S(2)}, u32[]{:S(2)}) collective-permute-start(bf16[2,32,256]{2,1,0:T(8,128)(2,1)S(1)} %get-tuple-element.85), channel_id=1, source_target_pairs={{0,3},{1,2},{2,0},{3,1},{4,7},{5,6},{6,5},{7,4},{8,11},{9,10},{10,... | collective-permute-start | bytes 98312 | tf_op jit(solution)/shard_map/ppermute | solution.py:283
  24.8 3.9 %collective-permute-start.13 = (bf16[2,32,256]{2,1,0:T(8,128)(2,1)S(1)}, bf16[2,32,256]{2,1,0:T(8,128)(2,1)S(1)}, u32[]{:S(2)}, u32[]{:S(2)}) collective-permute-start(bf16[2,32,256]{2,1,0:T(8,128)(2,1)S(1)} %get-tuple-element.86), channel_id=1, source_target_pairs={{0,1},{1,0},{2,3},{3,2},{4,6},{5,4},{6,7},{7,5},{8,9},{9,8},{10,11... | collective-permute-start | bytes 98312 | tf_op jit(solution)/shard_map/ppermute | solution.py:283

commit v9 on v8

--- a/solution.py
+++ b/solution.py
@@ -89,15 +89,6 @@
         stats_refs[i][2] = jnp.sum(weights * dprobs.reshape(-1, 8, unit), axis=0)
 
 
-def merge_stats(left, right):
-    top = jnp.maximum(left[0:1], right[0:1])
-    first, second = jnp.exp2(left[0:1] - top), jnp.exp2(right[0:1] - top)
-    return jnp.concatenate(
-        [top, left[1:2] * first + right[1:2] * second, left[2:3] * first + right[2:3] * second],
-        axis=0,
-    )
-
-
 def collect_kernel(units, *refs):
     for r in range(SHARE):
         parts = [refs[r * units + u] for u in range(units)]
@@ -128,9 +119,12 @@
     sub = width // GROUP
     dk, dv = 0.0, 0.0
     for r in range(SHARE):
-        whole = functools.reduce(merge_stats, [all_refs[s][r ^ s] for s in range(SHARE)])
-        share = jnp.exp2(stats_refs[r][0] - whole[0:1]) / whole[1:2]
-        delta = whole[2:3] / whole[1:2]
+        stats = [all_refs[s][r ^ s] for s in range(SHARE)]
+        top = functools.reduce(jnp.maximum, [x[0:1] for x in stats])
+        factors = [jnp.exp2(x[0:1] - top) for x in stats]
+        inverse = 1.0 / sum(x[1:2] * factor for x, factor in zip(stats, factors))
+        share = jnp.exp2(stats_refs[r][0] - top) * inverse
+        delta = sum(x[2:3] * factor for x, factor in zip(stats, factors)) * inverse
         probs = (exp_refs[r][...].reshape(-1, 8, unit) * share).reshape(unit, unit)
         dprobs = dprob_refs[r][...]
         dscores = (probs * (dprobs - delta)).astype(BF16)

time: 29.5 us -> 29.5 us (level)
  no operation moved by 1% of the time
where the time goes in v9:
time: 29.5 us; the launch traced here: 29.3 us
  starting transfers between devices  14.3 us (48%)
  waiting for transfers between devices  8.2 us (28%)
  Pallas kernels  5.1 us (17%)
  other arithmetic  0.94 us (3%)
  between operations  0.76 us (3%)
    ppermute x11, starting transfers between devices, swap(): return lax.ppermute(x, 'ctx', [(i, i ^ step) for i in range(ctx_size)])  10.1 us
    ppermute x11, waiting for transfers between devices, swap(): return lax.ppermute(x, 'ctx', [(i, i ^ step) for i in range(ctx_size)])  5.32 us
    pallas_call x11, Pallas kernels, call(): pl.pallas_call(kernel, out_shape=out_shape, in_specs=in_specs or [vmem()...  5.1 us
    ppermute x3, starting transfers between devices, cross(): return lax.ppermute(x, ('ctx', 'fsdp'), pairs)  4.22 us
    ppermute x3, waiting for transfers between devices, cross(): return lax.ppermute(x, ('ctx', 'fsdp'), pairs)  2.89 us
    another operation x2, other arithmetic, body(): qg, kv = (jnp.stack([queries, out_grad]), jnp.stack([keys, values]))  0.94 us
  transfers between devices with their start and end apart: 14, of which 8 were waited for; matrix products, arithmetic and copies ran while one was open for 0% of the time, Pallas kernels for 12%

profile of v9, /device:TPU:0, one launch (start us, length us, event | category | flops | bytes accessed | tf_op | source)
XLA Modules:
  0.0 29.3 jit_solution(15145950406921306987)
XLA Ops:
  0.6 0.0 copy-start.2
  0.6 0.0 copy-start.3
  0.7 0.9 %pad_maximum_fusion.refs_2_.refs_4_ = bf16[2,256,128]{2,1,0:T(8,128)(2,1)S(1)} fusion(bf16[1,256,128]{2,1,0:T(8,128)(2,1)} %bitcast.6, bf16[1,256,128]{2,1,0:T(8,128)(2,1)} %bitcast.7), kind=kLoop, calls=%fused_computation | loop fusion | flops 65536 | bytes 262144 | tf_op jit(solution)/shard_map/stack | solution.py:202
  1.6 3.0 %collective-permute-start = (bf16[2,256,128]{2,1,0:T(8,128)(2,1)S(1)}, bf16[2,256,128]{2,1,0:T(8,128)(2,1)S(1)}, u32[]{:S(2)}, u32[]{:S(2)}) collective-permute-start(bf16[2,256,128]{2,1,0:T(8,128)(2,1)S(1)} %pad_maximum_fusion.refs_2_.refs_4_), channel_id=1, source_target_pairs={{0,8},{4,12},{8,0},{12,4},{16,24},{20,28},{24,16},{28,20},{1,9},{5... | collective-permute-start | bytes 393224 | tf_op jit(solution)/shard_map/ppermute | solution.py:200
  4.6 0.0 copy-done.2
  4.6 0.0 copy-done.3
  4.6 0.0 copy-start
  4.6 0.0 copy-start.1
  4.6 1.6 %collective-permute-start.2 = (bf16[2,256,128]{2,1,0:T(8,128)(2,1)S(1)}, bf16[2,256,128]{2,1,0:T(8,128)(2,1)S(1)}, u32[]{:S(2)}, u32[]{:S(2)}) collective-permute-start(bf16[2,256,128]{2,1,0:T(8,128)(2,1)S(1)} %pad_maximum_fusion.1.refs_4_.refs_5_.refs_10_.refs_2_), channel_id=1, source_target_pairs={{0,16},{4,20},{8,24},{12,28},{16,0},{20,4},{24,8},{28,12},{1,17},{... | collective-permute-start | bytes 393224 | tf_op jit(solution)/shard_map/ppermute | solution.py:200
  6.2 0.0 collective-permute-start.3
  6.2 0.0 copy-done
  6.2 0.0 copy-done.1
  6.2 0.8 %shard_map.85 = (s32[4,256]{1,0:T(4,128)S(1)}, s32[4,256]{1,0:T(4,128)S(1)}, s32[4,256]{1,0:T(4,128)S(1)}, s32[4,256]{1,0:T(4,128)S(1)}) custom-call(s32[16]{0:T(128)S(1)} %copy-done.1, s32[16,16]{1,0:T(8,128)S(1)} %copy-done), custom_call_target="tpu_custom_call" | custom-call | bytes 17472 | tf_op jit(solution)/shard_map/pallas_call | solution.py:33
  7.0 1.1 %collective-permute-done.in_ref.refs_3_.refs_5_.refs_6_ = bf16[2,256,128]{2,1,0:T(8,128)(2,1)S(1)} collective-permute-done((bf16[2,256,128]{2,1,0:T(8,128)(2,1)S(1)}, bf16[2,256,128]{2,1,0:T(8,128)(2,1)S(1)}, u32[]{:S(2)}, u32[]{:S(2)}) %collective-permute-start) | collective-permute-done | bytes 131104 | tf_op jit(solution)/shard_map/ppermute | solution.py:200
  8.1 0.1 collective-permute-start.1
  8.2 0.4 %shard_map.87 = (f32[256,256]{1,0:T(8,128)S(1)}, f32[256,256]{1,0:T(8,128)S(1)}, f32[256,256]{1,0:T(8,128)S(1)}, f32[256,256]{1,0:T(8,128)S(1)}, f32[3,8,256]{2,1,0:T(8,128)S(1)}, /*index=5*/f32[3,8,256]{2,1,0:T(8,128)S(1)}) custom-call(s32[4,256]{1,0:T(4,128)S(1)} %get-tuple-element.47.after_ref.refs_0_, s32[4,256]{1,0:T(4,128)S(1)} %get-tuple-element.48.refs_1_, ...), custom_call_target="tpu_custom_call" | custom-call | flops 67108864 | bytes 1630208 | tf_op jit(solution)/shard_map/pallas_call | solution.py:33
  8.6 1.1 %collective-permute-done.2.refs_8_.refs_9_.refs_11_.refs_5_.refs_3_ = bf16[2,256,128]{2,1,0:T(8,128)(2,1)S(1)} collective-permute-done((bf16[2,256,128]{2,1,0:T(8,128)(2,1)S(1)}, bf16[2,256,128]{2,1,0:T(8,128)(2,1)S(1)}, u32[]{:S(2)}, u32[]{:S(2)}) %collective-permute-start.2) | collective-permute-done | bytes 131104 | tf_op jit(solution)/shard_map/ppermute | solution.py:200
  9.6 0.0 collective-permute-done.3.refs_6_.refs_7_.refs_5_
  9.7 0.6 %shard_map.88 = (f32[256,256]{1,0:T(8,128)S(1)}, f32[256,256]{1,0:T(8,128)S(1)}, f32[256,256]{1,0:T(8,128)S(1)}, f32[256,256]{1,0:T(8,128)S(1)}, f32[256,256]{1,...) custom-call(s32[4,256]{1,0:T(4,128)S(1)} %get-tuple-element.47.after, ...), custom_call_target="tpu_custom_call" | custom-call | flops 134217728 | bytes 3260416 | tf_op jit(solution)/shard_map/pallas_call | solution.py:33
  10.2 0.0 collective-permute-done.1.refs_2_.refs_3_.refs_7_
  10.2 0.4 %shard_map.89 = (f32[256,256]{1,0:T(8,128)S(1)}, f32[256,256]{1,0:T(8,128)S(1)}, f32[256,256]{1,0:T(8,128)S(1)}, f32[256,256]{1,0:T(8,128)S(1)}, f32[3,8,256]{2,...) custom-call(s32[4,256]{1,0:T(4,128)S(1)} %get-tuple-element.46.refs_0_.refs_1_, ...), custom_call_target="tpu_custom_call" | custom-call | flops 67108864 | bytes 1789952 | tf_op jit(solution)/shard_map/pallas_call | solution.py:33
  10.7 0.8 %collective-permute-start.6 = (f32[4,3,256]{2,1,0:T(4,128)S(1)}, f32[4,3,256]{2,1,0:T(4,128)S(1)}, u32[]{:S(2)}, u32[]{:S(2)}) collective-permute-start(f32[4,3,256]{2,1,0:T(4,128)S(1)} %get-tuple-element.56.refs_0_), channel_id=1, source_target_pairs={{0,12},{4,8},{8,4},{12,0},{16,28},{20,24},{24,20},{28,16},{1,13},{... | collective-permute-start | bytes 36872 | tf_op jit(solution)/shard_map/ppermute | solution.py:200
  11.5 0.3 %collective-permute-start.5 = (f32[4,3,256]{2,1,0:T(4,128)S(1)}, f32[4,3,256]{2,1,0:T(4,128)S(1)}, u32[]{:S(2)}, u32[]{:S(2)}) collective-permute-start(f32[4,3,256]{2,1,0:T(4,128)S(1)} %get-tuple-element.56.refs_0_), channel_id=1, source_target_pairs={{0,8},{4,12},{8,0},{12,4},{16,24},{20,28},{24,16},{28,20},{1,9},{5... | collective-permute-start | bytes 36872 | tf_op jit(solution)/shard_map/ppermute | solution.py:200
  11.8 0.8 %collective-permute-start.4 = (f32[4,3,256]{2,1,0:T(4,128)S(1)}, f32[4,3,256]{2,1,0:T(4,128)S(1)}, u32[]{:S(2)}, u32[]{:S(2)}) collective-permute-start(f32[4,3,256]{2,1,0:T(4,128)S(1)} %get-tuple-element.56.refs_0_), channel_id=1, source_target_pairs={{0,4},{4,0},{8,12},{12,8},{16,20},{20,16},{24,28},{28,24},{1,5},{5... | collective-permute-start | bytes 36872 | tf_op jit(solution)/shard_map/ppermute | solution.py:200
  12.6 1.3 %collective-permute-done.6.refs_3_ = f32[4,3,256]{2,1,0:T(4,128)S(1)} collective-permute-done((f32[4,3,256]{2,1,0:T(4,128)S(1)}, f32[4,3,256]{2,1,0:T(4,128)S(1)}, u32[]{:S(2)}, u32[]{:S(2)}) %collective-permute-start.6) | collective-permute-done | bytes 12320 | tf_op jit(solution)/shard_map/ppermute | solution.py:200
  13.9 1.3 %collective-permute-done.5.refs_2_ = f32[4,3,256]{2,1,0:T(4,128)S(1)} collective-permute-done((f32[4,3,256]{2,1,0:T(4,128)S(1)}, f32[4,3,256]{2,1,0:T(4,128)S(1)}, u32[]{:S(2)}, u32[]{:S(2)}) %collective-permute-start.5) | collective-permute-done | bytes 12320 | tf_op jit(solution)/shard_map/ppermute | solution.py:200
  15.2 0.0 collective-permute-done.4.refs_1_
  15.2 0.6 %shard_map.91 = (bf16[256,1024]{1,0:T(8,128)(2,1)S(1)}, bf16[4,2,32,256]{3,2,1,0:T(8,128)(2,1)S(1)}) custom-call(f32[4,3,256]{2,1,0:T(4,128)S(1)} %get-tuple-element.56.refs_0_, f32[4,3,256]{2,1,0:T(4,128)S(1)} %collective-permute-done.4.refs_1_, f32[4,3,256]{2,1,0:T(4,128)S(1)} %collective-permute-done.5.refs_2_, ...), custom_call_target="tpu_custom_call" | custom-call | flops 134217728 | bytes 3424256 | tf_op jit(solution)/shard_map/pallas_call | solution.py:33
  15.8 1.6 %collective-permute-start.10 = (bf16[4,2,32,256]{3,2,1,0:T(8,128)(2,1)S(1)}, bf16[4,2,32,256]{3,2,1,0:T(8,128)(2,1)S(1)}, u32[]{:S(2)}, u32[]{:S(2)}) collective-permute-start(bf16[4,2,32,256]{3,2,1,0:T(8,128)(2,1)S(1)} %get-tuple-element.82), channel_id=1, source_target_pairs={{0,16},{4,20},{8,24},{12,28},{16,0},{20,4},{24,8},{28,12},{1,17},{... | collective-permute-start | bytes 393224 | tf_op jit(solution)/shard_map/ppermute | solution.py:200
  17.4 0.6 %shard_map.90 = (bf16[256,1024]{1,0:T(8,128)(2,1)S(1)}, f32[4,2,32,256]{3,2,1,0:T(8,128)S(1)}) custom-call(f32[4,3,256]{2,1,0:T(4,128)S(1)} %get-tuple-element.56.refs_0_, f32[4,3,256]{2,1,0:T(4,128)S(1)} %collective-permute-done.4.refs_1_, f32[4,3,256]{2,1,0:T(4,128)S(1)} %collective-permute-done.5.refs_2_, ...), custom_call_target="tpu_custom_call" | custom-call | flops 134217728 | bytes 3555328 | tf_op jit(solution)/shard_map/pallas_call | solution.py:33
  18.0 0.4 %shard_map.92 = (f32[256,128]{1,0:T(8,128)S(1)}, bf16[256,128]{1,0:T(8,128)(2,1)S(1)}, bf16[256,128]{1,0:T(8,128)(2,1)S(1)}, bf16[256,128]{1,0:T(8,128)(2,1)S(1)}) custom-call(bf16[256,1024]{1,0:T(8,128)(2,1)S(1)} %get-tuple-element.66.refs_0_, bf16[256,1024]{1,0:T(8,128)(2,1)S(1)} %get-tuple-element.76.refs_1_, ...), custom_call_target="tpu_custom_call" | custom-call | flops 134217728 | bytes 1638400 | tf_op jit(solution)/shard_map/pallas_call | solution.py:33
  18.4 0.1 collective-permute-start.7
  18.5 0.6 %collective-permute-start.8 = (bf16[256,128]{1,0:T(8,128)(2,1)S(1)}, bf16[256,128]{1,0:T(8,128)(2,1)S(1)}, u32[]{:S(2)}, u32[]{:S(2)}) collective-permute-start(bf16[256,128]{1,0:T(8,128)(2,1)S(1)} %get-tuple-element.79), channel_id=1, source_target_pairs={{0,8},{4,12},{8,0},{12,4},{16,24},{20,28},{24,16},{28,20},{1,9},{5... | collective-permute-start | bytes 196616 | tf_op jit(solution)/shard_map/ppermute | solution.py:200
  19.1 1.2 %collective-permute-start.9 = (bf16[256,128]{1,0:T(8,128)(2,1)S(1)}, bf16[256,128]{1,0:T(8,128)(2,1)S(1)}, u32[]{:S(2)}, u32[]{:S(2)}) collective-permute-start(bf16[256,128]{1,0:T(8,128)(2,1)S(1)} %get-tuple-element.80), channel_id=1, source_target_pairs={{0,12},{4,8},{8,4},{12,0},{16,28},{20,24},{24,20},{28,16},{1,13},{... | collective-permute-start | bytes 196616 | tf_op jit(solution)/shard_map/ppermute | solution.py:200
  20.4 0.5 %collective-permute-done.10.refs_1_ = bf16[4,2,32,256]{3,2,1,0:T(8,128)(2,1)S(1)} collective-permute-done((bf16[4,2,32,256]{3,2,1,0:T(8,128)(2,1)S(1)}, bf16[4,2,32,256]{3,2,1,0:T(8,128)(2,1)S(1)}, u32[]{:S(2)}, u32[]{:S(2)}) %collective-permute-start.10) | collective-permute-done | bytes 131104 | tf_op jit(solution)/shard_map/ppermute | solution.py:200
  20.9 2.6 %collective-permute-start.11 = (bf16[2,32,256]{2,1,0:T(8,128)(2,1)S(1)}, bf16[2,32,256]{2,1,0:T(8,128)(2,1)S(1)}, u32[]{:S(2)}, u32[]{:S(2)}) collective-permute-start(bf16[2,32,256]{2,1,0:T(8,128)(2,1)S(1)} %get-tuple-element.84), channel_id=1, source_target_pairs={{0,2},{1,3},{2,1},{3,0},{4,5},{5,7},{6,4},{7,6},{8,10},{9,11},{10,... | collective-permute-start | bytes 98312 | tf_op jit(solution)/shard_map/ppermute | solution.py:277
  23.5 1.2 %collective-permute-start.12 = (bf16[2,32,256]{2,1,0:T(8,128)(2,1)S(1)}, bf16[2,32,256]{2,1,0:T(8,128)(2,1)S(1)}, u32[]{:S(2)}, u32[]{:S(2)}) collective-permute-start(bf16[2,32,256]{2,1,0:T(8,128)(2,1)S(1)} %get-tuple-element.85), channel_id=1, source_target_pairs={{0,3},{1,2},{2,0},{3,1},{4,7},{5,6},{6,5},{7,4},{8,11},{9,10},{10,... | collective-permute-start | bytes 98312 | tf_op jit(solution)/shard_map/ppermute | solution.py:277
  24.8 0.0 collective-permute-done.7.refs_1_
  24.8 0.3 %collective-permute-start.13 = (bf16[2,32,256]{2,1,0:T(8,128)(2,1)S(1)}, bf16[2,32,256]{2,1,0:T(8,128)(2,1)S(1)}, u32[]{:S(2)}, u32[]{:S(2)}) collective-permute-start(bf16[2,32,256]{2,1,0:T(8,128)(2,1)S(1)} %get-tuple-element.86), channel_id=1, source_target_pairs={{0,1},{1,0},{2,3},{3,2},{4,6},{5,4},{6,7},{7,5},{8,9},{9,8},{10,11... | collective-permute-start | bytes 98312 | tf_op jit(solution)/shard_map/ppermute | solution.py:277
  25.1 0.0 collective-permute-done.8.refs_2_
  25.1 0.0 collective-permute-done.9.refs_3_
  25.1 0.7 %shard_map.93 = f32[256,128]{1,0:T(8,128)} custom-call(f32[256,128]{1,0:T(8,128)S(1)} %get-tuple-element.77.refs_0_, bf16[256,128]{1,0:T(8,128)(2,1)S(1)} %collective-permute-done.7.refs_1_, bf16[256,128]{1,0:T(8,128)(2,1)S(1)} %collective-permute-done.8.refs_2_, bf16[256,128]{1,0:T(8,128)(2,1)S(1)} %collective-permute-done.9.refs_3_), custom_call_target="tpu_custom_call" | custom-call | bytes 458752 | tf_op jit(solution)/shard_map/pallas_call | solution.py:33
  25.8 1.0 %collective-permute-done.11.refs_1_ = bf16[2,32,256]{2,1,0:T(8,128)(2,1)S(1)} collective-permute-done((bf16[2,32,256]{2,1,0:T(8,128)(2,1)S(1)}, bf16[2,32,256]{2,1,0:T(8,128)(2,1)S(1)}, u32[]{:S(2)}, u32[]{:S(2)}) %collective-permute-start.11) | collective-permute-done | bytes 32800 | tf_op jit(solution)/shard_map/ppermute | solution.py:277
  26.8 1.5 %collective-permute-done.12.refs_2_ = bf16[2,32,256]{2,1,0:T(8,128)(2,1)S(1)} collective-permute-done((bf16[2,32,256]{2,1,0:T(8,128)(2,1)S(1)}, bf16[2,32,256]{2,1,0:T(8,128)(2,1)S(1)}, u32[]{:S(2)}, u32[]{:S(2)}) %collective-permute-start.12) | collective-permute-done | bytes 32800 | tf_op jit(solution)/shard_map/ppermute | solution.py:277
  28.4 0.4 %collective-permute-done.13.refs_3_ = bf16[2,32,256]{2,1,0:T(8,128)(2,1)S(1)} collective-permute-done((bf16[2,32,256]{2,1,0:T(8,128)(2,1)S(1)}, bf16[2,32,256]{2,1,0:T(8,128)(2,1)S(1)}, u32[]{:S(2)}, u32[]{:S(2)}) %collective-permute-start.13) | collective-permute-done | bytes 32800 | tf_op jit(solution)/shard_map/ppermute | solution.py:277
  28.7 0.6 %shard_map.95 = (f32[32,256]{1,0:T(8,128)}, f32[32,256]{1,0:T(8,128)}) custom-call(f32[2,32,256]{2,1,0:T(8,128)S(1)} %get-tuple-element.83.refs_0_, bf16[2,32,256]{2,1,0:T(8,128)(2,1)S(1)} %collective-permute-done.11.refs_1_, bf16[2,32,256]{2,1,0:T(8,128)(2,1)S(1)} %collective-permute-done.12.refs_2_, bf16[2,32,256]{2,1,0:T(8,128)(2,1)S(1)} %collective-permute-done.13.refs_3_), custom_call_target="tpu_custom_call" | custom-call | bytes 229376 | tf_op jit(solution)/shard_map/pallas_call | solution.py:33
  (3 shorter events, 0.1 us)
Async XLA Ops:
  0.6 3.9 %copy-start.2 = (bf16[256,128]{1,0:T(8,128)(2,1)S(1)}, bf16[256,128]{1,0:T(8,128)(2,1)}, u32[]{:S(2)}) copy-start(bf16[256,128]{1,0:T(8,128)(2,1)} %param.8) | copy-start | bytes 196612
  0.6 3.9 %copy-start.3 = (bf16[256,128]{1,0:T(8,128)(2,1)S(1)}, bf16[256,128]{1,0:T(8,128)(2,1)}, u32[]{:S(2)}) copy-start(bf16[256,128]{1,0:T(8,128)(2,1)} %param.7) | copy-start | bytes 196612
  1.6 6.5 %collective-permute-start = (bf16[2,256,128]{2,1,0:T(8,128)(2,1)S(1)}, bf16[2,256,128]{2,1,0:T(8,128)(2,1)S(1)}, u32[]{:S(2)}, u32[]{:S(2)}) collective-permute-start(bf16[2,256,128]{2,1,0:T(8,128)(2,1)S(1)} %pad_maximum_fusion.refs_2_.refs_4_), channel_id=1, source_target_pairs={{0,8},{4,12},{8,0},{12,4},{16,24},{20,28},{24,16},{28,20},{1,9},{5... | collective-permute-start | bytes 393224 | tf_op jit(solution)/shard_map/ppermute | solution.py:200
  4.6 1.6 %copy-start = (s32[16,16]{1,0:T(8,128)S(1)}, s32[16,16]{1,0:T(8,128)}, u32[]{:S(2)}) copy-start(s32[16,16]{1,0:T(8,128)} %mask_ref.1) | copy-start | bytes 3076
  4.6 1.6 %copy-start.1 = (s32[16]{0:T(128)S(1)}, s32[16]{0:T(128)}, u32[]{:S(2)}) copy-start(s32[16]{0:T(128)} %ids_ref.1) | copy-start | bytes 196
  4.6 5.0 %collective-permute-start.2 = (bf16[2,256,128]{2,1,0:T(8,128)(2,1)S(1)}, bf16[2,256,128]{2,1,0:T(8,128)(2,1)S(1)}, u32[]{:S(2)}, u32[]{:S(2)}) collective-permute-start(bf16[2,256,128]{2,1,0:T(8,128)(2,1)S(1)} %pad_maximum_fusion.1.refs_4_.refs_5_.refs_10_.refs_2_), channel_id=1, source_target_pairs={{0,16},{4,20},{8,24},{12,28},{16,0},{20,4},{24,8},{28,12},{1,17},{... | collective-permute-start | bytes 393224 | tf_op jit(solution)/shard_map/ppermute | solution.py:200
  6.2 3.5 %collective-permute-start.3 = (bf16[2,256,128]{2,1,0:T(8,128)(2,1)S(1)}, bf16[2,256,128]{2,1,0:T(8,128)(2,1)S(1)}, u32[]{:S(2)}, u32[]{:S(2)}) collective-permute-start(bf16[2,256,128]{2,1,0:T(8,128)(2,1)S(1)} %pad_maximum_fusion.refs_2_.refs_4_), channel_id=1, source_target_pairs={{0,4},{4,0},{8,12},{12,8},{16,20},{20,16},{24,28},{28,24},{1,5},{5... | collective-permute-start | bytes 393224 | tf_op jit(solution)/shard_map/ppermute | solution.py:200
  8.1 2.1 %collective-permute-start.1 = (bf16[2,256,128]{2,1,0:T(8,128)(2,1)S(1)}, bf16[2,256,128]{2,1,0:T(8,128)(2,1)S(1)}, u32[]{:S(2)}, u32[]{:S(2)}) collective-permute-start(bf16[2,256,128]{2,1,0:T(8,128)(2,1)S(1)} %shard_map.86), channel_id=1, source_target_pairs={{0,4},{4,0},{8,12},{12,8},{16,20},{20,16},{24,28},{28,24},{1,5},{5... | collective-permute-start | bytes 393224 | tf_op jit(solution)/shard_map/ppermute | solution.py:200
  10.7 3.2 %collective-permute-start.6 = (f32[4,3,256]{2,1,0:T(4,128)S(1)}, f32[4,3,256]{2,1,0:T(4,128)S(1)}, u32[]{:S(2)}, u32[]{:S(2)}) collective-permute-start(f32[4,3,256]{2,1,0:T(4,128)S(1)} %get-tuple-element.56.refs_0_), channel_id=1, source_target_pairs={{0,12},{4,8},{8,4},{12,0},{16,28},{20,24},{24,20},{28,16},{1,13},{... | collective-permute-start | bytes 36872 | tf_op jit(solution)/shard_map/ppermute | solution.py:200
  11.5 3.7 %collective-permute-start.5 = (f32[4,3,256]{2,1,0:T(4,128)S(1)}, f32[4,3,256]{2,1,0:T(4,128)S(1)}, u32[]{:S(2)}, u32[]{:S(2)}) collective-permute-start(f32[4,3,256]{2,1,0:T(4,128)S(1)} %get-tuple-element.56.refs_0_), channel_id=1, source_target_pairs={{0,8},{4,12},{8,0},{12,4},{16,24},{20,28},{24,16},{28,20},{1,9},{5... | collective-permute-start | bytes 36872 | tf_op jit(solution)/shard_map/ppermute | solution.py:200
  11.8 3.4 %collective-permute-start.4 = (f32[4,3,256]{2,1,0:T(4,128)S(1)}, f32[4,3,256]{2,1,0:T(4,128)S(1)}, u32[]{:S(2)}, u32[]{:S(2)}) collective-permute-start(f32[4,3,256]{2,1,0:T(4,128)S(1)} %get-tuple-element.56.refs_0_), channel_id=1, source_target_pairs={{0,4},{4,0},{8,12},{12,8},{16,20},{20,16},{24,28},{28,24},{1,5},{5... | collective-permute-start | bytes 36872 | tf_op jit(solution)/shard_map/ppermute | solution.py:200
  15.8 5.0 %collective-permute-start.10 = (bf16[4,2,32,256]{3,2,1,0:T(8,128)(2,1)S(1)}, bf16[4,2,32,256]{3,2,1,0:T(8,128)(2,1)S(1)}, u32[]{:S(2)}, u32[]{:S(2)}) collective-permute-start(bf16[4,2,32,256]{3,2,1,0:T(8,128)(2,1)S(1)} %get-tuple-element.82), channel_id=1, source_target_pairs={{0,16},{4,20},{8,24},{12,28},{16,0},{20,4},{24,8},{28,12},{1,17},{... | collective-permute-start | bytes 393224 | tf_op jit(solution)/shard_map/ppermute | solution.py:200
  18.4 6.4 %collective-permute-start.7 = (bf16[256,128]{1,0:T(8,128)(2,1)S(1)}, bf16[256,128]{1,0:T(8,128)(2,1)S(1)}, u32[]{:S(2)}, u32[]{:S(2)}) collective-permute-start(bf16[256,128]{1,0:T(8,128)(2,1)S(1)} %get-tuple-element.78), channel_id=1, source_target_pairs={{0,4},{4,0},{8,12},{12,8},{16,20},{20,16},{24,28},{28,24},{1,5},{5... | collective-permute-start | bytes 196616 | tf_op jit(solution)/shard_map/ppermute | solution.py:200
  18.5 6.6 %collective-permute-start.8 = (bf16[256,128]{1,0:T(8,128)(2,1)S(1)}, bf16[256,128]{1,0:T(8,128)(2,1)S(1)}, u32[]{:S(2)}, u32[]{:S(2)}) collective-permute-start(bf16[256,128]{1,0:T(8,128)(2,1)S(1)} %get-tuple-element.79), channel_id=1, source_target_pairs={{0,8},{4,12},{8,0},{12,4},{16,24},{20,28},{24,16},{28,20},{1,9},{5... | collective-permute-start | bytes 196616 | tf_op jit(solution)/shard_map/ppermute | solution.py:200
  19.1 6.0 %collective-permute-start.9 = (bf16[256,128]{1,0:T(8,128)(2,1)S(1)}, bf16[256,128]{1,0:T(8,128)(2,1)S(1)}, u32[]{:S(2)}, u32[]{:S(2)}) collective-permute-start(bf16[256,128]{1,0:T(8,128)(2,1)S(1)} %get-tuple-element.80), channel_id=1, source_target_pairs={{0,12},{4,8},{8,4},{12,0},{16,28},{20,24},{24,20},{28,16},{1,13},{... | collective-permute-start | bytes 196616 | tf_op jit(solution)/shard_map/ppermute | solution.py:200
  20.9 5.9 %collective-permute-start.11 = (bf16[2,32,256]{2,1,0:T(8,128)(2,1)S(1)}, bf16[2,32,256]{2,1,0:T(8,128)(2,1)S(1)}, u32[]{:S(2)}, u32[]{:S(2)}) collective-permute-start(bf16[2,32,256]{2,1,0:T(8,128)(2,1)S(1)} %get-tuple-element.84), channel_id=1, source_target_pairs={{0,2},{1,3},{2,1},{3,0},{4,5},{5,7},{6,4},{7,6},{8,10},{9,11},{10,... | collective-permute-start | bytes 98312 | tf_op jit(solution)/shard_map/ppermute | solution.py:277
  23.5 4.8 %collective-permute-start.12 = (bf16[2,32,256]{2,1,0:T(8,128)(2,1)S(1)}, bf16[2,32,256]{2,1,0:T(8,128)(2,1)S(1)}, u32[]{:S(2)}, u32[]{:S(2)}) collective-permute-start(bf16[2,32,256]{2,1,0:T(8,128)(2,1)S(1)} %get-tuple-element.85), channel_id=1, source_target_pairs={{0,3},{1,2},{2,0},{3,1},{4,7},{5,6},{6,5},{7,4},{8,11},{9,10},{10,... | collective-permute-start | bytes 98312 | tf_op jit(solution)/shard_map/ppermute | solution.py:277
  24.8 3.9 %collective-permute-start.13 = (bf16[2,32,256]{2,1,0:T(8,128)(2,1)S(1)}, bf16[2,32,256]{2,1,0:T(8,128)(2,1)S(1)}, u32[]{:S(2)}, u32[]{:S(2)}) collective-permute-start(bf16[2,32,256]{2,1,0:T(8,128)(2,1)S(1)} %get-tuple-element.86), channel_id=1, source_target_pairs={{0,1},{1,0},{2,3},{3,2},{4,6},{5,4},{6,7},{7,5},{8,9},{9,8},{10,11... | collective-permute-start | bytes 98312 | tf_op jit(solution)/shard_map/ppermute | solution.py:277

commit v10 on v9

--- a/solution.py
+++ b/solution.py
@@ -140,7 +140,7 @@
 
 TARGETS = (
     ((2, 3, 1, 0), (3, 2, 0, 1), (1, 0, 3, 2)),
-    ((1, 3, 0, 2), (3, 2, 1, 0), (2, 0, 3, 1)),
+    ((1, 2, 3, 0), (2, 3, 0, 1), (3, 0, 1, 2)),
 )
 
 

time: 29.5 us -> 29.5 us (level)
  no operation moved by 1% of the time
where the time goes in v10:
time: 29.5 us; the launch traced here: 29.3 us
  starting transfers between devices  14.3 us (48%)
  waiting for transfers between devices  8.2 us (28%)
  Pallas kernels  5.1 us (17%)
  other arithmetic  0.94 us (3%)
  between operations  0.76 us (3%)
    ppermute x11, starting transfers between devices, swap(): return lax.ppermute(x, 'ctx', [(i, i ^ step) for i in range(ctx_size)])  10.1 us
    ppermute x11, waiting for transfers between devices, swap(): return lax.ppermute(x, 'ctx', [(i, i ^ step) for i in range(ctx_size)])  5.32 us
    pallas_call x11, Pallas kernels, call(): pl.pallas_call(kernel, out_shape=out_shape, in_specs=in_specs or [vmem()...  5.1 us
    ppermute x3, starting transfers between devices, cross(): return lax.ppermute(x, ('ctx', 'fsdp'), pairs)  4.22 us
    ppermute x3, waiting for transfers between devices, cross(): return lax.ppermute(x, ('ctx', 'fsdp'), pairs)  2.89 us
    another operation x2, other arithmetic, body(): qg, kv = (jnp.stack([queries, out_grad]), jnp.stack([keys, values]))  0.94 us
  transfers between devices with their start and end apart: 14, of which 8 were waited for; matrix products, arithmetic and copies ran while one was open for 0% of the time, Pallas kernels for 12%

profile of v10, /device:TPU:0, one launch (start us, length us, event | category | flops | bytes accessed | tf_op | source)
XLA Modules:
  0.0 29.3 jit_solution(4890275928130403260)
XLA Ops:
  0.6 0.0 copy-start.2
  0.6 0.0 copy-start.3
  0.7 0.9 %pad_maximum_fusion.refs_2_.refs_4_ = bf16[2,256,128]{2,1,0:T(8,128)(2,1)S(1)} fusion(bf16[1,256,128]{2,1,0:T(8,128)(2,1)} %bitcast.6, bf16[1,256,128]{2,1,0:T(8,128)(2,1)} %bitcast.7), kind=kLoop, calls=%fused_computation | loop fusion | flops 65536 | bytes 262144 | tf_op jit(solution)/shard_map/stack | solution.py:202
  1.6 3.0 %collective-permute-start = (bf16[2,256,128]{2,1,0:T(8,128)(2,1)S(1)}, bf16[2,256,128]{2,1,0:T(8,128)(2,1)S(1)}, u32[]{:S(2)}, u32[]{:S(2)}) collective-permute-start(bf16[2,256,128]{2,1,0:T(8,128)(2,1)S(1)} %pad_maximum_fusion.refs_2_.refs_4_), channel_id=1, source_target_pairs={{0,8},{4,12},{8,0},{12,4},{16,24},{20,28},{24,16},{28,20},{1,9},{5... | collective-permute-start | bytes 393224 | tf_op jit(solution)/shard_map/ppermute | solution.py:200
  4.6 0.0 copy-done.2
  4.6 0.0 copy-done.3
  4.6 0.0 copy-start
  4.6 0.0 copy-start.1
  4.6 1.6 %collective-permute-start.2 = (bf16[2,256,128]{2,1,0:T(8,128)(2,1)S(1)}, bf16[2,256,128]{2,1,0:T(8,128)(2,1)S(1)}, u32[]{:S(2)}, u32[]{:S(2)}) collective-permute-start(bf16[2,256,128]{2,1,0:T(8,128)(2,1)S(1)} %pad_maximum_fusion.1.refs_4_.refs_5_.refs_10_.refs_2_), channel_id=1, source_target_pairs={{0,16},{4,20},{8,24},{12,28},{16,0},{20,4},{24,8},{28,12},{1,17},{... | collective-permute-start | bytes 393224 | tf_op jit(solution)/shard_map/ppermute | solution.py:200
  6.2 0.0 collective-permute-start.3
  6.2 0.0 copy-done
  6.2 0.0 copy-done.1
  6.2 0.8 %shard_map.85 = (s32[4,256]{1,0:T(4,128)S(1)}, s32[4,256]{1,0:T(4,128)S(1)}, s32[4,256]{1,0:T(4,128)S(1)}, s32[4,256]{1,0:T(4,128)S(1)}) custom-call(s32[16]{0:T(128)S(1)} %copy-done.1, s32[16,16]{1,0:T(8,128)S(1)} %copy-done), custom_call_target="tpu_custom_call" | custom-call | bytes 17472 | tf_op jit(solution)/shard_map/pallas_call | solution.py:33
  7.0 1.1 %collective-permute-done.in_ref.refs_3_.refs_5_.refs_6_ = bf16[2,256,128]{2,1,0:T(8,128)(2,1)S(1)} collective-permute-done((bf16[2,256,128]{2,1,0:T(8,128)(2,1)S(1)}, bf16[2,256,128]{2,1,0:T(8,128)(2,1)S(1)}, u32[]{:S(2)}, u32[]{:S(2)}) %collective-permute-start) | collective-permute-done | bytes 131104 | tf_op jit(solution)/shard_map/ppermute | solution.py:200
  8.1 0.1 collective-permute-start.1
  8.2 0.4 %shard_map.87 = (f32[256,256]{1,0:T(8,128)S(1)}, f32[256,256]{1,0:T(8,128)S(1)}, f32[256,256]{1,0:T(8,128)S(1)}, f32[256,256]{1,0:T(8,128)S(1)}, f32[3,8,256]{2,1,0:T(8,128)S(1)}, /*index=5*/f32[3,8,256]{2,1,0:T(8,128)S(1)}) custom-call(s32[4,256]{1,0:T(4,128)S(1)} %get-tuple-element.47.after_ref.refs_0_, s32[4,256]{1,0:T(4,128)S(1)} %get-tuple-element.48.refs_1_, ...), custom_call_target="tpu_custom_call" | custom-call | flops 67108864 | bytes 1630208 | tf_op jit(solution)/shard_map/pallas_call | solution.py:33
  8.6 1.1 %collective-permute-done.2.refs_8_.refs_9_.refs_11_.refs_5_.refs_3_ = bf16[2,256,128]{2,1,0:T(8,128)(2,1)S(1)} collective-permute-done((bf16[2,256,128]{2,1,0:T(8,128)(2,1)S(1)}, bf16[2,256,128]{2,1,0:T(8,128)(2,1)S(1)}, u32[]{:S(2)}, u32[]{:S(2)}) %collective-permute-start.2) | collective-permute-done | bytes 131104 | tf_op jit(solution)/shard_map/ppermute | solution.py:200
  9.6 0.0 collective-permute-done.3.refs_6_.refs_7_.refs_5_
  9.7 0.6 %shard_map.88 = (f32[256,256]{1,0:T(8,128)S(1)}, f32[256,256]{1,0:T(8,128)S(1)}, f32[256,256]{1,0:T(8,128)S(1)}, f32[256,256]{1,0:T(8,128)S(1)}, f32[256,256]{1,...) custom-call(s32[4,256]{1,0:T(4,128)S(1)} %get-tuple-element.47.after, ...), custom_call_target="tpu_custom_call" | custom-call | flops 134217728 | bytes 3260416 | tf_op jit(solution)/shard_map/pallas_call | solution.py:33
  10.2 0.0 collective-permute-done.1.refs_2_.refs_3_.refs_7_
  10.2 0.4 %shard_map.89 = (f32[256,256]{1,0:T(8,128)S(1)}, f32[256,256]{1,0:T(8,128)S(1)}, f32[256,256]{1,0:T(8,128)S(1)}, f32[256,256]{1,0:T(8,128)S(1)}, f32[3,8,256]{2,...) custom-call(s32[4,256]{1,0:T(4,128)S(1)} %get-tuple-element.46.refs_0_.refs_1_, ...), custom_call_target="tpu_custom_call" | custom-call | flops 67108864 | bytes 1789952 | tf_op jit(solution)/shard_map/pallas_call | solution.py:33
  10.7 0.8 %collective-permute-start.6 = (f32[4,3,256]{2,1,0:T(4,128)S(1)}, f32[4,3,256]{2,1,0:T(4,128)S(1)}, u32[]{:S(2)}, u32[]{:S(2)}) collective-permute-start(f32[4,3,256]{2,1,0:T(4,128)S(1)} %get-tuple-element.56.refs_0_), channel_id=1, source_target_pairs={{0,12},{4,8},{8,4},{12,0},{16,28},{20,24},{24,20},{28,16},{1,13},{... | collective-permute-start | bytes 36872 | tf_op jit(solution)/shard_map/ppermute | solution.py:200
  11.5 0.3 %collective-permute-start.5 = (f32[4,3,256]{2,1,0:T(4,128)S(1)}, f32[4,3,256]{2,1,0:T(4,128)S(1)}, u32[]{:S(2)}, u32[]{:S(2)}) collective-permute-start(f32[4,3,256]{2,1,0:T(4,128)S(1)} %get-tuple-element.56.refs_0_), channel_id=1, source_target_pairs={{0,8},{4,12},{8,0},{12,4},{16,24},{20,28},{24,16},{28,20},{1,9},{5... | collective-permute-start | bytes 36872 | tf_op jit(solution)/shard_map/ppermute | solution.py:200
  11.8 0.8 %collective-permute-start.4 = (f32[4,3,256]{2,1,0:T(4,128)S(1)}, f32[4,3,256]{2,1,0:T(4,128)S(1)}, u32[]{:S(2)}, u32[]{:S(2)}) collective-permute-start(f32[4,3,256]{2,1,0:T(4,128)S(1)} %get-tuple-element.56.refs_0_), channel_id=1, source_target_pairs={{0,4},{4,0},{8,12},{12,8},{16,20},{20,16},{24,28},{28,24},{1,5},{5... | collective-permute-start | bytes 36872 | tf_op jit(solution)/shard_map/ppermute | solution.py:200
  12.6 1.3 %collective-permute-done.6.refs_3_ = f32[4,3,256]{2,1,0:T(4,128)S(1)} collective-permute-done((f32[4,3,256]{2,1,0:T(4,128)S(1)}, f32[4,3,256]{2,1,0:T(4,128)S(1)}, u32[]{:S(2)}, u32[]{:S(2)}) %collective-permute-start.6) | collective-permute-done | bytes 12320 | tf_op jit(solution)/shard_map/ppermute | solution.py:200
  13.9 1.3 %collective-permute-done.5.refs_2_ = f32[4,3,256]{2,1,0:T(4,128)S(1)} collective-permute-done((f32[4,3,256]{2,1,0:T(4,128)S(1)}, f32[4,3,256]{2,1,0:T(4,128)S(1)}, u32[]{:S(2)}, u32[]{:S(2)}) %collective-permute-start.5) | collective-permute-done | bytes 12320 | tf_op jit(solution)/shard_map/ppermute | solution.py:200
  15.2 0.0 collective-permute-done.4.refs_1_
  15.2 0.6 %shard_map.91 = (bf16[256,1024]{1,0:T(8,128)(2,1)S(1)}, bf16[4,2,32,256]{3,2,1,0:T(8,128)(2,1)S(1)}) custom-call(f32[4,3,256]{2,1,0:T(4,128)S(1)} %get-tuple-element.56.refs_0_, f32[4,3,256]{2,1,0:T(4,128)S(1)} %collective-permute-done.4.refs_1_, f32[4,3,256]{2,1,0:T(4,128)S(1)} %collective-permute-done.5.refs_2_, ...), custom_call_target="tpu_custom_call" | custom-call | flops 134217728 | bytes 3424256 | tf_op jit(solution)/shard_map/pallas_call | solution.py:33
  15.8 1.6 %collective-permute-start.10 = (bf16[4,2,32,256]{3,2,1,0:T(8,128)(2,1)S(1)}, bf16[4,2,32,256]{3,2,1,0:T(8,128)(2,1)S(1)}, u32[]{:S(2)}, u32[]{:S(2)}) collective-permute-start(bf16[4,2,32,256]{3,2,1,0:T(8,128)(2,1)S(1)} %get-tuple-element.82), channel_id=1, source_target_pairs={{0,16},{4,20},{8,24},{12,28},{16,0},{20,4},{24,8},{28,12},{1,17},{... | collective-permute-start | bytes 393224 | tf_op jit(solution)/shard_map/ppermute | solution.py:200
  17.4 0.6 %shard_map.90 = (bf16[256,1024]{1,0:T(8,128)(2,1)S(1)}, f32[4,2,32,256]{3,2,1,0:T(8,128)S(1)}) custom-call(f32[4,3,256]{2,1,0:T(4,128)S(1)} %get-tuple-element.56.refs_0_, f32[4,3,256]{2,1,0:T(4,128)S(1)} %collective-permute-done.4.refs_1_, f32[4,3,256]{2,1,0:T(4,128)S(1)} %collective-permute-done.5.refs_2_, ...), custom_call_target="tpu_custom_call" | custom-call | flops 134217728 | bytes 3555328 | tf_op jit(solution)/shard_map/pallas_call | solution.py:33
  18.0 0.4 %shard_map.92 = (f32[256,128]{1,0:T(8,128)S(1)}, bf16[256,128]{1,0:T(8,128)(2,1)S(1)}, bf16[256,128]{1,0:T(8,128)(2,1)S(1)}, bf16[256,128]{1,0:T(8,128)(2,1)S(1)}) custom-call(bf16[256,1024]{1,0:T(8,128)(2,1)S(1)} %get-tuple-element.66.refs_0_, bf16[256,1024]{1,0:T(8,128)(2,1)S(1)} %get-tuple-element.76.refs_1_, ...), custom_call_target="tpu_custom_call" | custom-call | flops 134217728 | bytes 1638400 | tf_op jit(solution)/shard_map/pallas_call | solution.py:33
  18.4 0.1 collective-permute-start.7
  18.5 0.6 %collective-permute-start.8 = (bf16[256,128]{1,0:T(8,128)(2,1)S(1)}, bf16[256,128]{1,0:T(8,128)(2,1)S(1)}, u32[]{:S(2)}, u32[]{:S(2)}) collective-permute-start(bf16[256,128]{1,0:T(8,128)(2,1)S(1)} %get-tuple-element.79), channel_id=1, source_target_pairs={{0,8},{4,12},{8,0},{12,4},{16,24},{20,28},{24,16},{28,20},{1,9},{5... | collective-permute-start | bytes 196616 | tf_op jit(solution)/shard_map/ppermute | solution.py:200
  19.1 1.2 %collective-permute-start.9 = (bf16[256,128]{1,0:T(8,128)(2,1)S(1)}, bf16[256,128]{1,0:T(8,128)(2,1)S(1)}, u32[]{:S(2)}, u32[]{:S(2)}) collective-permute-start(bf16[256,128]{1,0:T(8,128)(2,1)S(1)} %get-tuple-element.80), channel_id=1, source_target_pairs={{0,12},{4,8},{8,4},{12,0},{16,28},{20,24},{24,20},{28,16},{1,13},{... | collective-permute-start | bytes 196616 | tf_op jit(solution)/shard_map/ppermute | solution.py:200
  20.4 0.5 %collective-permute-done.10.refs_1_ = bf16[4,2,32,256]{3,2,1,0:T(8,128)(2,1)S(1)} collective-permute-done((bf16[4,2,32,256]{3,2,1,0:T(8,128)(2,1)S(1)}, bf16[4,2,32,256]{3,2,1,0:T(8,128)(2,1)S(1)}, u32[]{:S(2)}, u32[]{:S(2)}) %collective-permute-start.10) | collective-permute-done | bytes 131104 | tf_op jit(solution)/shard_map/ppermute | solution.py:200
  20.9 2.6 %collective-permute-start.11 = (bf16[2,32,256]{2,1,0:T(8,128)(2,1)S(1)}, bf16[2,32,256]{2,1,0:T(8,128)(2,1)S(1)}, u32[]{:S(2)}, u32[]{:S(2)}) collective-permute-start(bf16[2,32,256]{2,1,0:T(8,128)(2,1)S(1)} %get-tuple-element.84), channel_id=1, source_target_pairs={{0,2},{1,3},{2,1},{3,0},{4,5},{5,6},{6,7},{7,4},{8,10},{9,11},{10,... | collective-permute-start | bytes 98312 | tf_op jit(solution)/shard_map/ppermute | solution.py:277
  23.5 1.2 %collective-permute-start.12 = (bf16[2,32,256]{2,1,0:T(8,128)(2,1)S(1)}, bf16[2,32,256]{2,1,0:T(8,128)(2,1)S(1)}, u32[]{:S(2)}, u32[]{:S(2)}) collective-permute-start(bf16[2,32,256]{2,1,0:T(8,128)(2,1)S(1)} %get-tuple-element.85), channel_id=1, source_target_pairs={{0,3},{1,2},{2,0},{3,1},{4,6},{5,7},{6,4},{7,5},{8,11},{9,10},{10,... | collective-permute-start | bytes 98312 | tf_op jit(solution)/shard_map/ppermute | solution.py:277
  24.8 0.0 collective-permute-done.7.refs_1_
  24.8 0.3 %collective-permute-start.13 = (bf16[2,32,256]{2,1,0:T(8,128)(2,1)S(1)}, bf16[2,32,256]{2,1,0:T(8,128)(2,1)S(1)}, u32[]{:S(2)}, u32[]{:S(2)}) collective-permute-start(bf16[2,32,256]{2,1,0:T(8,128)(2,1)S(1)} %get-tuple-element.86), channel_id=1, source_target_pairs={{0,1},{1,0},{2,3},{3,2},{4,7},{5,4},{6,5},{7,6},{8,9},{9,8},{10,11... | collective-permute-start | bytes 98312 | tf_op jit(solution)/shard_map/ppermute | solution.py:277
  25.1 0.0 collective-permute-done.8.refs_2_
  25.1 0.0 collective-permute-done.9.refs_3_
  25.1 0.7 %shard_map.93 = f32[256,128]{1,0:T(8,128)} custom-call(f32[256,128]{1,0:T(8,128)S(1)} %get-tuple-element.77.refs_0_, bf16[256,128]{1,0:T(8,128)(2,1)S(1)} %collective-permute-done.7.refs_1_, bf16[256,128]{1,0:T(8,128)(2,1)S(1)} %collective-permute-done.8.refs_2_, bf16[256,128]{1,0:T(8,128)(2,1)S(1)} %collective-permute-done.9.refs_3_), custom_call_target="tpu_custom_call" | custom-call | bytes 458752 | tf_op jit(solution)/shard_map/pallas_call | solution.py:33
  25.8 0.9 %collective-permute-done.11.refs_1_ = bf16[2,32,256]{2,1,0:T(8,128)(2,1)S(1)} collective-permute-done((bf16[2,32,256]{2,1,0:T(8,128)(2,1)S(1)}, bf16[2,32,256]{2,1,0:T(8,128)(2,1)S(1)}, u32[]{:S(2)}, u32[]{:S(2)}) %collective-permute-start.11) | collective-permute-done | bytes 32800 | tf_op jit(solution)/shard_map/ppermute | solution.py:277
  26.7 1.6 %collective-permute-done.12.refs_2_ = bf16[2,32,256]{2,1,0:T(8,128)(2,1)S(1)} collective-permute-done((bf16[2,32,256]{2,1,0:T(8,128)(2,1)S(1)}, bf16[2,32,256]{2,1,0:T(8,128)(2,1)S(1)}, u32[]{:S(2)}, u32[]{:S(2)}) %collective-permute-start.12) | collective-permute-done | bytes 32800 | tf_op jit(solution)/shard_map/ppermute | solution.py:277
  28.4 0.4 %collective-permute-done.13.refs_3_ = bf16[2,32,256]{2,1,0:T(8,128)(2,1)S(1)} collective-permute-done((bf16[2,32,256]{2,1,0:T(8,128)(2,1)S(1)}, bf16[2,32,256]{2,1,0:T(8,128)(2,1)S(1)}, u32[]{:S(2)}, u32[]{:S(2)}) %collective-permute-start.13) | collective-permute-done | bytes 32800 | tf_op jit(solution)/shard_map/ppermute | solution.py:277
  28.7 0.6 %shard_map.95 = (f32[32,256]{1,0:T(8,128)}, f32[32,256]{1,0:T(8,128)}) custom-call(f32[2,32,256]{2,1,0:T(8,128)S(1)} %get-tuple-element.83.refs_0_, bf16[2,32,256]{2,1,0:T(8,128)(2,1)S(1)} %collective-permute-done.11.refs_1_, bf16[2,32,256]{2,1,0:T(8,128)(2,1)S(1)} %collective-permute-done.12.refs_2_, bf16[2,32,256]{2,1,0:T(8,128)(2,1)S(1)} %collective-permute-done.13.refs_3_), custom_call_target="tpu_custom_call" | custom-call | bytes 229376 | tf_op jit(solution)/shard_map/pallas_call | solution.py:33
  (3 shorter events, 0.1 us)
Async XLA Ops:
  0.6 3.9 %copy-start.2 = (bf16[256,128]{1,0:T(8,128)(2,1)S(1)}, bf16[256,128]{1,0:T(8,128)(2,1)}, u32[]{:S(2)}) copy-start(bf16[256,128]{1,0:T(8,128)(2,1)} %param.8) | copy-start | bytes 196612
  0.6 3.9 %copy-start.3 = (bf16[256,128]{1,0:T(8,128)(2,1)S(1)}, bf16[256,128]{1,0:T(8,128)(2,1)}, u32[]{:S(2)}) copy-start(bf16[256,128]{1,0:T(8,128)(2,1)} %param.7) | copy-start | bytes 196612
  1.6 6.5 %collective-permute-start = (bf16[2,256,128]{2,1,0:T(8,128)(2,1)S(1)}, bf16[2,256,128]{2,1,0:T(8,128)(2,1)S(1)}, u32[]{:S(2)}, u32[]{:S(2)}) collective-permute-start(bf16[2,256,128]{2,1,0:T(8,128)(2,1)S(1)} %pad_maximum_fusion.refs_2_.refs_4_), channel_id=1, source_target_pairs={{0,8},{4,12},{8,0},{12,4},{16,24},{20,28},{24,16},{28,20},{1,9},{5... | collective-permute-start | bytes 393224 | tf_op jit(solution)/shard_map/ppermute | solution.py:200
  4.6 1.6 %copy-start = (s32[16,16]{1,0:T(8,128)S(1)}, s32[16,16]{1,0:T(8,128)}, u32[]{:S(2)}) copy-start(s32[16,16]{1,0:T(8,128)} %mask_ref.1) | copy-start | bytes 3076
  4.6 1.6 %copy-start.1 = (s32[16]{0:T(128)S(1)}, s32[16]{0:T(128)}, u32[]{:S(2)}) copy-start(s32[16]{0:T(128)} %ids_ref.1) | copy-start | bytes 196
  4.6 5.0 %collective-permute-start.2 = (bf16[2,256,128]{2,1,0:T(8,128)(2,1)S(1)}, bf16[2,256,128]{2,1,0:T(8,128)(2,1)S(1)}, u32[]{:S(2)}, u32[]{:S(2)}) collective-permute-start(bf16[2,256,128]{2,1,0:T(8,128)(2,1)S(1)} %pad_maximum_fusion.1.refs_4_.refs_5_.refs_10_.refs_2_), channel_id=1, source_target_pairs={{0,16},{4,20},{8,24},{12,28},{16,0},{20,4},{24,8},{28,12},{1,17},{... | collective-permute-start | bytes 393224 | tf_op jit(solution)/shard_map/ppermute | solution.py:200
  6.2 3.5 %collective-permute-start.3 = (bf16[2,256,128]{2,1,0:T(8,128)(2,1)S(1)}, bf16[2,256,128]{2,1,0:T(8,128)(2,1)S(1)}, u32[]{:S(2)}, u32[]{:S(2)}) collective-permute-start(bf16[2,256,128]{2,1,0:T(8,128)(2,1)S(1)} %pad_maximum_fusion.refs_2_.refs_4_), channel_id=1, source_target_pairs={{0,4},{4,0},{8,12},{12,8},{16,20},{20,16},{24,28},{28,24},{1,5},{5... | collective-permute-start | bytes 393224 | tf_op jit(solution)/shard_map/ppermute | solution.py:200
  8.1 2.1 %collective-permute-start.1 = (bf16[2,256,128]{2,1,0:T(8,128)(2,1)S(1)}, bf16[2,256,128]{2,1,0:T(8,128)(2,1)S(1)}, u32[]{:S(2)}, u32[]{:S(2)}) collective-permute-start(bf16[2,256,128]{2,1,0:T(8,128)(2,1)S(1)} %shard_map.86), channel_id=1, source_target_pairs={{0,4},{4,0},{8,12},{12,8},{16,20},{20,16},{24,28},{28,24},{1,5},{5... | collective-permute-start | bytes 393224 | tf_op jit(solution)/shard_map/ppermute | solution.py:200
  10.7 3.2 %collective-permute-start.6 = (f32[4,3,256]{2,1,0:T(4,128)S(1)}, f32[4,3,256]{2,1,0:T(4,128)S(1)}, u32[]{:S(2)}, u32[]{:S(2)}) collective-permute-start(f32[4,3,256]{2,1,0:T(4,128)S(1)} %get-tuple-element.56.refs_0_), channel_id=1, source_target_pairs={{0,12},{4,8},{8,4},{12,0},{16,28},{20,24},{24,20},{28,16},{1,13},{... | collective-permute-start | bytes 36872 | tf_op jit(solution)/shard_map/ppermute | solution.py:200
  11.5 3.7 %collective-permute-start.5 = (f32[4,3,256]{2,1,0:T(4,128)S(1)}, f32[4,3,256]{2,1,0:T(4,128)S(1)}, u32[]{:S(2)}, u32[]{:S(2)}) collective-permute-start(f32[4,3,256]{2,1,0:T(4,128)S(1)} %get-tuple-element.56.refs_0_), channel_id=1, source_target_pairs={{0,8},{4,12},{8,0},{12,4},{16,24},{20,28},{24,16},{28,20},{1,9},{5... | collective-permute-start | bytes 36872 | tf_op jit(solution)/shard_map/ppermute | solution.py:200
  11.8 3.4 %collective-permute-start.4 = (f32[4,3,256]{2,1,0:T(4,128)S(1)}, f32[4,3,256]{2,1,0:T(4,128)S(1)}, u32[]{:S(2)}, u32[]{:S(2)}) collective-permute-start(f32[4,3,256]{2,1,0:T(4,128)S(1)} %get-tuple-element.56.refs_0_), channel_id=1, source_target_pairs={{0,4},{4,0},{8,12},{12,8},{16,20},{20,16},{24,28},{28,24},{1,5},{5... | collective-permute-start | bytes 36872 | tf_op jit(solution)/shard_map/ppermute | solution.py:200
  15.8 5.0 %collective-permute-start.10 = (bf16[4,2,32,256]{3,2,1,0:T(8,128)(2,1)S(1)}, bf16[4,2,32,256]{3,2,1,0:T(8,128)(2,1)S(1)}, u32[]{:S(2)}, u32[]{:S(2)}) collective-permute-start(bf16[4,2,32,256]{3,2,1,0:T(8,128)(2,1)S(1)} %get-tuple-element.82), channel_id=1, source_target_pairs={{0,16},{4,20},{8,24},{12,28},{16,0},{20,4},{24,8},{28,12},{1,17},{... | collective-permute-start | bytes 393224 | tf_op jit(solution)/shard_map/ppermute | solution.py:200
  18.4 6.4 %collective-permute-start.7 = (bf16[256,128]{1,0:T(8,128)(2,1)S(1)}, bf16[256,128]{1,0:T(8,128)(2,1)S(1)}, u32[]{:S(2)}, u32[]{:S(2)}) collective-permute-start(bf16[256,128]{1,0:T(8,128)(2,1)S(1)} %get-tuple-element.78), channel_id=1, source_target_pairs={{0,4},{4,0},{8,12},{12,8},{16,20},{20,16},{24,28},{28,24},{1,5},{5... | collective-permute-start | bytes 196616 | tf_op jit(solution)/shard_map/ppermute | solution.py:200
  18.5 6.6 %collective-permute-start.8 = (bf16[256,128]{1,0:T(8,128)(2,1)S(1)}, bf16[256,128]{1,0:T(8,128)(2,1)S(1)}, u32[]{:S(2)}, u32[]{:S(2)}) collective-permute-start(bf16[256,128]{1,0:T(8,128)(2,1)S(1)} %get-tuple-element.79), channel_id=1, source_target_pairs={{0,8},{4,12},{8,0},{12,4},{16,24},{20,28},{24,16},{28,20},{1,9},{5... | collective-permute-start | bytes 196616 | tf_op jit(solution)/shard_map/ppermute | solution.py:200
  19.1 6.0 %collective-permute-start.9 = (bf16[256,128]{1,0:T(8,128)(2,1)S(1)}, bf16[256,128]{1,0:T(8,128)(2,1)S(1)}, u32[]{:S(2)}, u32[]{:S(2)}) collective-permute-start(bf16[256,128]{1,0:T(8,128)(2,1)S(1)} %get-tuple-element.80), channel_id=1, source_target_pairs={{0,12},{4,8},{8,4},{12,0},{16,28},{20,24},{24,20},{28,16},{1,13},{... | collective-permute-start | bytes 196616 | tf_op jit(solution)/shard_map/ppermute | solution.py:200
  20.9 5.8 %collective-permute-start.11 = (bf16[2,32,256]{2,1,0:T(8,128)(2,1)S(1)}, bf16[2,32,256]{2,1,0:T(8,128)(2,1)S(1)}, u32[]{:S(2)}, u32[]{:S(2)}) collective-permute-start(bf16[2,32,256]{2,1,0:T(8,128)(2,1)S(1)} %get-tuple-element.84), channel_id=1, source_target_pairs={{0,2},{1,3},{2,1},{3,0},{4,5},{5,6},{6,7},{7,4},{8,10},{9,11},{10,... | collective-permute-start | bytes 98312 | tf_op jit(solution)/shard_map/ppermute | solution.py:277
  23.5 4.8 %collective-permute-start.12 = (bf16[2,32,256]{2,1,0:T(8,128)(2,1)S(1)}, bf16[2,32,256]{2,1,0:T(8,128)(2,1)S(1)}, u32[]{:S(2)}, u32[]{:S(2)}) collective-permute-start(bf16[2,32,256]{2,1,0:T(8,128)(2,1)S(1)} %get-tuple-element.85), channel_id=1, source_target_pairs={{0,3},{1,2},{2,0},{3,1},{4,6},{5,7},{6,4},{7,5},{8,11},{9,10},{10,... | collective-permute-start | bytes 98312 | tf_op jit(solution)/shard_map/ppermute | solution.py:277
  24.8 3.9 %collective-permute-start.13 = (bf16[2,32,256]{2,1,0:T(8,128)(2,1)S(1)}, bf16[2,32,256]{2,1,0:T(8,128)(2,1)S(1)}, u32[]{:S(2)}, u32[]{:S(2)}) collective-permute-start(bf16[2,32,256]{2,1,0:T(8,128)(2,1)S(1)} %get-tuple-element.86), channel_id=1, source_target_pairs={{0,1},{1,0},{2,3},{3,2},{4,7},{5,4},{6,5},{7,6},{8,9},{9,8},{10,11... | collective-permute-start | bytes 98312 | tf_op jit(solution)/shard_map/ppermute | solution.py:277
